TPU v7x, 256 devices: a whole 4x4x8 slice. The times are simulated.
256 devices in a mesh: dp: 32 (over y, x, core), tensor: 8 (over z).
Axes of the slice: x: 4, y: 4, z: 8, core: 2. Of those that a mesh axis runs over, the one named last changes fastest.
Arguments:
- x_in: bfloat16 [32768, 8192], P(('dp', 'tensor')), may hold values from -6 to 6
- z_in: bfloat16 [32768, 8192], P(('dp', 'tensor')), may hold values from -6 to 6
- bc_in: bfloat16 [32768, 2048], P(('dp', 'tensor')), may hold values from -6 to 6
- dt_in: bfloat16 [32768, 128], P(('dp', 'tensor')), may hold values from -4 to 4
- conv_x_param: float32 [5, 8192], P(None, 'tensor'), may hold values from -3 to 3
- conv_bc_param: float32 [5, 2048], P(None, 'tensor'), may hold values from -3 to 3
- decay_rate: float32 [128], P('tensor'), may hold values from 0.01 to 2
- dt_bias: float32 [128], P('tensor'), may hold values from -3 to 0
- skip_gain: float32 [128], P('tensor'), may hold values from -3 to 3
- norm_gain: float32 [8192], P('tensor'), may hold values from 0.5 to 1.5
- ssm_state: float32 [128, 128, 64, 128], P('dp', 'tensor'), may hold values from -0.6 to 0.6
- conv_x_state: float32 [128, 3, 8192], P('dp', None, 'tensor'), may hold values from -6 to 6
- conv_bc_state: float32 [128, 3, 2048], P('dp', None, 'tensor'), may hold values from -6 to 6
- lengths: int32 [128], replicated, may hold values from 3 to 640, as said below
- prefill_owner: int32 [128], replicated, may hold values from 0 to 31, as said below
- row_start: int32 [128], replicated, may hold values from 0 to 1021, as said below
Outputs:
- y_out: bfloat16 [32768, 8192], P('dp', 'tensor')
- new_ssm_state: float32 [128, 128, 64, 128], P('dp', 'tensor')
- new_conv_x_state: float32 [128, 3, 8192], P('dp', None, 'tensor')
- new_conv_bc_state: float32 [128, 3, 2048], P('dp', None, 'tensor')
Inputs may be any that keep to these rules, and one draw needn't show every extreme that they name: `prefill_owner`: conversation c is held by index c // 4 along dp. Of the 4 conversations of one index, two are prefilled there, one on the next index and one on the previous index, cyclically; so every index prefills 4 conversations. The lengths of the conversations of one prefill owner add up to 1024. `row_start`: the conversations of one prefill owner cover its 1024 rows in consecutive runs, each row in exactly one.
All inputs are finite; a program needn't handle non-finite values.
Results may differ from a plain program's by a relative error of at most 0.005.
Values may be sent and summed in bfloat16 or wider, within the bound.
No kernel may reach another device: no remote copies, remote signals or barrier semaphores. Data moves between devices by JAX's collectives and lax.ppermute only.
A program may use at most 128 MiB of HBM per device.

v0:
```python
import functools
import math

import jax
import jax.numpy as jnp
from jax import lax
from jax.experimental import pallas as pl
from jax.experimental.pallas import tpu as pltpu
from jax.sharding import PartitionSpec as P

HEADS = 128
HEADDIM = 64
STATE = 128
GROUPS = 8
SLOTS = 4
ROWS = 1024
GH = HEADS // GROUPS
GC = GH * HEADDIM
Q = 256
CHUNKS = ROWS // Q
TENSOR = 8
SRC_ROWS = ROWS // TENSOR
EPSILON = 1e-05
LOG2E = math.log2(math.e)
MIB = 1 << 20

F32 = jnp.float32
BF16 = jnp.bfloat16


def mm(a, b):
    return jnp.dot(a, b, preferred_element_type=F32)


def iota(shape, dim):
    return lax.broadcasted_iota(jnp.int32, shape, dim)


def silu(v):
    half = v * 0.5
    return half + half * jnp.tanh(half)


def split2(v):
    hi = v.astype(BF16)
    return hi, (v - hi.astype(F32)).astype(BF16)


def split3(v):
    hi = v.astype(BF16)
    rest = v - hi.astype(F32)
    mid = rest.astype(BF16)
    return hi, mid, (rest - mid.astype(F32)).astype(BF16)


def segment_of(row_ids, seg):
    total = jnp.zeros(row_ids.shape, jnp.int32)
    for k in range(1, SLOTS):
        total = total + (row_ids >= seg[k]).astype(jnp.int32)
    return total


def boundary_targets(shape, dim, seg):
    idx = iota(shape, dim) % 16
    target = jnp.full(shape, -1, jnp.int32)
    for s in range(SLOTS):
        for q in range(3):
            target = jnp.where(idx == 3 * s + q, seg[s] + q, target)
    return jnp.where(iota(shape, dim) < 48, target, -1)


def last_rows(x_ref, lanes, seg):
    idx = iota((16, 1), 0)
    target = jnp.full((16, 1), -1, jnp.int32)
    for s in range(SLOTS):
        for q in range(3):
            target = jnp.where(idx == 3 * s + q, seg[4 + s] - 3 + q, target)
    picker = (iota((16, ROWS), 1) == target).astype(F32).astype(BF16)
    return mm(picker, x_ref[0:ROWS, lanes])


def boundary_terms(last, state, param, lanes):
    diff = state - pltpu.roll(last, 3, 0)
    q = iota((16, 1), 0) % 3
    term = param[0:1, lanes] * diff
    term = term + jnp.where(q <= 1, param[1:2, lanes] * pltpu.roll(diff, 15, 0), 0.0)
    term = term + jnp.where(q == 0, param[2:3, lanes] * pltpu.roll(diff, 14, 0), 0.0)
    return split3(term)


def conv_rows(x_ref, r0, count, lanes, param, terms_ref, targets):
    prev = pl.multiple_of(jnp.maximum(r0 - 16, 0), 16)
    halo = x_ref[pl.ds(prev, 16), lanes].astype(F32) * jnp.where(r0 > 0, 1.0, 0.0)
    value = jnp.concatenate([halo, x_ref[pl.ds(r0, count), lanes].astype(F32)], axis=0)
    onehot = (iota((count, 128), 0) + r0 == targets).astype(F32).astype(BF16)
    total = mm(onehot, terms_ref[:, lanes]) + param[4:5, lanes]
    total = total + param[3:4, lanes] * value[16:]
    for lag in (1, 2, 3):
        total = total + param[3 - lag : 4 - lag, lanes] * pltpu.roll(value, lag, 0)[16:]
    return silu(total)


def store_terms(terms_ref, lanes, parts):
    for i, part in enumerate(parts):
        terms_ref[16 * i : 16 * i + 16, lanes] = part


def pack_kernel(bc, dt, out):
    dt_t = dt[...].astype(F32).T.astype(BF16)
    for t in range(TENSOR):
        out[t, 0:SRC_ROWS, :] = bc[:, 2 * STATE * t : 2 * STATE * (t + 1)]
        out[t, SRC_ROWS : SRC_ROWS + GH, 0:SRC_ROWS] = dt_t[GH * t : GH * (t + 1), :]
        out[t, SRC_ROWS : SRC_ROWS + GH, SRC_ROWS:] = jnp.zeros((GH, SRC_ROWS), BF16)


def prep_kernel(
    seg,
    bcdt,
    conv_state,
    own,
    lft,
    rgt,
    param,
    rate,
    bias,
    b_t_out,
    c_out,
    mix_out,
    col_out,
    row_out,
    dec_out,
    last_out,
    init_out,
    bc_rows,
    b_rows,
    terms,
):
    for s in range(TENSOR):
        bc_rows[SRC_ROWS * s : SRC_ROWS * (s + 1), :] = bcdt[s, 0:SRC_ROWS, :]
    every = slice(0, 2 * STATE)
    last = last_rows(bc_rows, every, seg)
    last_out[...] = last
    terms[...] = jnp.zeros_like(terms)
    store_terms(terms, every, boundary_terms(last, conv_state[...], param, every))
    targets = boundary_targets((1, 128), 1, seg)

    @pl.loop(0, ROWS // 64)
    def _(i):
        r0 = pl.multiple_of(i * 64, 64)
        value = conv_rows(bc_rows, r0, 64, every, param, terms, targets).astype(BF16)
        b_rows[pl.ds(r0, 64), :] = value[:, 0:STATE]
        c_out[pl.ds(r0, 64), :] = value[:, STATE:]

    dec_sum = jnp.zeros((GH, 128), F32)
    for c in range(CHUNKS):
        b_t = b_rows[Q * c : Q * (c + 1), :].astype(F32).T.astype(BF16)
        b_t_out[c] = b_t
        seg_col = segment_of(iota((Q, 1), 0) + Q * c, seg)
        seg_row = segment_of(iota((1, Q), 1) + Q * c, seg)
        same = seg_col == seg_row
        row_id, col_id = iota((Q, Q), 0), iota((Q, Q), 1)
        mix = mm(c_out[Q * c : Q * (c + 1), :], b_t)
        mix_out[c] = jnp.where(same & (col_id <= row_id), mix, 0.0)
        up_to = jnp.where(same & (row_id <= col_id), 1.0, 0.0).astype(BF16)
        after = jnp.where(same & (row_id > col_id), 1.0, 0.0).astype(BF16)
        raw = jnp.concatenate(
            [bcdt[s, SRC_ROWS : SRC_ROWS + GH, 0:SRC_ROWS] for s in (2 * c, 2 * c + 1)], axis=1
        ).astype(F32) + bias[...]
        step = jnp.maximum(raw, 0.0) + jnp.log1p(jnp.exp(-jnp.abs(raw)))
        log_decay = step * rate[...] * (-LOG2E)
        parts = jnp.concatenate(split3(log_decay), axis=0)

        def summed(mask):
            three = mm(parts, mask)
            return three[0:GH] + three[GH : 2 * GH] + three[2 * GH : 3 * GH]

        running = summed(up_to)
        rest = summed(after)
        row_out[c] = running - jnp.log2(step)
        stack = jnp.concatenate(
            [running, jnp.exp2(running), jnp.exp2(rest) * step, jnp.zeros((80, Q), F32)], axis=0
        )
        col_out[c] = stack.T
        pair = jnp.where(seg_col + SLOTS * c == iota((Q, 128), 1), 1.0, 0.0).astype(BF16)
        dec_sum = dec_sum + summed(pair)
    decay = jnp.concatenate([jnp.exp2(dec_sum), jnp.zeros((128 - GH, 128), F32)], axis=0).T[0:16]
    spread = jnp.where(iota((128, GC), 0) == iota((128, GC), 1) // HEADDIM, 1.0, 0.0).astype(BF16)
    dec_hi, dec_lo = split2(decay)
    dec_out[...] = mm(dec_hi, spread) + mm(dec_lo, spread)

    def load_state(k, ref_of):
        for b in range(GC // 128):
            init_out[k, :, 128 * b : 128 * (b + 1)] = ref_of(b).T

    @pl.loop(0, SLOTS)
    def _(k):
        source = seg[8 + k]

        @pl.when(source < SLOTS)
        def _():
            load_state(k, lambda b: own[jnp.minimum(source, SLOTS - 1), 128 * b : 128 * (b + 1), :])

        @pl.when(source == SLOTS)
        def _():
            load_state(k, lambda b: lft[128 * b : 128 * (b + 1), :])

        @pl.when(source == SLOTS + 1)
        def _():
            load_state(k, lambda b: rgt[128 * b : 128 * (b + 1), :])


def main_kernel(
    seg,
    x_in,
    conv_state,
    param,
    skip,
    b_t_in,
    c_in,
    mix_in,
    col_in,
    row_in,
    dec_in,
    init_in,
    y_out,
    own_out,
    lft_out,
    rgt_out,
    last_out,
    terms,
    x_conv,
    x_weighted,
    state,
    inter,
    spread_e,
    spread_w,
):
    terms[...] = jnp.zeros_like(terms)
    targets = boundary_targets((1, 128), 1, seg)
    for lt in range(GC // 256):
        lanes = slice(256 * lt, 256 * (lt + 1))
        last = last_rows(x_in, lanes, seg)
        last_out[:, lanes] = last
        store_terms(terms, lanes, boundary_terms(last, conv_state[:, lanes], param, lanes))
        row_id = iota((256, 256), 0) % 128
        head_id = (iota((256, 256), 1) + 256 * lt) // HEADDIM
        spread_e[:, lanes] = jnp.where(row_id - GH == head_id, 1.0, 0.0).astype(BF16)
        spread_w[:, lanes] = jnp.where(row_id - 2 * GH == head_id, 1.0, 0.0).astype(BF16)

    @pl.loop(0, ROWS // 64)
    def _(i):
        r0 = pl.multiple_of(i * 64, 64)
        for lt in range(GC // 256):
            lanes = slice(256 * lt, 256 * (lt + 1))
            value = conv_rows(x_in, r0, 64, lanes, param, terms, targets)
            x_conv[pl.ds(r0, 64), lanes] = value.astype(BF16)

    @pl.loop(0, SLOTS)
    def _(k):
        state[k] = init_in[k]

    @pl.loop(0, CHUNKS)
    def _(c):
        r0 = pl.multiple_of(c * Q, Q)
        rows = pl.ds(r0, Q)
        col = col_in[c]
        col_hi, col_lo = split2(col)
        col_two = jnp.concatenate([col_hi, col_lo], axis=1)
        for lt in range(GC // 256):
            lanes = slice(256 * lt, 256 * (lt + 1))
            weight = mm(col_two, spread_w[:, lanes])
            x_weighted[:, lanes] = (x_conv[rows, lanes].astype(F32) * weight).astype(BF16)
            inter[:, lanes] = jnp.zeros((Q, 256), F32)

        @pl.loop(0, SLOTS)
        def _(k):
            first, end = seg[k], seg[4 + k]

            @pl.when((first < r0 + Q) & (end > r0))
            def _():
                row_id = iota((Q, STATE), 0) + r0
                c_part = jnp.where(
                    (row_id >= first) & (row_id < end), c_in[rows, :].astype(F32), 0.0
                ).astype(BF16)
                c_two = jnp.concatenate([c_part, c_part], axis=1)
                col_id = iota((STATE, Q), 1) + r0
                b_part = jnp.where(
                    (col_id >= first) & (col_id < end), b_t_in[c].astype(F32), 0.0
                ).astype(BF16)
                decay = dec_in[pl.ds(c * SLOTS + k, 1), :]
                for lt in range(GC // 256):
                    lanes = slice(256 * lt, 256 * (lt + 1))
                    old = state[k, :, lanes]
                    both = jnp.concatenate(split2(old), axis=0)
                    inter[:, lanes] += mm(c_two, both)
                    state[k, :, lanes] = old * decay[:, lanes] + mm(b_part, x_weighted[:, lanes])

        low_half = iota((Q, 128), 1) < HEADDIM
        for lt in range(GC // 256):
            lanes = slice(256 * lt, 256 * (lt + 1))
            scale = mm(col_two, spread_e[:, lanes])
            inter[:, lanes] = inter[:, lanes] * scale + x_conv[rows, lanes].astype(F32) * skip[
                0:1, lanes
            ]
        for hp in range(GH // 2):
            lanes = slice(128 * hp, 128 * (hp + 1))
            x_pair = x_conv[rows, lanes].astype(F32)
            x_low = jnp.where(low_half, x_pair, 0.0).astype(BF16)
            x_high = jnp.where(low_half, 0.0, x_pair).astype(BF16)
            for half in range(2):
                depth = 128 * (half + 1)
                part = slice(128 * half, 128 * (half + 1))
                mix = mix_in[c, part, 0:depth]
                total = inter[part, lanes]
                for h, x_one in ((2 * hp, x_low), (2 * hp + 1, x_high)):
                    spread = col[part, h : h + 1] - row_in[c, h : h + 1, 0:depth]
                    scores = (jnp.exp2(jnp.minimum(spread, 126.0)) * mix).astype(BF16)
                    total = total + mm(scores, x_one[0:depth])
                y_out[pl.ds(r0 + 128 * half, 128), lanes] = total

    @pl.loop(0, SLOTS)
    def _(k):
        source = seg[8 + k]
        for b in range(GC // 128):
            part = slice(128 * b, 128 * (b + 1))
            block = state[k, :, part].T

            @pl.when(source < SLOTS)
            def _():
                own_out[jnp.minimum(source, SLOTS - 1), part, :] = block

            @pl.when(source == SLOTS)
            def _():
                lft_out[part, :] = block.astype(BF16)

            @pl.when(source == SLOTS + 1)
            def _():
                rgt_out[part, :] = block.astype(BF16)


def gate_kernel(y_in, z_in, gain, out):
    gated = y_in[...] * silu(z_in[...].astype(F32))
    mean = jnp.sum(gated * gated, axis=1, keepdims=True) * (1.0 / GC)
    out[...] = (gated * lax.rsqrt(mean + EPSILON) * gain[...]).astype(BF16)


VMEM = pl.BlockSpec(memory_space=pltpu.VMEM)
SMEM = pl.BlockSpec(memory_space=pltpu.SMEM)


def params(mib):
    return pltpu.CompilerParams(vmem_limit_bytes=mib * MIB)


def pack(bc_in, dt_in):
    return pl.pallas_call(
        pack_kernel,
        out_shape=jax.ShapeDtypeStruct((TENSOR, SRC_ROWS + GH, 2 * STATE), BF16),
        in_specs=[VMEM, VMEM],
        out_specs=VMEM,
        compiler_params=params(8),
        name="pack",
    )(bc_in, dt_in)


def prep(seg, bcdt, conv_state, own, lft, rgt, param, rate, bias):
    return pl.pallas_call(
        prep_kernel,
        out_shape=(
            jax.ShapeDtypeStruct((CHUNKS, STATE, Q), BF16),
            jax.ShapeDtypeStruct((ROWS, STATE), BF16),
            jax.ShapeDtypeStruct((CHUNKS, Q, Q), F32),
            jax.ShapeDtypeStruct((CHUNKS, Q, 128), F32),
            jax.ShapeDtypeStruct((CHUNKS, GH, Q), F32),
            jax.ShapeDtypeStruct((16, GC), F32),
            jax.ShapeDtypeStruct((16, 2 * STATE), F32),
            jax.ShapeDtypeStruct((SLOTS, STATE, GC), F32),
        ),
        in_specs=[SMEM] + [VMEM] * 8,
        out_specs=(VMEM,) * 8,
        scratch_shapes=[
            pltpu.VMEM((ROWS, 2 * STATE), BF16),
            pltpu.VMEM((ROWS, STATE), BF16),
            pltpu.VMEM((128, 2 * STATE), BF16),
        ],
        compiler_params=params(24),
        cost_estimate=pl.CostEstimate(
            flops=6_000_000_000, bytes_accessed=8 * MIB, transcendentals=500_000
        ),
        name="prep",
    )(seg, bcdt, conv_state, own, lft, rgt, param, rate, bias)


def scan(seg, x_rows, conv_state, param, skip, prepared):
    b_t, c_rows, mix, col, row, dec, init = prepared
    return pl.pallas_call(
        main_kernel,
        out_shape=(
            jax.ShapeDtypeStruct((ROWS, GC), F32),
            jax.ShapeDtypeStruct((SLOTS, GC, STATE), F32),
            jax.ShapeDtypeStruct((GC, STATE), BF16),
            jax.ShapeDtypeStruct((GC, STATE), BF16),
            jax.ShapeDtypeStruct((16, GC), F32),
        ),
        in_specs=[SMEM] + [VMEM] * 11,
        out_specs=(VMEM,) * 5,
        scratch_shapes=[
            pltpu.VMEM((128, GC), BF16),
            pltpu.VMEM((ROWS, GC), BF16),
            pltpu.VMEM((Q, GC), BF16),
            pltpu.VMEM((SLOTS, STATE, GC), F32),
            pltpu.VMEM((Q, GC), F32),
            pltpu.VMEM((256, GC), BF16),
            pltpu.VMEM((256, GC), BF16),
        ],
        compiler_params=params(40),
        cost_estimate=pl.CostEstimate(
            flops=20_000_000_000, bytes_accessed=16 * MIB, transcendentals=5_000_000
        ),
        name="scan",
    )(seg, x_rows, conv_state, param, skip, b_t, c_rows, mix, col, row, dec, init)


def gate(y, z_rows, gain):
    block = 128
    return pl.pallas_call(
        gate_kernel,
        out_shape=jax.ShapeDtypeStruct((ROWS, GC), BF16),
        grid=(ROWS // block,),
        in_specs=[
            pl.BlockSpec((block, GC), lambda i: (i, 0)),
            pl.BlockSpec((block, GC), lambda i: (i, 0)),
            pl.BlockSpec((1, GC), lambda i: (0, 0)),
        ],
        out_specs=pl.BlockSpec((block, GC), lambda i: (i, 0)),
        compiler_params=params(16),
        cost_estimate=pl.CostEstimate(
            flops=20_000_000, bytes_accessed=8 * MIB, transcendentals=1_000_000
        ),
        name="gate",
    )(y, z_rows, gain)


def shifted(value, steps):
    count = lax.axis_size("dp")
    pairs = [(source, (source + steps) % count) for source in range(count)]
    return lax.ppermute(value, "dp", pairs)


def plan(lengths, prefill_owner, row_start, me, left, right):
    ids = jnp.arange(prefill_owner.shape[0], dtype=jnp.int32)
    mine = prefill_owner == me
    home = ids // SLOTS
    code = jnp.where(home == me, ids % SLOTS, jnp.where(home == left, SLOTS, SLOTS + 1))
    before = mine[None, :] & (row_start[None, :] < row_start[:, None])
    rank = jnp.sum(before.astype(jnp.int32), axis=1)
    chosen = mine[None, :] & (rank[None, :] == jnp.arange(SLOTS, dtype=jnp.int32)[:, None])

    def pick(values):
        return jnp.sum(jnp.where(chosen, values[None, :], 0), axis=1)

    starts = pick(row_start)
    codes = pick(code)
    seg = jnp.concatenate([starts, starts + pick(lengths), codes, jnp.zeros((4,), jnp.int32)])
    slot_right = jnp.sum(jnp.where((home == me) & (prefill_owner == right), ids % SLOTS, 0))
    slot_left = jnp.sum(jnp.where((home == me) & (prefill_owner == left), ids % SLOTS, 0))
    return seg, codes, slot_right, slot_left


def shards(
    x_in,
    z_in,
    bc_in,
    dt_in,
    conv_x_param,
    conv_bc_param,
    decay_rate,
    dt_bias,
    skip_gain,
    norm_gain,
    ssm_state,
    conv_x_state,
    conv_bc_state,
    lengths,
    prefill_owner,
    row_start,
):
    dp_count = lax.axis_size("dp")
    me = lax.axis_index("dp")
    left = (me + dp_count - 1) % dp_count
    right = (me + 1) % dp_count
    bcdt = lax.all_to_all(pack(bc_in, dt_in), "tensor", split_axis=0, concat_axis=0, tiled=True)
    x_rows = lax.all_to_all(x_in, "tensor", split_axis=1, concat_axis=0, tiled=True)
    z_rows = lax.all_to_all(z_in, "tensor", split_axis=1, concat_axis=0, tiled=True)

    seg, codes, slot_right, slot_left = plan(lengths, prefill_owner, row_start, me, left, right)

    own = ssm_state.reshape(SLOTS, GC, STATE)
    conv = jnp.concatenate([conv_x_state, conv_bc_state], axis=2)
    width = conv.shape[2]
    lines = 3 * width // STATE

    def mover(slot):
        state = lax.dynamic_index_in_dim(own, slot, 0, keepdims=False)
        small = lax.dynamic_index_in_dim(conv, slot, 0, keepdims=False).reshape(lines, STATE)
        return jnp.concatenate([state, small, jnp.zeros((2, STATE), F32)], axis=0)

    from_left = shifted(mover(slot_right), 1)
    from_right = shifted(mover(slot_left), -1)

    def small_of(packed):
        return packed[GC : GC + lines].reshape(1, 3, width)

    candidates = jnp.concatenate([conv, small_of(from_left), small_of(from_right)], axis=0)
    match = codes[:, None] == jnp.arange(SLOTS + 2, dtype=jnp.int32)[None, :]
    conv_init = jnp.sum(jnp.where(match[:, :, None, None], candidates[None], 0.0), axis=1)
    conv_init = jnp.concatenate([conv_init.reshape(3 * SLOTS, width), jnp.zeros((4, width), F32)])

    b_t, c_rows, mix, col, row, dec, last_bc, init = prep(
        seg,
        bcdt,
        conv_init[:, GC:],
        own,
        from_left,
        from_right,
        conv_bc_param,
        decay_rate[:, None],
        dt_bias[:, None],
    )
    y, own_new, back_left, back_right, last_x = scan(
        seg,
        x_rows,
        conv_init[:, :GC],
        conv_x_param,
        jnp.repeat(skip_gain, HEADDIM)[None, :],
        (b_t, c_rows, mix, col, row, dec, init),
    )
    last = jnp.concatenate([last_x, last_bc], axis=1)[: 3 * SLOTS].reshape(SLOTS, 3, width)

    def last_of(code):
        return jnp.sum(jnp.where((codes == code)[:, None, None], last, 0.0), axis=0)

    def back(state, code):
        small = last_of(code).astype(BF16).reshape(lines, STATE)
        return jnp.concatenate([state, small, jnp.zeros((2, STATE), BF16)], axis=0)

    returned_right = shifted(back(back_left, SLOTS), -1)
    returned_left = shifted(back(back_right, SLOTS + 1), 1)

    new_ssm = own_new
    for packed, slot in ((returned_right, slot_right), (returned_left, slot_left)):
        new_ssm = lax.dynamic_update_index_in_dim(new_ssm, packed[:GC].astype(F32), slot, 0)
    slots = jnp.arange(SLOTS, dtype=jnp.int32)
    stay = slots[:, None] == codes[None, :]
    new_conv = jnp.sum(jnp.where(stay[:, :, None, None], last[None], 0.0), axis=1)
    for packed, slot in ((returned_right, slot_right), (returned_left, slot_left)):
        new_conv = jnp.where(
            (slots == slot)[:, None, None], small_of(packed).astype(F32), new_conv
        )
    y_out = gate(y, z_rows, norm_gain[None, :])
    return (
        y_out,
        new_ssm.reshape(ssm_state.shape),
        new_conv[:, :, :GC],
        new_conv[:, :, GC:],
    )


def solution(mesh):
    in_specs = (
        P(("dp", "tensor"), None),
        P(("dp", "tensor"), None),
        P(("dp", "tensor"), None),
        P(("dp", "tensor"), None),
        P(None, "tensor"),
        P(None, "tensor"),
        P("tensor"),
        P("tensor"),
        P("tensor"),
        P("tensor"),
        P("dp", "tensor", None, None),
        P("dp", None, "tensor"),
        P("dp", None, "tensor"),
        P(),
        P(),
        P(),
    )
    out_specs = (
        P("dp", "tensor"),
        P("dp", "tensor", None, None),
        P("dp", None, "tensor"),
        P("dp", None, "tensor"),
    )
    return jax.shard_map(shards, mesh=mesh, in_specs=in_specs, out_specs=out_specs, check_vma=False)
```

profile of v0, /device:TPU:36, one launch (start us, length us, event | category | flops | bytes accessed | tf_op | source)
XLA Modules:
  0.0 150.2 jit_solution(10504854976541670147)
XLA Ops:
  0.6 0.0 copy-start.4
  0.6 1.0 copy-done.4
  1.7 0.8 copy-done.6
  2.4 0.9 pack.1
  3.4 8.6 %all-to-all-start.1 = ((bf16[8,144,256]{2,1,0:T(8,128)(2,1)}), bf16[8,144,256]{2,1,0:T(8,128)(2,1)S(1)}, u32[]{:S(2)}, u32[]{:S(2)}) async-start(bf16[8,144,256]{2,1,0:T(8,128)(2,1)} %pack.1), calls=%async_computation.1 | async-start | bytes 1179648 | tf_op jit(solution)/shard_map/all_to_all | solution.py:492
  11.9 0.0 copy-done.10
  11.9 1.6 %copy.50 = bf16[16,8,8,1024]{3,2,0,1:T(8,128)(2,1)} copy(bf16[16,8,8,1024]{3,2,1,0:T(8,128)(2,1)S(1)} %bitcast.40) | data formatting | bytes 4194304 | tf_op jit(solution)/shard_map/all_to_all | solution.py:493
  13.5 15.9 %all-to-all-done.1.bcdt = bf16[8,144,256]{2,1,0:T(8,128)(2,1)S(1)} async-done(((bf16[8,144,256]{2,1,0:T(8,128)(2,1)}), bf16[8,144,256]{2,1,0:T(8,128)(2,1)S(1)}, u32[]{:S(2)}, u32[]{:S(2)}) %all-to-all-start.1) | async-done | bytes 589856 | tf_op jit(solution)/shard_map/all_to_all | solution.py:492
  29.4 5.1 %all-to-all-start = ((bf16[128,8,1024]{2,0,1:T(8,128)(2,1)}), bf16[128,8,1024]{2,0,1:T(8,128)(2,1)S(1)}, u32[]{:S(2)}, u32[]{:S(2)}) async-start(bf16[128,8,1024]{2,0,1:T(8,128)(2,1)} %bitcast.38), calls=%async_computation | async-start | bytes 4194304 | tf_op jit(solution)/shard_map/all_to_all | solution.py:493
  34.5 0.0 copy-done.17
  34.5 0.6 fusion.2
  39.0 0.1 dynamic-slice_reduce_fusion.1
  39.2 0.0 copy-start.14
  39.2 0.0 copy-start.15
  39.2 0.0 copy-start.16
  39.2 2.1 %dynamic-slice_bitcast_fusion.1 = (f32[1024,128]{1,0:T(8,128)}, f32[1024,128]{1,0:T(8,128)S(1)}) fusion(f32[4,1024,128]{2,1,0:T(8,128)} %bitcast.35, s32[]{:T(128)S(6)} %select_n.118, s32[]{:T(128)S(6)} %select_n.120), kind=kLoop, calls=%fused_computation.5 | loop fusion | bytes 2097160 | tf_op jit(solution)/shard_map/jit(dynamic_index_in_dim)/squeeze | solution.py:504
  41.3 3.6 %concatenate.29 = f32[1056,128]{1,0:T(8,128)} concatenate(f32[1024,128]{1,0:T(8,128)} %get-tuple-element.43, f32[30,128]{1,0:T(8,128)S(1)} %reshape.151, f32[2,128]{1,0:T(2,128)S(1)} %broadcast.142), dimensions={0} | concatenate | bytes 1081344 | tf_op jit(solution)/shard_map/concatenate | solution.py:506
  44.9 0.0 collective-permute-start
  44.9 2.8 %concatenate.30 = f32[1056,128]{1,0:T(8,128)} concatenate(f32[1024,128]{1,0:T(8,128)S(1)} %get-tuple-element.44, f32[30,128]{1,0:T(8,128)S(1)} %reshape.153, f32[2,128]{1,0:T(2,128)S(1)} %broadcast.142), dimensions={0} | concatenate | bytes 1081344 | tf_op jit(solution)/shard_map/concatenate | solution.py:506
  47.7 1.7 %collective-permute-start.1 = (f32[1056,128]{1,0:T(8,128)}, f32[1056,128]{1,0:T(8,128)}, u32[]{:S(2)}, u32[]{:S(2)}) collective-permute-start(f32[1056,128]{1,0:T(8,128)} %concatenate.30), channel_id=1, source_target_pairs={{0,248},{8,0},{16,8},{24,16},{32,24},{40,32},{48,40},{56,48},{64,5... | collective-permute-start | bytes 1622024 | tf_op jit(solution)/shard_map/ppermute | solution.py:447
  49.4 0.1 copy.39.rate
  49.5 0.1 copy.40.bias
  49.6 0.1 broadcast_in_dim.171
  49.7 0.1 broadcast_in_dim_reshape.4.skip
  49.8 3.2 %copy.49 = bf16[16,8,8,1024]{3,2,0,1:T(8,128)(2,1)} copy(bf16[16,8,8,1024]{3,2,1,0:T(8,128)(2,1)} %bitcast.41) | data formatting | bytes 4194304 | tf_op jit(solution)/shard_map/all_to_all | solution.py:494
  52.9 0.2 convert_reduce_fusion
  53.1 0.0 copy-done.18
  53.1 0.1 select_reduce_fusion.5
  53.3 0.1 pad_add_fusion.seg
  53.4 0.6 collective-permute-done.lft
  54.0 0.7 slice.44
  54.8 1.9 %collective-permute-done.1.rgt = f32[1056,128]{1,0:T(8,128)} collective-permute-done((f32[1056,128]{1,0:T(8,128)}, f32[1056,128]{1,0:T(8,128)}, u32[]{:S(2)}, u32[]{:S(2)}) %collective-permute-start.1) | collective-permute-done | bytes 540704 | tf_op jit(solution)/shard_map/ppermute | solution.py:447
  56.6 0.7 slice.45
  57.4 27.3 %all-to-all-done = bf16[128,8,1024]{2,0,1:T(8,128)(2,1)S(1)} async-done(((bf16[128,8,1024]{2,0,1:T(8,128)(2,1)}), bf16[128,8,1024]{2,0,1:T(8,128)(2,1)S(1)}, u32[]{:S(2)}, u32[]{:S(2)}) %all-to-all-start) | async-done | bytes 2097184 | tf_op jit(solution)/shard_map/all_to_all | solution.py:493
  84.7 1.3 copy-done.2
  86.0 3.7 %all-to-all-start.2 = ((bf16[128,8,1024]{2,0,1:T(8,128)(2,1)}), bf16[128,8,1024]{2,0,1:T(8,128)(2,1)S(1)}, u32[]{:S(2)}, u32[]{:S(2)}) async-start(bf16[128,8,1024]{2,0,1:T(8,128)(2,1)} %bitcast.39), calls=%async_computation.2 | async-start | bytes 4194304 | tf_op jit(solution)/shard_map/all_to_all | solution.py:494
  89.8 0.1 copy.37
  89.8 0.2 select_reduce_fusion
  90.1 0.0 copy-done.9
  90.1 0.0 copy-start.5
  90.1 1.6 %copy-done.5 = f32[4,16,64,128]{3,2,1,0:T(8,128)S(1)} copy-done((f32[4,16,64,128]{3,2,1,0:T(8,128)S(1)}, f32[4,16,64,128]{3,2,1,0:T(8,128)}, u32[]{:S(2)}) %copy-start.5) | copy-done | bytes 2097176
  91.7 5.9 %prep.1 = (bf16[4,128,256]{2,1,0:T(8,128)(2,1)S(1)}, bf16[1024,128]{1,0:T(8,128)(2,1)S(1)}, f32[4,256,256]{2,1,0:T(8,128)S(1)}, f32[4,256,128]{2,1,0:T(8,128)S(1...) custom-call(s32[16]{0:T(128)S(1)} %pad_add_fusion.seg, ...), custom_call_target="tpu_custom_call" | custom-call | flops 6000000000 | bytes 8388608 | tf_op jit(solution)/shard_map/prep/pallas_call | solution.py:367
  97.6 0.0 copy-start.7
  97.6 18.8 %scan.1 = (f32[1024,1024]{1,0:T(8,128)S(1)}, f32[4,1024,128]{2,1,0:T(8,128)}, bf16[1024,128]{1,0:T(8,128)(2,1)S(1)}, bf16[1024,128]{1,0:T(8,128)(2,1)S(1)}, f32[16,1024]{1,0:T(8,128)S(1)}) custom-call(s32[16]{0:T(128)S(1)} %pad_add_fusion.seg, bf16[1024,1024]{1,0:T(8,128)(2,1)S(1)} %bitcast.34, f32[16,1024]{1,0:T(8,128)S(1)} %pad_slice_fusion.1.conv_state, ...), custom_call_target="tpu_custom_call" | custom-call | flops 20000000000 | bytes 16777216 | tf_op jit(solution)/shard_map/scan/pallas_call | solution.py:396
  116.4 1.9 %copy-done = f32[1024,1024]{1,0:T(8,128)} copy-done((f32[1024,1024]{1,0:T(8,128)}, f32[1024,1024]{1,0:T(8,128)S(1)}, u32[]{:S(2)}) %copy-start) | copy-done | bytes 4194328
  118.3 0.1 select_reduce_fusion.2
  118.5 0.2 concatenate.35
  118.6 0.1 collective-permute-start.3
  118.7 0.7 iota_compare_fusion.3
  119.4 0.7 iota_compare_fusion.4
  120.1 0.1 concatenate.34
  120.2 1.8 %collective-permute-start.2 = (bf16[1056,128]{1,0:T(8,128)(2,1)S(1)}, bf16[1056,128]{1,0:T(8,128)(2,1)}, u32[]{:S(2)}, u32[]{:S(2)}) collective-permute-start(bf16[1056,128]{1,0:T(8,128)(2,1)S(1)} %concatenate.34), channel_id=1, source_target_pairs={{0,248},{8,0},{16,8},{24,16},{32,24},{40,32},{48,40},{56,48},{64,5... | collective-permute-start | bytes 811016 | tf_op jit(solution)/shard_map/ppermute | solution.py:447
  122.0 0.2 select_reduce_fusion.1
  122.3 17.0 %all-to-all-done.2 = bf16[128,8,1024]{2,0,1:T(8,128)(2,1)S(1)} async-done(((bf16[128,8,1024]{2,0,1:T(8,128)(2,1)}), bf16[128,8,1024]{2,0,1:T(8,128)(2,1)S(1)}, u32[]{:S(2)}, u32[]{:S(2)}) %all-to-all-start.2) | async-done | bytes 2097184 | tf_op jit(solution)/shard_map/all_to_all | solution.py:494
  139.3 2.2 %copy-done.1 = f32[1024,1024]{1,0:T(8,128)S(1)} copy-done((f32[1024,1024]{1,0:T(8,128)S(1)}, f32[1024,1024]{1,0:T(8,128)}, u32[]{:S(2)}) %copy-start.1) | copy-done | bytes 4194328
  141.5 4.0 %gate.1 = bf16[1024,1024]{1,0:T(8,128)(2,1)} custom-call(f32[1024,1024]{1,0:T(8,128)S(1)} %copy-done.1, bf16[1024,1024]{1,0:T(8,128)(2,1)S(1)} %bitcast.33, f32[1,1024]{1,0:T(1,128)S(1)} %bitcast.37), custom_call_target="tpu_custom_call" | custom-call | flops 20000000 | bytes 8388608 | tf_op jit(solution)/shard_map/gate/pallas_call | solution.py:426
  145.4 0.0 collective-permute-done.3
  145.4 0.0 collective-permute-done.2
  145.4 0.7 slice_convert_fusion
  146.2 0.1 select_select_fusion
  146.3 0.7 copy.43
  146.9 0.6 copy.44
  147.6 1.8 %convert_dynamic-update-slice_fusion.1 = f32[4,1024,128]{2,1,0:T(8,128)} fusion(f32[4,1024,128]{2,1,0:T(8,128)} %get-tuple-element.25, s32[]{:T(128)S(6)} %select_n.118, bf16[1056,128]{1,0:T(8,128)(2,1)} %collective-permute-done.2), kind=kLoop, calls=%fused_computation.3 | loop fusion | flops 131072 | bytes 786436 | tf_op jit(solution)/shard_map/jit(dynamic_update_index_in_dim)/dynamic_update_slice | solution.py:552
  149.3 0.8 convert_dynamic-update-slice_fusion
  (51 shorter events, 0.4 us)
Async XLA Ops:
  0.6 1.0 copy-start.4
  1.7 0.8 copy-start.6
  2.4 9.5 %copy-start.10 = (bf16[128,8192]{1,0:T(8,128)(2,1)S(1)}, bf16[128,8192]{1,0:T(8,128)(2,1)}, u32[]{:S(2)}) copy-start(bf16[128,8192]{1,0:T(8,128)(2,1)} %param.18) | copy-start | bytes 6291460
  3.4 26.0 %all-to-all-start.1 = ((bf16[8,144,256]{2,1,0:T(8,128)(2,1)}), bf16[8,144,256]{2,1,0:T(8,128)(2,1)S(1)}, u32[]{:S(2)}, u32[]{:S(2)}) async-start(bf16[8,144,256]{2,1,0:T(8,128)(2,1)} %pack.1), calls=%async_computation.1 | async-start | bytes 1179648 | tf_op jit(solution)/shard_map/all_to_all | solution.py:492
  29.4 5.1 %copy-start.17 = (s32[128]{0:T(128)S(1)}, s32[128]{0:T(128)}, u32[]{:S(2)}) copy-start(s32[128]{0:T(128)} %param.32) | copy-start | bytes 1540
  29.4 9.6 %copy-start.11 = (f32[4,3,1024]{2,0,1:T(4,128)S(1)}, f32[4,3,1024]{2,0,1:T(4,128)}, u32[]{:S(2)}) copy-start(f32[4,3,1024]{2,0,1:T(4,128)} %param.29) | copy-start | bytes 147460
  29.4 9.7 %copy-start.12 = (f32[4,3,256]{2,0,1:T(4,128)S(1)}, f32[4,3,256]{2,0,1:T(4,128)}, u32[]{:S(2)}) copy-start(f32[4,3,256]{2,0,1:T(4,128)} %param.30) | copy-start | bytes 36868
  29.4 55.3 %all-to-all-start = ((bf16[128,8,1024]{2,0,1:T(8,128)(2,1)}), bf16[128,8,1024]{2,0,1:T(8,128)(2,1)S(1)}, u32[]{:S(2)}, u32[]{:S(2)}) async-start(bf16[128,8,1024]{2,0,1:T(8,128)(2,1)} %bitcast.38), calls=%async_computation | async-start | bytes 4194304 | tf_op jit(solution)/shard_map/all_to_all | solution.py:493
  39.2 10.3 %copy-start.14 = (f32[16]{0:T(128)S(1)}, f32[16]{0:T(128)}, u32[]{:S(2)}) copy-start(f32[16]{0:T(128)} %param.24) | copy-start | bytes 196
  39.2 10.3 %copy-start.15 = (f32[16]{0:T(128)S(1)}, f32[16]{0:T(128)}, u32[]{:S(2)}) copy-start(f32[16]{0:T(128)} %param.25) | copy-start | bytes 196
  39.2 10.4 %copy-start.16 = (f32[16]{0:T(128)S(1)}, f32[16]{0:T(128)}, u32[]{:S(2)}) copy-start(f32[16]{0:T(128)} %param.26) | copy-start | bytes 196
  44.9 9.1 %collective-permute-start = (f32[1056,128]{1,0:T(8,128)}, f32[1056,128]{1,0:T(8,128)}, u32[]{:S(2)}, u32[]{:S(2)}) collective-permute-start(f32[1056,128]{1,0:T(8,128)} %concatenate.29), channel_id=1, source_target_pairs={{0,8},{8,16},{16,24},{24,32},{32,40},{40,48},{48,56},{56,64},{64,7... | collective-permute-start | bytes 1622024 | tf_op jit(solution)/shard_map/ppermute | solution.py:447
  47.7 8.9 %collective-permute-start.1 = (f32[1056,128]{1,0:T(8,128)}, f32[1056,128]{1,0:T(8,128)}, u32[]{:S(2)}, u32[]{:S(2)}) collective-permute-start(f32[1056,128]{1,0:T(8,128)} %concatenate.30), channel_id=1, source_target_pairs={{0,248},{8,0},{16,8},{24,16},{32,24},{40,32},{48,40},{56,48},{64,5... | collective-permute-start | bytes 1622024 | tf_op jit(solution)/shard_map/ppermute | solution.py:447
  49.8 3.2 %copy-start.13 = (s32[128]{0:T(128)S(1)}, s32[128]{0:T(128)}, u32[]{:S(2)}) copy-start(s32[128]{0:T(128)} %param.33) | copy-start | bytes 1540
  49.8 3.4 %copy-start.18 = (s32[128]{0:T(128)S(1)}, s32[128]{0:T(128)}, u32[]{:S(2)}) copy-start(s32[128]{0:T(128)} %param.31) | copy-start | bytes 1540
  84.7 1.3 copy-start.2
  86.0 4.1 %copy-start.9 = (f32[5,256]{1,0:T(8,128)S(1)}, f32[5,256]{1,0:T(8,128)}, u32[]{:S(2)}) copy-start(f32[5,256]{1,0:T(8,128)} %param.34) | copy-start | bytes 15364
  86.0 53.2 %all-to-all-start.2 = ((bf16[128,8,1024]{2,0,1:T(8,128)(2,1)}), bf16[128,8,1024]{2,0,1:T(8,128)(2,1)S(1)}, u32[]{:S(2)}, u32[]{:S(2)}) async-start(bf16[128,8,1024]{2,0,1:T(8,128)(2,1)} %bitcast.39), calls=%async_computation.2 | async-start | bytes 4194304 | tf_op jit(solution)/shard_map/all_to_all | solution.py:494
  90.1 1.6 %copy-start.5 = (f32[4,16,64,128]{3,2,1,0:T(8,128)S(1)}, f32[4,16,64,128]{3,2,1,0:T(8,128)}, u32[]{:S(2)}) copy-start(f32[4,16,64,128]{3,2,1,0:T(8,128)} %param.28) | copy-start | bytes 6291460
  91.7 5.9 %copy-start.3 = (bf16[128,8,1024]{2,0,1:T(8,128)(2,1)S(1)}, bf16[128,8,1024]{2,0,1:T(8,128)(2,1)}, u32[]{:S(2)}) copy-start(bf16[128,8,1024]{2,0,1:T(8,128)(2,1)} %copy-done.2) | copy-start | bytes 6291460
  91.7 5.9 %copy-start.8 = (f32[5,1024]{1,0:T(8,128)S(1)}, f32[5,1024]{1,0:T(8,128)}, u32[]{:S(2)}) copy-start(f32[5,1024]{1,0:T(8,128)} %param.35) | copy-start | bytes 61444
  97.6 41.7 %copy-start.7 = (f32[1024]{0:T(1024)S(1)}, f32[1024]{0:T(1024)}, u32[]{:S(2)}) copy-start(f32[1024]{0:T(1024)} %param.27) | copy-start | bytes 12292
  116.4 1.9 %copy-start = (f32[1024,1024]{1,0:T(8,128)}, f32[1024,1024]{1,0:T(8,128)S(1)}, u32[]{:S(2)}) copy-start(f32[1024,1024]{1,0:T(8,128)S(1)} %get-tuple-element.24.y_in) | copy-start | bytes 12582916
  118.6 26.8 %collective-permute-start.3 = (bf16[1056,128]{1,0:T(8,128)(2,1)S(1)}, bf16[1056,128]{1,0:T(8,128)(2,1)S(1)}, u32[]{:S(2)}, u32[]{:S(2)}) collective-permute-start(bf16[1056,128]{1,0:T(8,128)(2,1)S(1)} %concatenate.35), channel_id=1, source_target_pairs={{0,8},{8,16},{16,24},{24,32},{32,40},{40,48},{48,56},{56,64},{64,7... | collective-permute-start | bytes 811016 | tf_op jit(solution)/shard_map/ppermute | solution.py:447
  120.2 25.2 %collective-permute-start.2 = (bf16[1056,128]{1,0:T(8,128)(2,1)S(1)}, bf16[1056,128]{1,0:T(8,128)(2,1)}, u32[]{:S(2)}, u32[]{:S(2)}) collective-permute-start(bf16[1056,128]{1,0:T(8,128)(2,1)S(1)} %concatenate.34), channel_id=1, source_target_pairs={{0,248},{8,0},{16,8},{24,16},{32,24},{40,32},{48,40},{56,48},{64,5... | collective-permute-start | bytes 811016 | tf_op jit(solution)/shard_map/ppermute | solution.py:447
  139.3 2.2 %copy-start.1 = (f32[1024,1024]{1,0:T(8,128)S(1)}, f32[1024,1024]{1,0:T(8,128)}, u32[]{:S(2)}) copy-start(f32[1024,1024]{1,0:T(8,128)} %copy-done) | copy-start | bytes 12582916
where the time goes:
time: 152 us; the launch traced here: 150 us
  waiting for transfers between devices  62.7 us (41%)
  Pallas kernels  29.5 us (19%)
  local copies, waits for them, and re-layouts  25.8 us (17%)
  starting transfers between devices  21 us (14%)
  other arithmetic  6.31 us (4%)
  between operations  4.83 us (3%)
    all_to_all x1, waiting for transfers between devices, shards(): lax.all_to_all(x_in, 'tensor', split_axis=1, concat_axis=0, tiled=True)  27.3 us
    pallas_call x1, Pallas kernels, scan(): pl.pallas_call(main_kernel, out_shape=(jax.ShapeDtypeStruct((ROWS, GC), F...  18.8 us
    all_to_all x1, waiting for transfers between devices, shards(): lax.all_to_all(z_in, 'tensor', split_axis=1, concat_axis=0, tiled=True)  17 us
    all_to_all x1, waiting for transfers between devices, shards(): lax.all_to_all(pack(bc_in, dt_in), 'tensor', split_axis=0, concat_axis=0,...  15.9 us
    unnamed x41, local copies, waits for them, and re-layouts  10.1 us
    all_to_all x1, starting transfers between devices, shards(): lax.all_to_all(pack(bc_in, dt_in), 'tensor', split_axis=0, concat_axis=0,...  8.57 us
    concatenate x2, local copies, waits for them, and re-layouts, mover(): return jnp.concatenate([state, small, jnp.zeros((2, STATE), F32)], axis=0)  6.39 us
    pallas_call x1, Pallas kernels, prep(): pl.pallas_call(prep_kernel, out_shape=(jax.ShapeDtypeStruct((CHUNKS, STAT...  5.87 us
  transfers between devices with their start and end apart: 7, of which 5 were waited for; matrix products, arithmetic and copies ran while one was open for 12% of the time, Pallas kernels for 19%

commit v1 on v0

--- a/solution.py
+++ b/solution.py
@@ -22,6 +22,17 @@
 SRC_ROWS = ROWS // TENSOR
 EPSILON = 1e-05
 LOG2E = math.log2(math.e)
+LANES = 2 * STATE
+TILES = GC // LANES
+BC_ROW = TILES * SRC_ROWS
+DT_ROW = BC_ROW + SRC_ROWS
+BLOCK_ROWS = DT_ROW + GH
+MOVER_ROWS = GC + 32
+GATE_ROWS = 128
+ORDER = (4, 3, 5, 2, 6, 1, 7)
+FIRST = (4, 3, 5)
+SECOND = (2, 6)
+THIRD = (1, 7)
 MIB = 1 << 20
 
 F32 = jnp.float32
@@ -105,21 +116,104 @@
         terms_ref[16 * i : 16 * i + 16, lanes] = part
 
 
-def pack_kernel(bc, dt, out):
-    dt_t = dt[...].astype(F32).T.astype(BF16)
-    for t in range(TENSOR):
-        out[t, 0:SRC_ROWS, :] = bc[:, 2 * STATE * t : 2 * STATE * (t + 1)]
-        out[t, SRC_ROWS : SRC_ROWS + GH, 0:SRC_ROWS] = dt_t[GH * t : GH * (t + 1), :]
-        out[t, SRC_ROWS : SRC_ROWS + GH, SRC_ROWS:] = jnp.zeros((GH, SRC_ROWS), BF16)
+def copy_all(copies, sems):
+    started = [
+        pltpu.make_async_copy(source, target, sems.at[i])
+        for i, (source, target) in enumerate(copies)
+    ]
+    for copy in started:
+        copy.start()
+    for copy in started:
+        copy.wait()
+
+
+def pack_kernel(offsets, here, x, bc, dt, *rest):
+    count = len(offsets)
+    outs, (stage, dt_all, dt_turned, sems, out_sems, dt_sem) = rest[:count], rest[count:]
+    dt_load = pltpu.make_async_copy(dt, dt_all, dt_sem)
+    dt_load.start()
+    loads = []
+    for n, d in enumerate(offsets):
+        to = (here[0] + d) % TENSOR
+        sources = []
+        for i in range(TILES):
+            lanes = pl.ds(pl.multiple_of(to * GC + LANES * i, LANES), LANES)
+            sources.append(x.at[:, lanes])
+        sources.append(bc.at[:, pl.ds(pl.multiple_of(to * LANES, LANES), LANES)])
+        loads.append(
+            [
+                pltpu.make_async_copy(
+                    source,
+                    stage.at[n, SRC_ROWS * i : SRC_ROWS * (i + 1), :],
+                    sems.at[n * (TILES + 1) + i],
+                )
+                for i, source in enumerate(sources)
+            ]
+        )
+        for copy in loads[-1]:
+            copy.start()
+    dt_load.wait()
+    dt_turned[...] = dt_all[...].astype(F32).T.astype(BF16)
+    stores = []
+    for n, d in enumerate(offsets):
+        to = (here[0] + d) % TENSOR
+        heads = pl.ds(pl.multiple_of(to * GH, GH), GH)
+        stage[n, DT_ROW:BLOCK_ROWS, 0:SRC_ROWS] = dt_turned[heads, :]
+        stage[n, DT_ROW:BLOCK_ROWS, SRC_ROWS:] = jnp.zeros((GH, LANES - SRC_ROWS), BF16)
+        for copy in loads[n]:
+            copy.wait()
+        stores.append(pltpu.make_async_copy(stage.at[n], outs[n], out_sems.at[n]))
+        stores[-1].start()
+    for copy in stores:
+        copy.wait()
+
+
+def mover_kernel(slots, own, small, right_out, left_out, sems):
+    outs = (right_out, left_out)
+    for i in range(2):
+        outs[i][GC:MOVER_ROWS, :] = small[i]
+    copy_all([(own.at[slots[i]], outs[i].at[0:GC, :]) for i in range(2)], sems)
+
+
+def init_kernel(seg, own, lft, rgt, init_out):
+    def load_state(k, block_of):
+        for b in range(GC // 128):
+            init_out[k, :, 128 * b : 128 * (b + 1)] = block_of(b).T
+
+    @pl.loop(0, SLOTS)
+    def _(k):
+        source = seg[8 + k]
+
+        @pl.when(source < SLOTS)
+        def _():
+            load_state(k, lambda b: own[jnp.minimum(source, SLOTS - 1), 128 * b : 128 * (b + 1), :])
+
+        @pl.when(source == SLOTS)
+        def _():
+            load_state(k, lambda b: lft[128 * b : 128 * (b + 1), :])
+
+        @pl.when(source == SLOTS + 1)
+        def _():
+            load_state(k, lambda b: rgt[128 * b : 128 * (b + 1), :])
+
+
+def source_of(here, d):
+    return (here[0] + (TENSOR - d)) % TENSOR
 
 
 def prep_kernel(
     seg,
-    bcdt,
+    here,
+    *rest,
+):
+    prep_body(seg, here, rest[:TENSOR], *rest[TENSOR:])
+
+
+def prep_body(
+    seg,
+    here,
+    blocks,
     conv_state,
-    own,
-    lft,
-    rgt,
     param,
     rate,
     bias,
@@ -130,13 +224,19 @@
     row_out,
     dec_out,
     last_out,
-    init_out,
     bc_rows,
+    dt_rows,
     b_rows,
     terms,
+    sems,
 ):
-    for s in range(TENSOR):
-        bc_rows[SRC_ROWS * s : SRC_ROWS * (s + 1), :] = bcdt[s, 0:SRC_ROWS, :]
+    copies = []
+    for d in range(TENSOR):
+        source = source_of(here, d)
+        rows = pl.ds(pl.multiple_of(source * SRC_ROWS, SRC_ROWS), SRC_ROWS)
+        copies.append((blocks[d].at[BC_ROW:DT_ROW, :], bc_rows.at[rows, :]))
+        copies.append((blocks[d].at[DT_ROW:BLOCK_ROWS, :], dt_rows.at[source]))
+    copy_all(copies, sems)
     every = slice(0, 2 * STATE)
     last = last_rows(bc_rows, every, seg)
     last_out[...] = last
@@ -164,7 +264,7 @@
         up_to = jnp.where(same & (row_id <= col_id), 1.0, 0.0).astype(BF16)
         after = jnp.where(same & (row_id > col_id), 1.0, 0.0).astype(BF16)
         raw = jnp.concatenate(
-            [bcdt[s, SRC_ROWS : SRC_ROWS + GH, 0:SRC_ROWS] for s in (2 * c, 2 * c + 1)], axis=1
+            [dt_rows[s, :, 0:SRC_ROWS] for s in (2 * c, 2 * c + 1)], axis=1
         ).astype(F32) + bias[...]
         step = jnp.maximum(raw, 0.0) + jnp.log1p(jnp.exp(-jnp.abs(raw)))
         log_decay = step * rate[...] * (-LOG2E)
@@ -188,30 +288,15 @@
     dec_hi, dec_lo = split2(decay)
     dec_out[...] = mm(dec_hi, spread) + mm(dec_lo, spread)
 
-    def load_state(k, ref_of):
-        for b in range(GC // 128):
-            init_out[k, :, 128 * b : 128 * (b + 1)] = ref_of(b).T
-
-    @pl.loop(0, SLOTS)
-    def _(k):
-        source = seg[8 + k]
-
-        @pl.when(source < SLOTS)
-        def _():
-            load_state(k, lambda b: own[jnp.minimum(source, SLOTS - 1), 128 * b : 128 * (b + 1), :])
-
-        @pl.when(source == SLOTS)
-        def _():
-            load_state(k, lambda b: lft[128 * b : 128 * (b + 1), :])
-
-        @pl.when(source == SLOTS + 1)
-        def _():
-            load_state(k, lambda b: rgt[128 * b : 128 * (b + 1), :])
-
-
-def main_kernel(
+
+def main_kernel(seg, here, *rest):
+    main_body(seg, here, rest[:TENSOR], *rest[TENSOR:])
+
+
+def main_body(
     seg,
-    x_in,
+    here,
+    blocks,
     conv_state,
     param,
     skip,
@@ -222,6 +307,7 @@
     row_in,
     dec_in,
     init_in,
+    last_bc,
     y_out,
     own_out,
     lft_out,
@@ -234,7 +320,23 @@
     inter,
     spread_e,
     spread_w,
+    x_in,
+    tail,
+    sems,
+    y_stage,
+    y_sems,
 ):
+    def store(c):
+        rows = pl.ds(pl.multiple_of(c * Q, Q), Q)
+        return pltpu.make_async_copy(y_stage.at[rows, :], y_out.at[rows, :], y_sems.at[c])
+
+    copies = []
+    for d in range(TENSOR):
+        rows = pl.ds(pl.multiple_of(source_of(here, d) * SRC_ROWS, SRC_ROWS), SRC_ROWS)
+        for i in range(TILES):
+            part = blocks[d].at[SRC_ROWS * i : SRC_ROWS * (i + 1), :]
+            copies.append((part, x_in.at[rows, LANES * i : LANES * (i + 1)]))
+    copy_all(copies, sems)
     terms[...] = jnp.zeros_like(terms)
     targets = boundary_targets((1, 128), 1, seg)
     for lt in range(GC // 256):
@@ -316,54 +418,138 @@
                     spread = col[part, h : h + 1] - row_in[c, h : h + 1, 0:depth]
                     scores = (jnp.exp2(jnp.minimum(spread, 126.0)) * mix).astype(BF16)
                     total = total + mm(scores, x_one[0:depth])
-                y_out[pl.ds(r0 + 128 * half, 128), lanes] = total
+                y_stage[pl.ds(r0 + 128 * half, 128), lanes] = total
+        store(c).start()
+
+    def send_back(k, out):
+        for b in range(GC // 128):
+            part = slice(128 * b, 128 * (b + 1))
+            out[part, :] = state[k, :, part].T.astype(BF16)
+        lines = (GC + LANES) // 128
+        tail[...] = jnp.zeros_like(tail)
+        for j in range(3):
+            row = pl.ds(3 * k + j, 1)
+            line = jnp.concatenate([last_out[row, :], last_bc[row, :]], axis=1)
+            for b in range(lines):
+                place = slice(j * lines + b, j * lines + b + 1)
+                tail[place, :] = line[:, 128 * b : 128 * (b + 1)]
+        out[GC:MOVER_ROWS, :] = tail[...].astype(BF16)
 
     @pl.loop(0, SLOTS)
     def _(k):
         source = seg[8 + k]
-        for b in range(GC // 128):
-            part = slice(128 * b, 128 * (b + 1))
-            block = state[k, :, part].T
-
-            @pl.when(source < SLOTS)
-            def _():
-                own_out[jnp.minimum(source, SLOTS - 1), part, :] = block
-
-            @pl.when(source == SLOTS)
-            def _():
-                lft_out[part, :] = block.astype(BF16)
-
-            @pl.when(source == SLOTS + 1)
-            def _():
-                rgt_out[part, :] = block.astype(BF16)
-
-
-def gate_kernel(y_in, z_in, gain, out):
-    gated = y_in[...] * silu(z_in[...].astype(F32))
-    mean = jnp.sum(gated * gated, axis=1, keepdims=True) * (1.0 / GC)
-    out[...] = (gated * lax.rsqrt(mean + EPSILON) * gain[...]).astype(BF16)
+
+        @pl.when(source < SLOTS)
+        def _():
+            for b in range(GC // 128):
+                part = slice(128 * b, 128 * (b + 1))
+                own_out[jnp.minimum(source, SLOTS - 1), part, :] = state[k, :, part].T
+
+        @pl.when(source == SLOTS)
+        def _():
+            send_back(k, lft_out)
+
+        @pl.when(source == SLOTS + 1)
+        def _():
+            send_back(k, rgt_out)
+
+    @pl.loop(0, CHUNKS)
+    def _(c):
+        store(c).wait()
+
+
+def gate_kernel(y_in, z_in, gain, out, y_stage, stage, load_sems, sems):
+    def rows_of(i):
+        return pl.ds(pl.multiple_of(i * GATE_ROWS, GATE_ROWS), GATE_ROWS)
+
+    def load(i):
+        return pltpu.make_async_copy(
+            y_in.at[rows_of(i), :], y_stage.at[rows_of(i), :], load_sems.at[i]
+        )
+
+    def store(i):
+        return pltpu.make_async_copy(stage.at[rows_of(i), :], out.at[rows_of(i), :], sems.at[i])
+
+    for i in range(ROWS // GATE_ROWS):
+        load(i).start()
+
+    @pl.loop(0, ROWS // GATE_ROWS)
+    def _(i):
+        load(i).wait()
+        for part in range(GATE_ROWS // 16):
+            rows = pl.ds(pl.multiple_of(i * GATE_ROWS + 16 * part, 16), 16)
+            gated = y_stage[rows, :] * silu(z_in[rows, :].astype(F32))
+            mean = jnp.sum(gated * gated, axis=1, keepdims=True) * (1.0 / GC)
+            stage[rows, :] = (gated * lax.rsqrt(mean + EPSILON) * gain[...]).astype(BF16)
+        store(i).start()
+
+    @pl.loop(0, ROWS // GATE_ROWS)
+    def _(i):
+        store(i).wait()
 
 
 VMEM = pl.BlockSpec(memory_space=pltpu.VMEM)
 SMEM = pl.BlockSpec(memory_space=pltpu.SMEM)
+ANY = pl.BlockSpec(memory_space=pl.ANY)
+HBM = pl.BlockSpec(memory_space=pltpu.HBM)
+
+
+def in_hbm(value):
+    return pltpu.with_memory_space_constraint(value, pltpu.HBM)
 
 
 def params(mib):
     return pltpu.CompilerParams(vmem_limit_bytes=mib * MIB)
 
 
-def pack(bc_in, dt_in):
+def pack(offsets, here, x_in, bc_in, dt_in):
+    count = len(offsets)
+    blocks = pl.pallas_call(
+        functools.partial(pack_kernel, offsets),
+        out_shape=(pltpu.HBM((BLOCK_ROWS, LANES), BF16),) * count,
+        in_specs=[SMEM, HBM, HBM, HBM],
+        out_specs=(HBM,) * count,
+        scratch_shapes=[
+            pltpu.VMEM((count, BLOCK_ROWS, LANES), BF16),
+            pltpu.VMEM((SRC_ROWS, HEADS), BF16),
+            pltpu.VMEM((HEADS, SRC_ROWS), BF16),
+            pltpu.SemaphoreType.DMA((count * (TILES + 1),)),
+            pltpu.SemaphoreType.DMA((count,)),
+            pltpu.SemaphoreType.DMA,
+        ],
+        compiler_params=params(8),
+        name="pack",
+    )(here, in_hbm(x_in), in_hbm(bc_in), in_hbm(dt_in))
+    return dict(zip(offsets, blocks))
+
+
+def movers(slots, own, small):
     return pl.pallas_call(
-        pack_kernel,
-        out_shape=jax.ShapeDtypeStruct((TENSOR, SRC_ROWS + GH, 2 * STATE), BF16),
-        in_specs=[VMEM, VMEM],
+        mover_kernel,
+        out_shape=(jax.ShapeDtypeStruct((MOVER_ROWS, STATE), F32),) * 2,
+        in_specs=[SMEM, HBM, VMEM],
+        out_specs=(VMEM,) * 2,
+        scratch_shapes=[pltpu.SemaphoreType.DMA((2,))],
+        compiler_params=params(8),
+        name="movers",
+    )(slots, in_hbm(own), small)
+
+
+def initial(seg, own, lft, rgt):
+    return pl.pallas_call(
+        init_kernel,
+        out_shape=jax.ShapeDtypeStruct((SLOTS, STATE, GC), F32),
+        in_specs=[SMEM] + [VMEM] * 3,
         out_specs=VMEM,
         compiler_params=params(8),
-        name="pack",
-    )(bc_in, dt_in)
-
-
-def prep(seg, bcdt, conv_state, own, lft, rgt, param, rate, bias):
+        cost_estimate=pl.CostEstimate(
+            flops=2_000_000_000, bytes_accessed=4 * MIB, transcendentals=0
+        ),
+        name="initial",
+    )(seg, own, lft, rgt)
+
+
+def prep(seg, here, blocks, conv_state, param, rate, bias):
     return pl.pallas_call(
         prep_kernel,
         out_shape=(
@@ -374,36 +560,37 @@
             jax.ShapeDtypeStruct((CHUNKS, GH, Q), F32),
             jax.ShapeDtypeStruct((16, GC), F32),
             jax.ShapeDtypeStruct((16, 2 * STATE), F32),
-            jax.ShapeDtypeStruct((SLOTS, STATE, GC), F32),
         ),
-        in_specs=[SMEM] + [VMEM] * 8,
-        out_specs=(VMEM,) * 8,
+        in_specs=[SMEM, SMEM] + [ANY] * TENSOR + [VMEM] * 4,
+        out_specs=(VMEM,) * 7,
         scratch_shapes=[
             pltpu.VMEM((ROWS, 2 * STATE), BF16),
+            pltpu.VMEM((TENSOR, GH, LANES), BF16),
             pltpu.VMEM((ROWS, STATE), BF16),
             pltpu.VMEM((128, 2 * STATE), BF16),
+            pltpu.SemaphoreType.DMA((2 * TENSOR,)),
         ],
-        compiler_params=params(24),
+        compiler_params=params(8),
         cost_estimate=pl.CostEstimate(
             flops=6_000_000_000, bytes_accessed=8 * MIB, transcendentals=500_000
         ),
         name="prep",
-    )(seg, bcdt, conv_state, own, lft, rgt, param, rate, bias)
-
-
-def scan(seg, x_rows, conv_state, param, skip, prepared):
-    b_t, c_rows, mix, col, row, dec, init = prepared
+    )(seg, here, *blocks, conv_state, param, rate, bias)
+
+
+def scan(seg, here, blocks, conv_state, param, skip, prepared, init):
+    b_t, c_rows, mix, col, row, dec, last_bc = prepared
     return pl.pallas_call(
         main_kernel,
         out_shape=(
-            jax.ShapeDtypeStruct((ROWS, GC), F32),
+            pltpu.HBM((ROWS, GC), F32),
             jax.ShapeDtypeStruct((SLOTS, GC, STATE), F32),
-            jax.ShapeDtypeStruct((GC, STATE), BF16),
-            jax.ShapeDtypeStruct((GC, STATE), BF16),
+            jax.ShapeDtypeStruct((MOVER_ROWS, STATE), BF16),
+            jax.ShapeDtypeStruct((MOVER_ROWS, STATE), BF16),
             jax.ShapeDtypeStruct((16, GC), F32),
         ),
-        in_specs=[SMEM] + [VMEM] * 11,
-        out_specs=(VMEM,) * 5,
+        in_specs=[SMEM, SMEM] + [ANY] * TENSOR + [VMEM] * 11,
+        out_specs=(HBM,) + (VMEM,) * 4,
         scratch_shapes=[
             pltpu.VMEM((128, GC), BF16),
             pltpu.VMEM((ROWS, GC), BF16),
@@ -412,39 +599,58 @@
             pltpu.VMEM((Q, GC), F32),
             pltpu.VMEM((256, GC), BF16),
             pltpu.VMEM((256, GC), BF16),
+            pltpu.VMEM((ROWS, GC), BF16),
+            pltpu.VMEM((32, STATE), F32),
+            pltpu.SemaphoreType.DMA((TENSOR * TILES,)),
+            pltpu.VMEM((ROWS, GC), F32),
+            pltpu.SemaphoreType.DMA((CHUNKS,)),
         ],
-        compiler_params=params(40),
+        compiler_params=params(20),
         cost_estimate=pl.CostEstimate(
             flops=20_000_000_000, bytes_accessed=16 * MIB, transcendentals=5_000_000
         ),
         name="scan",
-    )(seg, x_rows, conv_state, param, skip, b_t, c_rows, mix, col, row, dec, init)
+    )(
+        seg, here, *blocks, conv_state, param, skip, b_t, c_rows, mix, col, row, dec, init, last_bc
+    )
 
 
 def gate(y, z_rows, gain):
-    block = 128
     return pl.pallas_call(
         gate_kernel,
         out_shape=jax.ShapeDtypeStruct((ROWS, GC), BF16),
-        grid=(ROWS // block,),
-        in_specs=[
-            pl.BlockSpec((block, GC), lambda i: (i, 0)),
-            pl.BlockSpec((block, GC), lambda i: (i, 0)),
-            pl.BlockSpec((1, GC), lambda i: (0, 0)),
+        in_specs=[HBM, VMEM, VMEM],
+        out_specs=ANY,
+        scratch_shapes=[
+            pltpu.VMEM((ROWS, GC), F32),
+            pltpu.VMEM((ROWS, GC), BF16),
+            pltpu.SemaphoreType.DMA((ROWS // GATE_ROWS,)),
+            pltpu.SemaphoreType.DMA((ROWS // GATE_ROWS,)),
         ],
-        out_specs=pl.BlockSpec((block, GC), lambda i: (i, 0)),
-        compiler_params=params(16),
+        compiler_params=params(12),
         cost_estimate=pl.CostEstimate(
             flops=20_000_000, bytes_accessed=8 * MIB, transcendentals=1_000_000
         ),
         name="gate",
-    )(y, z_rows, gain)
+    )(in_hbm(y), z_rows, gain)
 
 
 def shifted(value, steps):
     count = lax.axis_size("dp")
     pairs = [(source, (source + steps) % count) for source in range(count)]
     return lax.ppermute(value, "dp", pairs)
+
+
+def rotated(value, steps):
+    count = lax.axis_size("tensor")
+    pairs = [(source, (source + steps) % count) for source in range(count)]
+    return lax.ppermute(value, "tensor", pairs)
+
+
+def after(value, *earlier):
+    if not earlier:
+        return value
+    return lax.optimization_barrier((value, *earlier))[0]
 
 
 def plan(lengths, prefill_owner, row_start, me, left, right):
@@ -489,9 +695,15 @@
     me = lax.axis_index("dp")
     left = (me + dp_count - 1) % dp_count
     right = (me + 1) % dp_count
-    bcdt = lax.all_to_all(pack(bc_in, dt_in), "tensor", split_axis=0, concat_axis=0, tiled=True)
-    x_rows = lax.all_to_all(x_in, "tensor", split_axis=1, concat_axis=0, tiled=True)
-    z_rows = lax.all_to_all(z_in, "tensor", split_axis=1, concat_axis=0, tiled=True)
+    here = lax.axis_index("tensor")
+    here_ref = here.astype(jnp.int32)[None]
+    packed = pack(FIRST, here_ref, x_in, bc_in, dt_in)
+    packed |= pack(
+        SECOND + THIRD + (0,), after(here_ref, packed[FIRST[0]]), x_in, bc_in, dt_in
+    )
+    blocks = {0: packed[0]}
+    for d in FIRST:
+        blocks[d] = rotated(packed[d], d)
 
     seg, codes, slot_right, slot_left = plan(lengths, prefill_owner, row_start, me, left, right)
 
@@ -500,13 +712,19 @@
     width = conv.shape[2]
     lines = 3 * width // STATE
 
-    def mover(slot):
-        state = lax.dynamic_index_in_dim(own, slot, 0, keepdims=False)
+    def small_mover(slot):
         small = lax.dynamic_index_in_dim(conv, slot, 0, keepdims=False).reshape(lines, STATE)
-        return jnp.concatenate([state, small, jnp.zeros((2, STATE), F32)], axis=0)
-
-    from_left = shifted(mover(slot_right), 1)
-    from_right = shifted(mover(slot_left), -1)
+        return jnp.concatenate([small, jnp.zeros((2, STATE), F32)], axis=0)
+
+    move_right, move_left = movers(
+        after(jnp.stack([slot_right, slot_left]).astype(jnp.int32), packed[0]),
+        own,
+        jnp.stack([small_mover(slot_right), small_mover(slot_left)]),
+    )
+    from_left = shifted(move_right, 1)
+    from_right = shifted(move_left, -1)
+    for d in SECOND:
+        blocks[d] = rotated(after(packed[d], from_left, from_right), d)
 
     def small_of(packed):
         return packed[GC : GC + lines].reshape(1, 3, width)
@@ -516,36 +734,49 @@
     conv_init = jnp.sum(jnp.where(match[:, :, None, None], candidates[None], 0.0), axis=1)
     conv_init = jnp.concatenate([conv_init.reshape(3 * SLOTS, width), jnp.zeros((4, width), F32)])
 
-    b_t, c_rows, mix, col, row, dec, last_bc, init = prep(
+    z_sent = z_in.reshape(SRC_ROWS, TENSOR, GC).transpose(1, 0, 2)
+    init = initial(seg, own, from_left, from_right)
+    conv_init, init, z_sent, seg, gain, skip, rate, bias = lax.optimization_barrier(
+        (
+            conv_init,
+            init,
+            z_sent,
+            seg,
+            norm_gain[None, :],
+            jnp.repeat(skip_gain, HEADDIM)[None, :],
+            decay_rate[:, None],
+            dt_bias[:, None],
+        )
+    )
+    for d in THIRD:
+        blocks[d] = rotated(after(packed[d], conv_init, z_sent, *[blocks[e] for e in FIRST[1:]]), d)
+    z_sent = after(z_sent, *[blocks[e] for e in FIRST])
+    z_rows = lax.all_to_all(z_sent, "tensor", split_axis=0, concat_axis=0, tiled=True)
+    z_rows = z_rows.reshape(ROWS, GC)
+
+    in_order = [blocks[d] for d in range(TENSOR)]
+    prepared = prep(
         seg,
-        bcdt,
+        here_ref,
+        in_order,
         conv_init[:, GC:],
-        own,
-        from_left,
-        from_right,
         conv_bc_param,
-        decay_rate[:, None],
-        dt_bias[:, None],
+        rate,
+        bias,
     )
     y, own_new, back_left, back_right, last_x = scan(
         seg,
-        x_rows,
+        here_ref,
+        in_order,
         conv_init[:, :GC],
         conv_x_param,
-        jnp.repeat(skip_gain, HEADDIM)[None, :],
-        (b_t, c_rows, mix, col, row, dec, init),
+        skip,
+        prepared,
+        init,
     )
-    last = jnp.concatenate([last_x, last_bc], axis=1)[: 3 * SLOTS].reshape(SLOTS, 3, width)
-
-    def last_of(code):
-        return jnp.sum(jnp.where((codes == code)[:, None, None], last, 0.0), axis=0)
-
-    def back(state, code):
-        small = last_of(code).astype(BF16).reshape(lines, STATE)
-        return jnp.concatenate([state, small, jnp.zeros((2, STATE), BF16)], axis=0)
-
-    returned_right = shifted(back(back_left, SLOTS), -1)
-    returned_left = shifted(back(back_right, SLOTS + 1), 1)
+    returned_right = shifted(back_left, -1)
+    returned_left = shifted(back_right, 1)
+    last = jnp.concatenate([last_x, prepared[6]], axis=1)[: 3 * SLOTS].reshape(SLOTS, 3, width)
 
     new_ssm = own_new
     for packed, slot in ((returned_right, slot_right), (returned_left, slot_left)):
@@ -557,13 +788,11 @@
         new_conv = jnp.where(
             (slots == slot)[:, None, None], small_of(packed).astype(F32), new_conv
         )
-    y_out = gate(y, z_rows, norm_gain[None, :])
-    return (
-        y_out,
-        new_ssm.reshape(ssm_state.shape),
-        new_conv[:, :, :GC],
-        new_conv[:, :, GC:],
-    )
+    new_cx, new_cbc = new_conv[:, :, :GC], new_conv[:, :, GC:]
+
+    y, new_ssm, new_cx, new_cbc = lax.optimization_barrier((y, new_ssm, new_cx, new_cbc))
+    y_out = gate(y, z_rows, gain)
+    return y_out, new_ssm.reshape(ssm_state.shape), new_cx, new_cbc
 
 
 def solution(mesh):

time: 152 us -> 122 us (0.80)
  waiting for transfers between devices: 62.7 us -> 34.4 us
  local copies, waits for them, and re-layouts: 25.8 us -> 6.67 us
  starting transfers between devices: 21 us -> 31.7 us
  Pallas kernels: 29.5 us -> 37.2 us
    all_to_all x3 -> x1, waiting for transfers between devices: 60.2 us -> 14.6 us  [shards(): lax.all_to_all(z_sent, 'tensor', split_axis=0, concat_axis=0, tiled=True)]
    ppermute x0 -> x7, starting transfers between devices: none -> 17.6 us  [rotated(): return lax.ppermute(value, 'tensor', pairs)]
    ppermute x0 -> x7, waiting for transfers between devices: none -> 11.7 us  [rotated(): return lax.ppermute(value, 'tensor', pairs)]
    pallas_call x2 -> x5, Pallas kernels: 19.7 us -> 27.9 us  [the longest x1 18.4 us: scan(): pl.pallas_call(main_kernel, out_shape=(pltpu.HBM((ROWS, GC), F32), jax.Sh...]
    unnamed x41 -> x33, local copies, waits for them, and re-layouts: 10.1 us -> 2.64 us
    concatenate x4 -> x1, local copies, waits for them, and re-layouts: 6.69 us -> 0.01 us  [shards(): jnp.concatenate([conv_init.reshape(3 * SLOTS, width), jnp.zeros((4, width...]
    all_to_all x3 -> x1, starting transfers between devices: 17.4 us -> 11.6 us  [shards(): lax.all_to_all(z_sent, 'tensor', split_axis=0, concat_axis=0, tiled=True)]
    ppermute x4, waiting for transfers between devices: 2.47 us -> 8.06 us  [shifted(): return lax.ppermute(value, 'dp', pairs)]
  transfers between devices with their start and end apart: 7 -> 12, of which waited for: 5 -> 7; matrix products, arithmetic and copies ran while one was open for 12% -> 9% of each run, Pallas kernels for 19% -> 26%
where the time goes in v1:
time: 122 us; the launch traced here: 121 us
  Pallas kernels  37.2 us (30%)
  waiting for transfers between devices  34.4 us (28%)
  starting transfers between devices  31.7 us (26%)
  local copies, waits for them, and re-layouts  6.67 us (5%)
  other arithmetic  5.92 us (5%)
  between operations  5.09 us (4%)
    pallas_call x1, Pallas kernels, scan(): pl.pallas_call(main_kernel, out_shape=(pltpu.HBM((ROWS, GC), F32), jax.Sh...  18.4 us
    ppermute x7, starting transfers between devices, rotated(): return lax.ppermute(value, 'tensor', pairs)  17.6 us
    all_to_all x1, waiting for transfers between devices, shards(): lax.all_to_all(z_sent, 'tensor', split_axis=0, concat_axis=0, tiled=True)  14.6 us
    ppermute x7, waiting for transfers between devices, rotated(): return lax.ppermute(value, 'tensor', pairs)  11.7 us
    all_to_all x1, starting transfers between devices, shards(): lax.all_to_all(z_sent, 'tensor', split_axis=0, concat_axis=0, tiled=True)  11.6 us
    ppermute x4, waiting for transfers between devices, shifted(): return lax.ppermute(value, 'dp', pairs)  8.06 us
    pallas_call x1, Pallas kernels, prep(): pl.pallas_call(prep_kernel, out_shape=(jax.ShapeDtypeStruct((CHUNKS, STAT...  5.62 us
    pallas_call x2, Pallas kernels, pack(): pl.pallas_call(functools.partial(pack_kernel, offsets), out_shape=(pltpu....  5.37 us
  transfers between devices with their start and end apart: 12, of which 7 were waited for; matrix products, arithmetic and copies ran while one was open for 9% of the time, Pallas kernels for 26%

profile of v1, /device:TPU:36, one launch (start us, length us, event | category | flops | bytes accessed | tf_op | source)
XLA Modules:
  0.0 121.1 jit_solution(17106196978944559621)
XLA Ops:
  0.6 0.0 copy-start.10
  0.6 0.0 copy-start.7
  0.7 0.0 copy-start.8
  0.7 2.4 %pack.2 = (bf16[656,256]{1,0:T(8,128)(2,1)}, bf16[656,256]{1,0:T(8,128)(2,1)}, bf16[656,256]{1,0:T(8,128)(2,1)}) custom-call(s32[1]{0:T(128)} %bitcast.2.here, bf16[128,8192]{1,0:T(8,128)(2,1)} %x.9, bf16[128,2048]{1,0:T(8,128)(2,1)} %bc.3, bf16[128,128]{1,0:T(8,128)(2,1)} %dt.3), custom_call_target="tpu_custom_call" | custom-call | tf_op jit(solution)/shard_map/pack/pallas_call | solution.py:507
  3.1 5.9 %collective-permute-start.2 = (bf16[656,256]{1,0:T(8,128)(2,1)}, bf16[656,256]{1,0:T(8,128)(2,1)}, u32[]{:S(2)}, u32[]{:S(2)}) collective-permute-start(bf16[656,256]{1,0:T(8,128)(2,1)} %get-tuple-element.55), channel_id=1, source_target_pairs={{0,3},{1,4},{2,5},{3,6},{4,7},{5,0},{6,1},{7,2},{8,11},{9,12},{10,... | collective-permute-start | bytes 1007624 | tf_op jit(solution)/shard_map/ppermute | solution.py:647
  9.0 0.1 collective-permute-start.3
  9.1 5.4 %collective-permute-start.6 = (bf16[656,256]{1,0:T(8,128)(2,1)}, bf16[656,256]{1,0:T(8,128)(2,1)}, u32[]{:S(2)}, u32[]{:S(2)}) collective-permute-start(bf16[656,256]{1,0:T(8,128)(2,1)} %get-tuple-element.45), channel_id=1, source_target_pairs={{0,4},{1,5},{2,6},{3,7},{4,0},{5,1},{6,2},{7,3},{8,12},{9,13},{10,... | collective-permute-start | bytes 1007624 | tf_op jit(solution)/shard_map/ppermute | solution.py:647
  14.5 0.0 copy-done.10
  14.5 0.6 fusion.2
  17.7 0.0 copy-done.7
  19.1 0.1 dynamic-slice_reduce_fusion.1
  19.2 0.0 copy-start.11
  19.2 3.0 %pack.3 = (bf16[656,256]{1,0:T(8,128)(2,1)}, bf16[656,256]{1,0:T(8,128)(2,1)}, bf16[656,256]{1,0:T(8,128)(2,1)}, bf16[656,256]{1,0:T(8,128)(2,1)}, bf16[656,256]{1,0:T(8,128)(2,1)}) custom-call(s32[1]{0:T(128)} %bitcast.2.here, bf16[128,8192]{1,0:T(8,128)(2,1)} %x.9, bf16[128,2048]{1,0:T(8,128)(2,1)} %bc.3, bf16[128,128]{1,0:T(8,128)(2,1)} %dt.3), custom_call_target="tpu_custom_call" | custom-call | tf_op jit(solution)/shard_map/pack/pallas_call | solution.py:507
  22.2 1.4 %pad_add_fusion.slots = s32[2]{0:T(128)S(1)} fusion(s32[1]{0:T(128)} %bitcast.1, s32[1]{0:T(128)} %bitcast), kind=kLoop, calls=%fused_computation.36 | loop fusion | flops 2 | bytes 16 | tf_op jit(solution)/shard_map/stack | solution.py:720
  23.6 2.7 %movers.1 = (f32[1056,128]{1,0:T(8,128)}, f32[1056,128]{1,0:T(8,128)}) custom-call(s32[2]{0:T(128)S(1)} %pad_add_fusion.slots, f32[4,1024,128]{2,1,0:T(8,128)} %bitcast.31, f32[2,32,128]{2,1,0:T(8,128)S(1)} %pad_maximum_fusion.2.small), custom_call_target="tpu_custom_call" | custom-call | tf_op jit(solution)/shard_map/movers/pallas_call | solution.py:527
  26.3 0.1 collective-permute-start
  26.4 1.7 %collective-permute-start.1 = (f32[1056,128]{1,0:T(8,128)}, f32[1056,128]{1,0:T(8,128)S(1)}, u32[]{:S(2)}, u32[]{:S(2)}) collective-permute-start(f32[1056,128]{1,0:T(8,128)} %get-tuple-element.50), channel_id=1, source_target_pairs={{0,248},{8,0},{16,8},{24,16},{32,24},{40,32},{48,40},{56,48},{64,5... | collective-permute-start | bytes 1622024 | tf_op jit(solution)/shard_map/ppermute | solution.py:641
  28.2 0.1 broadcast_in_dim.158
  28.2 0.1 broadcast_in_dim_reshape.4.rest_10_
  28.3 3.3 %copy.44 = bf16[16,8,8,1024]{3,2,0,1:T(8,128)(2,1)} copy(bf16[16,8,8,1024]{3,2,1,0:T(8,128)(2,1)} %bitcast.35) | data formatting | bytes 4194304 | tf_op jit(solution)/shard_map/reshape | solution.py:737
  31.6 0.0 copy-done.9
  31.6 0.2 convert_reduce_fusion
  31.8 0.1 select_reduce_fusion.2
  32.0 0.7 iota_compare_fusion.3
  32.6 0.1 pad_add_fusion.1.seg
  32.7 2.7 %collective-permute-done.lft = f32[1056,128]{1,0:T(8,128)S(1)} collective-permute-done((f32[1056,128]{1,0:T(8,128)}, f32[1056,128]{1,0:T(8,128)S(1)}, u32[]{:S(2)}, u32[]{:S(2)}) %collective-permute-start) | collective-permute-done | bytes 540704 | tf_op jit(solution)/shard_map/ppermute | solution.py:641
  35.4 0.0 collective-permute-done.1.rgt
  35.5 0.1 copy.34
  35.6 0.2 select_reduce_fusion
  35.8 0.3 collective-permute-start.5
  36.1 3.9 %collective-permute-start.7 = (bf16[656,256]{1,0:T(8,128)(2,1)}, bf16[656,256]{1,0:T(8,128)(2,1)}, u32[]{:S(2)}, u32[]{:S(2)}) collective-permute-start(bf16[656,256]{1,0:T(8,128)(2,1)} %get-tuple-element.61), channel_id=1, source_target_pairs={{0,6},{1,7},{2,0},{3,1},{4,2},{5,3},{6,4},{7,5},{8,14},{9,15},{10,... | collective-permute-start | bytes 1007624 | tf_op jit(solution)/shard_map/ppermute | solution.py:647
  40.0 0.0 copy-start.12
  40.0 0.0 copy-start.13
  40.1 1.4 %initial.1.rest_17_ = f32[4,128,1024]{2,1,0:T(8,128)S(1)} custom-call(s32[16]{0:T(128)S(1)} %pad_add_fusion.1.seg, f32[4,1024,128]{2,1,0:T(8,128)S(1)} %bitcast.32, f32[1056,128]{1,0:T(8,128)S(1)} %collective-permute-done.lft, f32[1056,128]{1,0:T(8,128)S(1)} %collective-permute-done.1.rgt), custom_call_target="tpu_custom_call" | custom-call | flops 2000000000 | bytes 4194304 | tf_op jit(solution)/shard_map/initial/pallas_call | solution.py:539
  41.5 0.0 copy-start.5
  41.5 1.3 %copy-done.5 = f32[4,128,1024]{2,1,0:T(8,128)} copy-done((f32[4,128,1024]{2,1,0:T(8,128)}, f32[4,128,1024]{2,1,0:T(8,128)S(1)}, u32[]{:S(2)}) %copy-start.5) | copy-done | bytes 2097176
  42.8 0.0 collective-permute-done.2.rest_3_
  42.8 0.0 collective-permute-done.3.rest_5_
  42.8 0.0 collective-permute-start.4
  42.8 2.0 %collective-permute-start.8 = (bf16[656,256]{1,0:T(8,128)(2,1)}, bf16[656,256]{1,0:T(8,128)(2,1)S(1)}, u32[]{:S(2)}, u32[]{:S(2)}) collective-permute-start(bf16[656,256]{1,0:T(8,128)(2,1)} %get-tuple-element.63), channel_id=1, source_target_pairs={{0,7},{1,0},{2,1},{3,2},{4,3},{5,4},{6,5},{7,6},{8,15},{9,8},{10,9... | collective-permute-start | bytes 1007624 | tf_op jit(solution)/shard_map/ppermute | solution.py:647
  44.8 0.6 iota_compare_fusion.4
  45.5 5.8 %collective-permute-done.6.rest_4_ = bf16[656,256]{1,0:T(8,128)(2,1)} collective-permute-done((bf16[656,256]{1,0:T(8,128)(2,1)}, bf16[656,256]{1,0:T(8,128)(2,1)}, u32[]{:S(2)}, u32[]{:S(2)}) %collective-permute-start.6) | collective-permute-done | bytes 335904 | tf_op jit(solution)/shard_map/ppermute | solution.py:647
  51.3 0.1 copy.37.rest_10_
  51.4 0.1 copy.38.rest_11_
  51.5 11.6 %all-to-all-start = ((bf16[8,128,1024]{2,1,0:T(8,128)(2,1)}), bf16[8,128,1024]{2,1,0:T(8,128)(2,1)S(1)}, u32[]{:S(2)}, u32[]{:S(2)}) async-start(bf16[8,128,1024]{2,1,0:T(8,128)(2,1)} %bitcast.34), calls=%async_computation | async-start | bytes 4194304 | tf_op jit(solution)/shard_map/all_to_all | solution.py:754
  63.1 0.0 collective-permute-done.5.rest_2_
  63.1 0.0 collective-permute-done.7.rest_6_
  63.1 5.6 %collective-permute-done.4.rest_1_ = bf16[656,256]{1,0:T(8,128)(2,1)S(1)} collective-permute-done((bf16[656,256]{1,0:T(8,128)(2,1)}, bf16[656,256]{1,0:T(8,128)(2,1)S(1)}, u32[]{:S(2)}, u32[]{:S(2)}) %collective-permute-start.4) | collective-permute-done | bytes 335904 | tf_op jit(solution)/shard_map/ppermute | solution.py:647
  68.8 0.3 collective-permute-done.8.rest_7_
  69.1 5.6 %prep.1 = (bf16[4,128,256]{2,1,0:T(8,128)(2,1)S(1)}, bf16[1024,128]{1,0:T(8,128)(2,1)S(1)}, f32[4,256,256]{2,1,0:T(8,128)S(1)}, f32[4,256,128]{2,1,0:T(8,128)S(1...) custom-call(s32[16]{0:T(128)S(1)} %pad_add_fusion.1.seg, s32[1]{0:T(128)} %bitcast.2.here, ...), custom_call_target="tpu_custom_call" | custom-call | flops 6000000000 | bytes 8388608 | tf_op jit(solution)/shard_map/prep/pallas_call | solution.py:553
  74.7 18.4 %scan.1 = (f32[1024,1024]{1,0:T(8,128)}, f32[4,1024,128]{2,1,0:T(8,128)}, bf16[1056,128]{1,0:T(8,128)(2,1)}, bf16[1056,128]{1,0:T(8,128)(2,1)S(1)}, f32[16,1024]{1,0:T(8,128)S(1)}) custom-call(s32[16]{0:T(128)S(1)} %pad_add_fusion.1.seg, s32[1]{0:T(128)} %bitcast.2.here, bf16[656,256]{1,0:T(8,128)(2,1)S(1)} %copy-done.2, ...), custom_call_target="tpu_custom_call" | custom-call | flops 20000000000 | bytes 16777216 | tf_op jit(solution)/shard_map/scan/pallas_call | solution.py:583
  93.1 0.0 copy-start.1
  93.1 0.3 collective-permute-start.9
  93.5 0.3 collective-permute-start.10
  93.8 0.2 select_reduce_fusion.1
  94.0 3.7 %collective-permute-done.9 = bf16[1056,128]{1,0:T(8,128)(2,1)S(1)} collective-permute-done((bf16[1056,128]{1,0:T(8,128)(2,1)}, bf16[1056,128]{1,0:T(8,128)(2,1)S(1)}, u32[]{:S(2)}, u32[]{:S(2)}) %collective-permute-start.9) | collective-permute-done | bytes 270368 | tf_op jit(solution)/shard_map/ppermute | solution.py:641
  97.7 1.7 %collective-permute-done.10 = bf16[1056,128]{1,0:T(8,128)(2,1)S(1)} collective-permute-done((bf16[1056,128]{1,0:T(8,128)(2,1)S(1)}, bf16[1056,128]{1,0:T(8,128)(2,1)S(1)}, u32[]{:S(2)}, u32[]{:S(2)}) %collective-permute-start.10) | collective-permute-done | bytes 270368 | tf_op jit(solution)/shard_map/ppermute | solution.py:641
  99.5 0.1 select_select_fusion
  99.6 0.8 convert_dynamic-update-slice_fusion.1
  100.4 0.8 convert_dynamic-update-slice_fusion
  101.2 0.6 copy.41
  101.8 0.7 copy.40
  102.5 14.6 %all-to-all-done = bf16[8,128,1024]{2,1,0:T(8,128)(2,1)S(1)} async-done(((bf16[8,128,1024]{2,1,0:T(8,128)(2,1)}), bf16[8,128,1024]{2,1,0:T(8,128)(2,1)S(1)}, u32[]{:S(2)}, u32[]{:S(2)}) %all-to-all-start) | async-done | bytes 2097184 | tf_op jit(solution)/shard_map/all_to_all | solution.py:754
  117.1 3.8 %gate.1 = bf16[1024,1024]{1,0:T(8,128)(2,1)} custom-call(f32[1024,1024]{1,0:T(8,128)} %get-tuple-element.80.y_in, bf16[1024,1024]{1,0:T(8,128)(2,1)S(1)} %bitcast.30, f32[1,1024]{1,0:T(1,128)S(1)} %bitcast.33), custom_call_target="tpu_custom_call" | custom-call | flops 20000000 | bytes 8388608 | tf_op jit(solution)/shard_map/gate/pallas_call | solution.py:619
  (49 shorter events, 0.4 us)
Async XLA Ops:
  0.6 13.9 %copy-start.10 = (s32[128]{0:T(128)S(1)}, s32[128]{0:T(128)}, u32[]{:S(2)}) copy-start(s32[128]{0:T(128)} %param.30) | copy-start | bytes 1540
  0.6 17.1 %copy-start.7 = (f32[4,3,1024]{2,0,1:T(4,128)S(1)}, f32[4,3,1024]{2,0,1:T(4,128)}, u32[]{:S(2)}) copy-start(f32[4,3,1024]{2,0,1:T(4,128)} %param.27) | copy-start | bytes 147460
  0.7 18.4 %copy-start.8 = (f32[4,3,256]{2,0,1:T(4,128)S(1)}, f32[4,3,256]{2,0,1:T(4,128)}, u32[]{:S(2)}) copy-start(f32[4,3,256]{2,0,1:T(4,128)} %param.28) | copy-start | bytes 36868
  3.1 39.7 %collective-permute-start.2 = (bf16[656,256]{1,0:T(8,128)(2,1)}, bf16[656,256]{1,0:T(8,128)(2,1)}, u32[]{:S(2)}, u32[]{:S(2)}) collective-permute-start(bf16[656,256]{1,0:T(8,128)(2,1)} %get-tuple-element.55), channel_id=1, source_target_pairs={{0,3},{1,4},{2,5},{3,6},{4,7},{5,0},{6,1},{7,2},{8,11},{9,12},{10,... | collective-permute-start | bytes 1007624 | tf_op jit(solution)/shard_map/ppermute | solution.py:647
  9.0 33.8 %collective-permute-start.3 = (bf16[656,256]{1,0:T(8,128)(2,1)}, bf16[656,256]{1,0:T(8,128)(2,1)}, u32[]{:S(2)}, u32[]{:S(2)}) collective-permute-start(bf16[656,256]{1,0:T(8,128)(2,1)} %get-tuple-element.56), channel_id=1, source_target_pairs={{0,5},{1,6},{2,7},{3,0},{4,1},{5,2},{6,3},{7,4},{8,13},{9,14},{10,... | collective-permute-start | bytes 1007624 | tf_op jit(solution)/shard_map/ppermute | solution.py:647
  9.1 42.2 %collective-permute-start.6 = (bf16[656,256]{1,0:T(8,128)(2,1)}, bf16[656,256]{1,0:T(8,128)(2,1)}, u32[]{:S(2)}, u32[]{:S(2)}) collective-permute-start(bf16[656,256]{1,0:T(8,128)(2,1)} %get-tuple-element.45), channel_id=1, source_target_pairs={{0,4},{1,5},{2,6},{3,7},{4,0},{5,1},{6,2},{7,3},{8,12},{9,13},{10,... | collective-permute-start | bytes 1007624 | tf_op jit(solution)/shard_map/ppermute | solution.py:647
  19.2 8.9 %copy-start.11 = (f32[16]{0:T(128)S(1)}, f32[16]{0:T(128)}, u32[]{:S(2)}) copy-start(f32[16]{0:T(128)} %param.24) | copy-start | bytes 196
  26.3 9.1 %collective-permute-start = (f32[1056,128]{1,0:T(8,128)}, f32[1056,128]{1,0:T(8,128)S(1)}, u32[]{:S(2)}, u32[]{:S(2)}) collective-permute-start(f32[1056,128]{1,0:T(8,128)} %get-tuple-element.49), channel_id=1, source_target_pairs={{0,8},{8,16},{16,24},{24,32},{32,40},{40,48},{48,56},{56,64},{64,7... | collective-permute-start | bytes 1622024 | tf_op jit(solution)/shard_map/ppermute | solution.py:641
  26.4 9.0 %collective-permute-start.1 = (f32[1056,128]{1,0:T(8,128)}, f32[1056,128]{1,0:T(8,128)S(1)}, u32[]{:S(2)}, u32[]{:S(2)}) collective-permute-start(f32[1056,128]{1,0:T(8,128)} %get-tuple-element.50), channel_id=1, source_target_pairs={{0,248},{8,0},{16,8},{24,16},{32,24},{40,32},{48,40},{56,48},{64,5... | collective-permute-start | bytes 1622024 | tf_op jit(solution)/shard_map/ppermute | solution.py:641
  28.3 3.3 %copy-start.9 = (s32[128]{0:T(128)S(1)}, s32[128]{0:T(128)}, u32[]{:S(2)}) copy-start(s32[128]{0:T(128)} %param.31) | copy-start | bytes 1540
  28.3 3.5 %copy-start.14 = (s32[128]{0:T(128)S(1)}, s32[128]{0:T(128)}, u32[]{:S(2)}) copy-start(s32[128]{0:T(128)} %param.29) | copy-start | bytes 1540
  28.3 11.7 %copy-start = (f32[4,16,64,128]{3,2,1,0:T(8,128)S(1)}, f32[4,16,64,128]{3,2,1,0:T(8,128)}, u32[]{:S(2)}) copy-start(f32[4,16,64,128]{3,2,1,0:T(8,128)} %param.26) | copy-start | bytes 6291460
  35.8 27.3 %collective-permute-start.5 = (bf16[656,256]{1,0:T(8,128)(2,1)}, bf16[656,256]{1,0:T(8,128)(2,1)}, u32[]{:S(2)}, u32[]{:S(2)}) collective-permute-start(bf16[656,256]{1,0:T(8,128)(2,1)} %get-tuple-element.59), channel_id=1, source_target_pairs={{0,2},{1,3},{2,4},{3,5},{4,6},{5,7},{6,0},{7,1},{8,10},{9,11},{10,... | collective-permute-start | bytes 1007624 | tf_op jit(solution)/shard_map/ppermute | solution.py:647
  36.1 27.0 %collective-permute-start.7 = (bf16[656,256]{1,0:T(8,128)(2,1)}, bf16[656,256]{1,0:T(8,128)(2,1)}, u32[]{:S(2)}, u32[]{:S(2)}) collective-permute-start(bf16[656,256]{1,0:T(8,128)(2,1)} %get-tuple-element.61), channel_id=1, source_target_pairs={{0,6},{1,7},{2,0},{3,1},{4,2},{5,3},{6,4},{7,5},{8,14},{9,15},{10,... | collective-permute-start | bytes 1007624 | tf_op jit(solution)/shard_map/ppermute | solution.py:647
  40.0 11.3 %copy-start.12 = (f32[16]{0:T(128)S(1)}, f32[16]{0:T(128)}, u32[]{:S(2)}) copy-start(f32[16]{0:T(128)} %param.22) | copy-start | bytes 196
  40.0 11.4 %copy-start.13 = (f32[16]{0:T(128)S(1)}, f32[16]{0:T(128)}, u32[]{:S(2)}) copy-start(f32[16]{0:T(128)} %param.23) | copy-start | bytes 196
  41.5 1.3 %copy-start.5 = (f32[4,128,1024]{2,1,0:T(8,128)}, f32[4,128,1024]{2,1,0:T(8,128)S(1)}, u32[]{:S(2)}) copy-start(f32[4,128,1024]{2,1,0:T(8,128)S(1)} %initial.1.rest_17_) | copy-start | bytes 6291460
  42.8 26.0 %collective-permute-start.4 = (bf16[656,256]{1,0:T(8,128)(2,1)}, bf16[656,256]{1,0:T(8,128)(2,1)S(1)}, u32[]{:S(2)}, u32[]{:S(2)}) collective-permute-start(bf16[656,256]{1,0:T(8,128)(2,1)} %get-tuple-element.57), channel_id=1, source_target_pairs={{0,1},{1,2},{2,3},{3,4},{4,5},{5,6},{6,7},{7,0},{8,9},{9,10},{10,1... | collective-permute-start | bytes 1007624 | tf_op jit(solution)/shard_map/ppermute | solution.py:647
  42.8 26.2 %collective-permute-start.8 = (bf16[656,256]{1,0:T(8,128)(2,1)}, bf16[656,256]{1,0:T(8,128)(2,1)S(1)}, u32[]{:S(2)}, u32[]{:S(2)}) collective-permute-start(bf16[656,256]{1,0:T(8,128)(2,1)} %get-tuple-element.63), channel_id=1, source_target_pairs={{0,7},{1,0},{2,1},{3,2},{4,3},{5,4},{6,5},{7,6},{8,15},{9,8},{10,9... | collective-permute-start | bytes 1007624 | tf_op jit(solution)/shard_map/ppermute | solution.py:647
  51.5 17.5 %copy-start.2 = (bf16[656,256]{1,0:T(8,128)(2,1)S(1)}, bf16[656,256]{1,0:T(8,128)(2,1)}, u32[]{:S(2)}) copy-start(bf16[656,256]{1,0:T(8,128)(2,1)} %get-tuple-element.47.rest_0_) | copy-start | bytes 1007620
  51.5 17.5 %copy-start.4 = (f32[5,256]{1,0:T(8,128)S(1)}, f32[5,256]{1,0:T(8,128)}, u32[]{:S(2)}) copy-start(f32[5,256]{1,0:T(8,128)} %rest_9_.2) | copy-start | bytes 15364
  51.5 65.6 %all-to-all-start = ((bf16[8,128,1024]{2,1,0:T(8,128)(2,1)}), bf16[8,128,1024]{2,1,0:T(8,128)(2,1)S(1)}, u32[]{:S(2)}, u32[]{:S(2)}) async-start(bf16[8,128,1024]{2,1,0:T(8,128)(2,1)} %bitcast.34), calls=%async_computation | async-start | bytes 4194304 | tf_op jit(solution)/shard_map/all_to_all | solution.py:754
  63.1 11.6 %copy-start.3 = (f32[5,1024]{1,0:T(8,128)S(1)}, f32[5,1024]{1,0:T(8,128)}, u32[]{:S(2)}) copy-start(f32[5,1024]{1,0:T(8,128)} %rest_9_.3) | copy-start | bytes 61444
  63.1 11.6 %copy-start.6 = (f32[4,128,1024]{2,1,0:T(8,128)S(1)}, f32[4,128,1024]{2,1,0:T(8,128)}, u32[]{:S(2)}) copy-start(f32[4,128,1024]{2,1,0:T(8,128)} %copy-done.5) | copy-start | bytes 6291460
  93.1 24.1 %copy-start.1 = (f32[1024]{0:T(1024)S(1)}, f32[1024]{0:T(1024)}, u32[]{:S(2)}) copy-start(f32[1024]{0:T(1024)} %param.25) | copy-start | bytes 12292
  93.1 4.6 %collective-permute-start.9 = (bf16[1056,128]{1,0:T(8,128)(2,1)}, bf16[1056,128]{1,0:T(8,128)(2,1)S(1)}, u32[]{:S(2)}, u32[]{:S(2)}) collective-permute-start(bf16[1056,128]{1,0:T(8,128)(2,1)} %get-tuple-element.77), channel_id=1, source_target_pairs={{0,248},{8,0},{16,8},{24,16},{32,24},{40,32},{48,40},{56,48},{64,5... | collective-permute-start | bytes 811016 | tf_op jit(solution)/shard_map/ppermute | solution.py:641
  93.5 6.0 %collective-permute-start.10 = (bf16[1056,128]{1,0:T(8,128)(2,1)S(1)}, bf16[1056,128]{1,0:T(8,128)(2,1)S(1)}, u32[]{:S(2)}, u32[]{:S(2)}) collective-permute-start(bf16[1056,128]{1,0:T(8,128)(2,1)S(1)} %get-tuple-element.78), channel_id=1, source_target_pairs={{0,8},{8,16},{16,24},{24,32},{32,40},{40,48},{48,56},{56,64},{64,7... | collective-permute-start | bytes 811016 | tf_op jit(solution)/shard_map/ppermute | solution.py:641

commit v2 on v1

--- a/solution.py
+++ b/solution.py
@@ -22,10 +22,11 @@
 SRC_ROWS = ROWS // TENSOR
 EPSILON = 1e-05
 LOG2E = math.log2(math.e)
-LANES = 2 * STATE
+LANES = 128
 TILES = GC // LANES
+BC_TILES = 2 * STATE // LANES
 BC_ROW = TILES * SRC_ROWS
-DT_ROW = BC_ROW + SRC_ROWS
+DT_ROW = BC_ROW + BC_TILES * SRC_ROWS
 BLOCK_ROWS = DT_ROW + GH
 MOVER_ROWS = GC + 32
 GATE_ROWS = 128
@@ -139,13 +140,15 @@
         for i in range(TILES):
             lanes = pl.ds(pl.multiple_of(to * GC + LANES * i, LANES), LANES)
             sources.append(x.at[:, lanes])
-        sources.append(bc.at[:, pl.ds(pl.multiple_of(to * LANES, LANES), LANES)])
+        for i in range(BC_TILES):
+            lanes = pl.ds(pl.multiple_of(to * 2 * STATE + LANES * i, LANES), LANES)
+            sources.append(bc.at[:, lanes])
         loads.append(
             [
                 pltpu.make_async_copy(
                     source,
                     stage.at[n, SRC_ROWS * i : SRC_ROWS * (i + 1), :],
-                    sems.at[n * (TILES + 1) + i],
+                    sems.at[n * (TILES + BC_TILES) + i],
                 )
                 for i, source in enumerate(sources)
             ]
@@ -158,8 +161,7 @@
     for n, d in enumerate(offsets):
         to = (here[0] + d) % TENSOR
         heads = pl.ds(pl.multiple_of(to * GH, GH), GH)
-        stage[n, DT_ROW:BLOCK_ROWS, 0:SRC_ROWS] = dt_turned[heads, :]
-        stage[n, DT_ROW:BLOCK_ROWS, SRC_ROWS:] = jnp.zeros((GH, LANES - SRC_ROWS), BF16)
+        stage[n, DT_ROW:BLOCK_ROWS, :] = dt_turned[heads, :]
         for copy in loads[n]:
             copy.wait()
         stores.append(pltpu.make_async_copy(stage.at[n], outs[n], out_sems.at[n]))
@@ -234,7 +236,9 @@
     for d in range(TENSOR):
         source = source_of(here, d)
         rows = pl.ds(pl.multiple_of(source * SRC_ROWS, SRC_ROWS), SRC_ROWS)
-        copies.append((blocks[d].at[BC_ROW:DT_ROW, :], bc_rows.at[rows, :]))
+        for i in range(BC_TILES):
+            part = blocks[d].at[BC_ROW + SRC_ROWS * i : BC_ROW + SRC_ROWS * (i + 1), :]
+            copies.append((part, bc_rows.at[rows, LANES * i : LANES * (i + 1)]))
         copies.append((blocks[d].at[DT_ROW:BLOCK_ROWS, :], dt_rows.at[source]))
     copy_all(copies, sems)
     every = slice(0, 2 * STATE)
@@ -425,7 +429,7 @@
         for b in range(GC // 128):
             part = slice(128 * b, 128 * (b + 1))
             out[part, :] = state[k, :, part].T.astype(BF16)
-        lines = (GC + LANES) // 128
+        lines = (GC + 2 * STATE) // 128
         tail[...] = jnp.zeros_like(tail)
         for j in range(3):
             row = pl.ds(3 * k + j, 1)
@@ -513,7 +517,7 @@
             pltpu.VMEM((count, BLOCK_ROWS, LANES), BF16),
             pltpu.VMEM((SRC_ROWS, HEADS), BF16),
             pltpu.VMEM((HEADS, SRC_ROWS), BF16),
-            pltpu.SemaphoreType.DMA((count * (TILES + 1),)),
+            pltpu.SemaphoreType.DMA((count * (TILES + BC_TILES),)),
             pltpu.SemaphoreType.DMA((count,)),
             pltpu.SemaphoreType.DMA,
         ],
@@ -568,7 +572,7 @@
             pltpu.VMEM((TENSOR, GH, LANES), BF16),
             pltpu.VMEM((ROWS, STATE), BF16),
             pltpu.VMEM((128, 2 * STATE), BF16),
-            pltpu.SemaphoreType.DMA((2 * TENSOR,)),
+            pltpu.SemaphoreType.DMA(((BC_TILES + 1) * TENSOR,)),
         ],
         compiler_params=params(8),
         cost_estimate=pl.CostEstimate(
@@ -697,10 +701,11 @@
     right = (me + 1) % dp_count
     here = lax.axis_index("tensor")
     here_ref = here.astype(jnp.int32)[None]
-    packed = pack(FIRST, here_ref, x_in, bc_in, dt_in)
-    packed |= pack(
-        SECOND + THIRD + (0,), after(here_ref, packed[FIRST[0]]), x_in, bc_in, dt_in
-    )
+    packed = {}
+    turn = here_ref
+    for offsets in (FIRST[:1], FIRST[1:], SECOND + THIRD + (0,)):
+        packed |= pack(offsets, turn, x_in, bc_in, dt_in)
+        turn = after(here_ref, packed[offsets[0]])
     blocks = {0: packed[0]}
     for d in FIRST:
         blocks[d] = rotated(packed[d], d)

time: 122 us -> 117 us (0.959)
  starting transfers between devices: 31.7 us -> 27.1 us
  waiting for transfers between devices: 34.4 us -> 31 us
  Pallas kernels: 37.2 us -> 39.3 us
    all_to_all x1, waiting for transfers between devices: 14.6 us -> 9.22 us  [shards(): lax.all_to_all(z_sent, 'tensor', split_axis=0, concat_axis=0, tiled=True)]
    all_to_all x1, starting transfers between devices: 11.6 us -> 6.95 us  [shards(): lax.all_to_all(z_sent, 'tensor', split_axis=0, concat_axis=0, tiled=True)]
    ppermute x7, waiting for transfers between devices: 11.7 us -> 13.9 us  [rotated(): return lax.ppermute(value, 'tensor', pairs)]
    pallas_call x2 -> x3, Pallas kernels: 5.37 us -> 7.35 us  [pack(): pl.pallas_call(functools.partial(pack_kernel, offsets), out_shape=(pltpu....]
  transfers between devices with their start and end apart: 12 -> 12, of which waited for: 7 -> 9; matrix products, arithmetic and copies ran while one was open for 9% -> 10% of each run, Pallas kernels for 26% -> 29%
where the time goes in v2:
time: 117 us; the launch traced here: 115 us
  Pallas kernels  39.3 us (34%)
  waiting for transfers between devices  31 us (26%)
  starting transfers between devices  27.1 us (23%)
  local copies, waits for them, and re-layouts  6.67 us (6%)
  other arithmetic  5.92 us (5%)
  between operations  5.11 us (4%)
    pallas_call x1, Pallas kernels, scan(): pl.pallas_call(main_kernel, out_shape=(pltpu.HBM((ROWS, GC), F32), jax.Sh...  18.7 us
    ppermute x7, starting transfers between devices, rotated(): return lax.ppermute(value, 'tensor', pairs)  17.7 us
    ppermute x7, waiting for transfers between devices, rotated(): return lax.ppermute(value, 'tensor', pairs)  13.9 us
    all_to_all x1, waiting for transfers between devices, shards(): lax.all_to_all(z_sent, 'tensor', split_axis=0, concat_axis=0, tiled=True)  9.22 us
    ppermute x4, waiting for transfers between devices, shifted(): return lax.ppermute(value, 'dp', pairs)  7.83 us
    pallas_call x3, Pallas kernels, pack(): pl.pallas_call(functools.partial(pack_kernel, offsets), out_shape=(pltpu....  7.35 us
    all_to_all x1, starting transfers between devices, shards(): lax.all_to_all(z_sent, 'tensor', split_axis=0, concat_axis=0, tiled=True)  6.95 us
    pallas_call x1, Pallas kernels, prep(): pl.pallas_call(prep_kernel, out_shape=(jax.ShapeDtypeStruct((CHUNKS, STAT...  5.4 us
  transfers between devices with their start and end apart: 12, of which 9 were waited for; matrix products, arithmetic and copies ran while one was open for 10% of the time, Pallas kernels for 29%

profile of v2, /device:TPU:36, one launch (start us, length us, event | category | flops | bytes accessed | tf_op | source)
XLA Modules:
  0.0 115.1 jit_solution(3318275792166528758)
XLA Ops:
  0.6 1.9 %pack.3 = bf16[1296,128]{1,0:T(8,128)(2,1)} custom-call(s32[1]{0:T(128)} %bitcast.2.here, bf16[128,8192]{1,0:T(8,128)(2,1)} %x.11, bf16[128,2048]{1,0:T(8,128)(2,1)} %bc.5, bf16[128,128]{1,0:T(8,128)(2,1)} %dt.5), custom_call_target="tpu_custom_call" | custom-call | tf_op jit(solution)/shard_map/pack/pallas_call | solution.py:511
  2.5 0.0 copy-start.10
  2.5 0.0 copy-start.7
  2.5 0.0 copy-start.8
  2.6 6.4 %collective-permute-start.6 = (bf16[1296,128]{1,0:T(8,128)(2,1)}, bf16[1296,128]{1,0:T(8,128)(2,1)}, u32[]{:S(2)}, u32[]{:S(2)}) collective-permute-start(bf16[1296,128]{1,0:T(8,128)(2,1)} %pack.3), channel_id=1, source_target_pairs={{0,4},{1,5},{2,6},{3,7},{4,0},{5,1},{6,2},{7,3},{8,12},{9,13},{10,... | collective-permute-start | bytes 995336 | tf_op jit(solution)/shard_map/ppermute | solution.py:651
  8.9 2.2 %pack.4 = (bf16[1296,128]{1,0:T(8,128)(2,1)}, bf16[1296,128]{1,0:T(8,128)(2,1)}) custom-call(s32[1]{0:T(128)} %bitcast.2.here, bf16[128,8192]{1,0:T(8,128)(2,1)} %x.11, bf16[128,2048]{1,0:T(8,128)(2,1)} %bc.5, bf16[128,128]{1,0:T(8,128)(2,1)} %dt.5), custom_call_target="tpu_custom_call" | custom-call | tf_op jit(solution)/shard_map/pack/pallas_call | solution.py:511
  11.2 0.2 collective-permute-start.3
  11.3 4.9 %collective-permute-start.2 = (bf16[1296,128]{1,0:T(8,128)(2,1)}, bf16[1296,128]{1,0:T(8,128)(2,1)}, u32[]{:S(2)}, u32[]{:S(2)}) collective-permute-start(bf16[1296,128]{1,0:T(8,128)(2,1)} %get-tuple-element.46), channel_id=1, source_target_pairs={{0,3},{1,4},{2,5},{3,6},{4,7},{5,0},{6,1},{7,2},{8,11},{9,12},{10,... | collective-permute-start | bytes 995336 | tf_op jit(solution)/shard_map/ppermute | solution.py:651
  16.3 0.6 fusion.2
  19.5 0.0 copy-done.7
  20.9 0.1 dynamic-slice_reduce_fusion.1
  21.0 0.0 copy-start.11
  21.0 3.2 %pack.5 = (bf16[1296,128]{1,0:T(8,128)(2,1)}, bf16[1296,128]{1,0:T(8,128)(2,1)}, bf16[1296,128]{1,0:T(8,128)(2,1)}, bf16[1296,128]{1,0:T(8,128)(2,1)}, bf16[1296,128]{1,0:T(8,128)(2,1)}) custom-call(s32[1]{0:T(128)} %bitcast.2.here, bf16[128,8192]{1,0:T(8,128)(2,1)} %x.11, bf16[128,2048]{1,0:T(8,128)(2,1)} %bc.5, bf16[128,128]{1,0:T(8,128)(2,1)} %dt.5), custom_call_target="tpu_custom_call" | custom-call | tf_op jit(solution)/shard_map/pack/pallas_call | solution.py:511
  24.3 1.4 %pad_add_fusion.slots = s32[2]{0:T(128)S(1)} fusion(s32[1]{0:T(128)} %bitcast.1, s32[1]{0:T(128)} %bitcast), kind=kLoop, calls=%fused_computation.36 | loop fusion | flops 2 | bytes 16 | tf_op jit(solution)/shard_map/stack | solution.py:725
  25.7 2.7 %movers.1 = (f32[1056,128]{1,0:T(8,128)}, f32[1056,128]{1,0:T(8,128)}) custom-call(s32[2]{0:T(128)S(1)} %pad_add_fusion.slots, f32[4,1024,128]{2,1,0:T(8,128)} %bitcast.31, f32[2,32,128]{2,1,0:T(8,128)S(1)} %pad_maximum_fusion.2.small), custom_call_target="tpu_custom_call" | custom-call | tf_op jit(solution)/shard_map/movers/pallas_call | solution.py:531
  28.4 0.1 collective-permute-start
  28.5 1.7 %collective-permute-start.1 = (f32[1056,128]{1,0:T(8,128)}, f32[1056,128]{1,0:T(8,128)S(1)}, u32[]{:S(2)}, u32[]{:S(2)}) collective-permute-start(f32[1056,128]{1,0:T(8,128)} %get-tuple-element.51), channel_id=1, source_target_pairs={{0,248},{8,0},{16,8},{24,16},{32,24},{40,32},{48,40},{56,48},{64,5... | collective-permute-start | bytes 1622024 | tf_op jit(solution)/shard_map/ppermute | solution.py:645
  30.2 0.0 copy-done.11
  30.2 0.1 broadcast_in_dim.158
  30.3 0.1 broadcast_in_dim_reshape.4.rest_10_
  30.4 3.3 %copy.44 = bf16[16,8,8,1024]{3,2,0,1:T(8,128)(2,1)} copy(bf16[16,8,8,1024]{3,2,1,0:T(8,128)(2,1)} %bitcast.35) | data formatting | bytes 4194304 | tf_op jit(solution)/shard_map/reshape | solution.py:742
  33.7 0.2 convert_reduce_fusion
  33.9 0.1 select_reduce_fusion.2
  34.0 0.7 iota_compare_fusion.3
  34.7 0.1 pad_add_fusion.1.seg
  34.8 2.7 %collective-permute-done.lft = f32[1056,128]{1,0:T(8,128)S(1)} collective-permute-done((f32[1056,128]{1,0:T(8,128)}, f32[1056,128]{1,0:T(8,128)S(1)}, u32[]{:S(2)}, u32[]{:S(2)}) %collective-permute-start) | collective-permute-done | bytes 540704 | tf_op jit(solution)/shard_map/ppermute | solution.py:645
  37.5 0.0 collective-permute-done.1.rgt
  37.6 0.1 copy.34
  37.7 0.2 select_reduce_fusion
  37.9 1.5 %collective-permute-start.5 = (bf16[1296,128]{1,0:T(8,128)(2,1)}, bf16[1296,128]{1,0:T(8,128)(2,1)}, u32[]{:S(2)}, u32[]{:S(2)}) collective-permute-start(bf16[1296,128]{1,0:T(8,128)(2,1)} %get-tuple-element.59), channel_id=1, source_target_pairs={{0,2},{1,3},{2,4},{3,5},{4,6},{5,7},{6,0},{7,1},{8,10},{9,11},{10,... | collective-permute-start | bytes 995336 | tf_op jit(solution)/shard_map/ppermute | solution.py:651
  39.4 2.7 %collective-permute-start.7 = (bf16[1296,128]{1,0:T(8,128)(2,1)}, bf16[1296,128]{1,0:T(8,128)(2,1)}, u32[]{:S(2)}, u32[]{:S(2)}) collective-permute-start(bf16[1296,128]{1,0:T(8,128)(2,1)} %get-tuple-element.61), channel_id=1, source_target_pairs={{0,6},{1,7},{2,0},{3,1},{4,2},{5,3},{6,4},{7,5},{8,14},{9,15},{10,... | collective-permute-start | bytes 995336 | tf_op jit(solution)/shard_map/ppermute | solution.py:651
  42.1 0.0 copy-start.12
  42.1 0.0 copy-start.13
  42.1 1.4 %initial.1.rest_17_ = f32[4,128,1024]{2,1,0:T(8,128)S(1)} custom-call(s32[16]{0:T(128)S(1)} %pad_add_fusion.1.seg, f32[4,1024,128]{2,1,0:T(8,128)S(1)} %bitcast.32, f32[1056,128]{1,0:T(8,128)S(1)} %collective-permute-done.lft, f32[1056,128]{1,0:T(8,128)S(1)} %collective-permute-done.1.rgt), custom_call_target="tpu_custom_call" | custom-call | flops 2000000000 | bytes 4194304 | tf_op jit(solution)/shard_map/initial/pallas_call | solution.py:543
  43.6 0.0 copy-start.5
  43.6 1.3 %copy-done.5 = f32[4,128,1024]{2,1,0:T(8,128)} copy-done((f32[4,128,1024]{2,1,0:T(8,128)}, f32[4,128,1024]{2,1,0:T(8,128)S(1)}, u32[]{:S(2)}) %copy-start.5) | copy-done | bytes 2097176
  44.9 0.2 collective-permute-done.3.rest_5_
  45.1 2.0 %collective-permute-done.2.rest_3_ = bf16[1296,128]{1,0:T(8,128)(2,1)} collective-permute-done((bf16[1296,128]{1,0:T(8,128)(2,1)}, bf16[1296,128]{1,0:T(8,128)(2,1)}, u32[]{:S(2)}, u32[]{:S(2)}) %collective-permute-start.2) | collective-permute-done | bytes 331808 | tf_op jit(solution)/shard_map/ppermute | solution.py:651
  47.1 0.0 collective-permute-start.4
  47.1 2.0 %collective-permute-start.8 = (bf16[1296,128]{1,0:T(8,128)(2,1)}, bf16[1296,128]{1,0:T(8,128)(2,1)S(1)}, u32[]{:S(2)}, u32[]{:S(2)}) collective-permute-start(bf16[1296,128]{1,0:T(8,128)(2,1)} %get-tuple-element.63), channel_id=1, source_target_pairs={{0,7},{1,0},{2,1},{3,2},{4,3},{5,4},{6,5},{7,6},{8,15},{9,8},{10,9... | collective-permute-start | bytes 995336 | tf_op jit(solution)/shard_map/ppermute | solution.py:651
  49.1 0.6 iota_compare_fusion.4
  49.8 0.0 collective-permute-done.6.rest_4_
  49.8 0.1 copy.37.rest_10_
  49.9 0.1 copy.38.rest_11_
  50.0 6.9 %all-to-all-start = ((bf16[8,128,1024]{2,1,0:T(8,128)(2,1)}), bf16[8,128,1024]{2,1,0:T(8,128)(2,1)S(1)}, u32[]{:S(2)}, u32[]{:S(2)}) async-start(bf16[8,128,1024]{2,1,0:T(8,128)(2,1)} %bitcast.34), calls=%async_computation | async-start | bytes 4194304 | tf_op jit(solution)/shard_map/all_to_all | solution.py:759
  56.9 2.5 %collective-permute-done.5.rest_2_ = bf16[1296,128]{1,0:T(8,128)(2,1)} collective-permute-done((bf16[1296,128]{1,0:T(8,128)(2,1)}, bf16[1296,128]{1,0:T(8,128)(2,1)}, u32[]{:S(2)}, u32[]{:S(2)}) %collective-permute-start.5) | collective-permute-done | bytes 331808 | tf_op jit(solution)/shard_map/ppermute | solution.py:651
  59.4 0.5 collective-permute-done.7.rest_6_
  60.0 8.7 %collective-permute-done.4.rest_1_ = bf16[1296,128]{1,0:T(8,128)(2,1)S(1)} collective-permute-done((bf16[1296,128]{1,0:T(8,128)(2,1)}, bf16[1296,128]{1,0:T(8,128)(2,1)S(1)}, u32[]{:S(2)}, u32[]{:S(2)}) %collective-permute-start.4) | collective-permute-done | bytes 331808 | tf_op jit(solution)/shard_map/ppermute | solution.py:651
  68.7 0.0 collective-permute-done.8.rest_7_
  68.7 5.4 %prep.1 = (bf16[4,128,256]{2,1,0:T(8,128)(2,1)S(1)}, bf16[1024,128]{1,0:T(8,128)(2,1)S(1)}, f32[4,256,256]{2,1,0:T(8,128)S(1)}, f32[4,256,128]{2,1,0:T(8,128)S(1...) custom-call(s32[16]{0:T(128)S(1)} %pad_add_fusion.1.seg, s32[1]{0:T(128)} %bitcast.2.here, ...), custom_call_target="tpu_custom_call" | custom-call | flops 6000000000 | bytes 8388608 | tf_op jit(solution)/shard_map/prep/pallas_call | solution.py:557
  74.1 18.7 %scan.1 = (f32[1024,1024]{1,0:T(8,128)}, f32[4,1024,128]{2,1,0:T(8,128)}, bf16[1056,128]{1,0:T(8,128)(2,1)}, bf16[1056,128]{1,0:T(8,128)(2,1)S(1)}, f32[16,1024]{1,0:T(8,128)S(1)}) custom-call(s32[16]{0:T(128)S(1)} %pad_add_fusion.1.seg, s32[1]{0:T(128)} %bitcast.2.here, bf16[1296,128]{1,0:T(8,128)(2,1)S(1)} %copy-done.2, ...), custom_call_target="tpu_custom_call" | custom-call | flops 20000000000 | bytes 16777216 | tf_op jit(solution)/shard_map/scan/pallas_call | solution.py:587
  92.8 0.0 copy-start.1
  92.8 0.1 collective-permute-start.9
  92.9 0.6 collective-permute-start.10
  93.5 0.2 select_reduce_fusion.1
  93.7 3.4 %collective-permute-done.9 = bf16[1056,128]{1,0:T(8,128)(2,1)S(1)} collective-permute-done((bf16[1056,128]{1,0:T(8,128)(2,1)}, bf16[1056,128]{1,0:T(8,128)(2,1)S(1)}, u32[]{:S(2)}, u32[]{:S(2)}) %collective-permute-start.9) | collective-permute-done | bytes 270368 | tf_op jit(solution)/shard_map/ppermute | solution.py:645
  97.2 1.7 %collective-permute-done.10 = bf16[1056,128]{1,0:T(8,128)(2,1)S(1)} collective-permute-done((bf16[1056,128]{1,0:T(8,128)(2,1)S(1)}, bf16[1056,128]{1,0:T(8,128)(2,1)S(1)}, u32[]{:S(2)}, u32[]{:S(2)}) %collective-permute-start.10) | collective-permute-done | bytes 270368 | tf_op jit(solution)/shard_map/ppermute | solution.py:645
  98.9 0.1 select_select_fusion
  99.0 0.8 convert_dynamic-update-slice_fusion.1
  99.9 0.8 convert_dynamic-update-slice_fusion
  100.7 0.6 copy.41
  101.3 0.7 copy.40
  102.0 9.2 %all-to-all-done = bf16[8,128,1024]{2,1,0:T(8,128)(2,1)S(1)} async-done(((bf16[8,128,1024]{2,1,0:T(8,128)(2,1)}), bf16[8,128,1024]{2,1,0:T(8,128)(2,1)S(1)}, u32[]{:S(2)}, u32[]{:S(2)}) %all-to-all-start) | async-done | bytes 2097184 | tf_op jit(solution)/shard_map/all_to_all | solution.py:759
  111.2 3.8 %gate.1 = bf16[1024,1024]{1,0:T(8,128)(2,1)} custom-call(f32[1024,1024]{1,0:T(8,128)} %get-tuple-element.80.y_in, bf16[1024,1024]{1,0:T(8,128)(2,1)S(1)} %bitcast.30, f32[1,1024]{1,0:T(1,128)S(1)} %bitcast.33), custom_call_target="tpu_custom_call" | custom-call | flops 20000000 | bytes 8388608 | tf_op jit(solution)/shard_map/gate/pallas_call | solution.py:623
  (50 shorter events, 0.4 us)
Async XLA Ops:
  2.5 13.8 %copy-start.10 = (s32[128]{0:T(128)S(1)}, s32[128]{0:T(128)}, u32[]{:S(2)}) copy-start(s32[128]{0:T(128)} %param.30) | copy-start | bytes 1540
  2.5 17.0 %copy-start.7 = (f32[4,3,1024]{2,0,1:T(4,128)S(1)}, f32[4,3,1024]{2,0,1:T(4,128)}, u32[]{:S(2)}) copy-start(f32[4,3,1024]{2,0,1:T(4,128)} %param.27) | copy-start | bytes 147460
  2.5 18.3 %copy-start.8 = (f32[4,3,256]{2,0,1:T(4,128)S(1)}, f32[4,3,256]{2,0,1:T(4,128)}, u32[]{:S(2)}) copy-start(f32[4,3,256]{2,0,1:T(4,128)} %param.28) | copy-start | bytes 36868
  2.6 47.2 %collective-permute-start.6 = (bf16[1296,128]{1,0:T(8,128)(2,1)}, bf16[1296,128]{1,0:T(8,128)(2,1)}, u32[]{:S(2)}, u32[]{:S(2)}) collective-permute-start(bf16[1296,128]{1,0:T(8,128)(2,1)} %pack.3), channel_id=1, source_target_pairs={{0,4},{1,5},{2,6},{3,7},{4,0},{5,1},{6,2},{7,3},{8,12},{9,13},{10,... | collective-permute-start | bytes 995336 | tf_op jit(solution)/shard_map/ppermute | solution.py:651
  11.2 33.9 %collective-permute-start.3 = (bf16[1296,128]{1,0:T(8,128)(2,1)}, bf16[1296,128]{1,0:T(8,128)(2,1)}, u32[]{:S(2)}, u32[]{:S(2)}) collective-permute-start(bf16[1296,128]{1,0:T(8,128)(2,1)} %get-tuple-element.56), channel_id=1, source_target_pairs={{0,5},{1,6},{2,7},{3,0},{4,1},{5,2},{6,3},{7,4},{8,13},{9,14},{10,... | collective-permute-start | bytes 995336 | tf_op jit(solution)/shard_map/ppermute | solution.py:651
  11.3 35.7 %collective-permute-start.2 = (bf16[1296,128]{1,0:T(8,128)(2,1)}, bf16[1296,128]{1,0:T(8,128)(2,1)}, u32[]{:S(2)}, u32[]{:S(2)}) collective-permute-start(bf16[1296,128]{1,0:T(8,128)(2,1)} %get-tuple-element.46), channel_id=1, source_target_pairs={{0,3},{1,4},{2,5},{3,6},{4,7},{5,0},{6,1},{7,2},{8,11},{9,12},{10,... | collective-permute-start | bytes 995336 | tf_op jit(solution)/shard_map/ppermute | solution.py:651
  21.0 9.2 %copy-start.11 = (f32[16]{0:T(128)S(1)}, f32[16]{0:T(128)}, u32[]{:S(2)}) copy-start(f32[16]{0:T(128)} %param.24) | copy-start | bytes 196
  28.4 9.1 %collective-permute-start = (f32[1056,128]{1,0:T(8,128)}, f32[1056,128]{1,0:T(8,128)S(1)}, u32[]{:S(2)}, u32[]{:S(2)}) collective-permute-start(f32[1056,128]{1,0:T(8,128)} %get-tuple-element.50), channel_id=1, source_target_pairs={{0,8},{8,16},{16,24},{24,32},{32,40},{40,48},{48,56},{56,64},{64,7... | collective-permute-start | bytes 1622024 | tf_op jit(solution)/shard_map/ppermute | solution.py:645
  28.5 9.0 %collective-permute-start.1 = (f32[1056,128]{1,0:T(8,128)}, f32[1056,128]{1,0:T(8,128)S(1)}, u32[]{:S(2)}, u32[]{:S(2)}) collective-permute-start(f32[1056,128]{1,0:T(8,128)} %get-tuple-element.51), channel_id=1, source_target_pairs={{0,248},{8,0},{16,8},{24,16},{32,24},{40,32},{48,40},{56,48},{64,5... | collective-permute-start | bytes 1622024 | tf_op jit(solution)/shard_map/ppermute | solution.py:645
  30.4 3.3 %copy-start.9 = (s32[128]{0:T(128)S(1)}, s32[128]{0:T(128)}, u32[]{:S(2)}) copy-start(s32[128]{0:T(128)} %param.31) | copy-start | bytes 1540
  30.4 3.5 %copy-start.14 = (s32[128]{0:T(128)S(1)}, s32[128]{0:T(128)}, u32[]{:S(2)}) copy-start(s32[128]{0:T(128)} %param.29) | copy-start | bytes 1540
  30.4 11.7 %copy-start = (f32[4,16,64,128]{3,2,1,0:T(8,128)S(1)}, f32[4,16,64,128]{3,2,1,0:T(8,128)}, u32[]{:S(2)}) copy-start(f32[4,16,64,128]{3,2,1,0:T(8,128)} %param.26) | copy-start | bytes 6291460
  37.9 21.6 %collective-permute-start.5 = (bf16[1296,128]{1,0:T(8,128)(2,1)}, bf16[1296,128]{1,0:T(8,128)(2,1)}, u32[]{:S(2)}, u32[]{:S(2)}) collective-permute-start(bf16[1296,128]{1,0:T(8,128)(2,1)} %get-tuple-element.59), channel_id=1, source_target_pairs={{0,2},{1,3},{2,4},{3,5},{4,6},{5,7},{6,0},{7,1},{8,10},{9,11},{10,... | collective-permute-start | bytes 995336 | tf_op jit(solution)/shard_map/ppermute | solution.py:651
  39.4 20.5 %collective-permute-start.7 = (bf16[1296,128]{1,0:T(8,128)(2,1)}, bf16[1296,128]{1,0:T(8,128)(2,1)}, u32[]{:S(2)}, u32[]{:S(2)}) collective-permute-start(bf16[1296,128]{1,0:T(8,128)(2,1)} %get-tuple-element.61), channel_id=1, source_target_pairs={{0,6},{1,7},{2,0},{3,1},{4,2},{5,3},{6,4},{7,5},{8,14},{9,15},{10,... | collective-permute-start | bytes 995336 | tf_op jit(solution)/shard_map/ppermute | solution.py:651
  42.1 7.7 %copy-start.12 = (f32[16]{0:T(128)S(1)}, f32[16]{0:T(128)}, u32[]{:S(2)}) copy-start(f32[16]{0:T(128)} %param.22) | copy-start | bytes 196
  42.1 7.8 %copy-start.13 = (f32[16]{0:T(128)S(1)}, f32[16]{0:T(128)}, u32[]{:S(2)}) copy-start(f32[16]{0:T(128)} %param.23) | copy-start | bytes 196
  43.6 1.3 %copy-start.5 = (f32[4,128,1024]{2,1,0:T(8,128)}, f32[4,128,1024]{2,1,0:T(8,128)S(1)}, u32[]{:S(2)}) copy-start(f32[4,128,1024]{2,1,0:T(8,128)S(1)} %initial.1.rest_17_) | copy-start | bytes 6291460
  47.1 21.6 %collective-permute-start.4 = (bf16[1296,128]{1,0:T(8,128)(2,1)}, bf16[1296,128]{1,0:T(8,128)(2,1)S(1)}, u32[]{:S(2)}, u32[]{:S(2)}) collective-permute-start(bf16[1296,128]{1,0:T(8,128)(2,1)} %get-tuple-element.57), channel_id=1, source_target_pairs={{0,1},{1,2},{2,3},{3,4},{4,5},{5,6},{6,7},{7,0},{8,9},{9,10},{10,1... | collective-permute-start | bytes 995336 | tf_op jit(solution)/shard_map/ppermute | solution.py:651
  47.1 21.6 %collective-permute-start.8 = (bf16[1296,128]{1,0:T(8,128)(2,1)}, bf16[1296,128]{1,0:T(8,128)(2,1)S(1)}, u32[]{:S(2)}, u32[]{:S(2)}) collective-permute-start(bf16[1296,128]{1,0:T(8,128)(2,1)} %get-tuple-element.63), channel_id=1, source_target_pairs={{0,7},{1,0},{2,1},{3,2},{4,3},{5,4},{6,5},{7,6},{8,15},{9,8},{10,9... | collective-permute-start | bytes 995336 | tf_op jit(solution)/shard_map/ppermute | solution.py:651
  50.0 18.7 %copy-start.2 = (bf16[1296,128]{1,0:T(8,128)(2,1)S(1)}, bf16[1296,128]{1,0:T(8,128)(2,1)}, u32[]{:S(2)}) copy-start(bf16[1296,128]{1,0:T(8,128)(2,1)} %get-tuple-element.48.rest_0_) | copy-start | bytes 995332
  50.0 18.7 %copy-start.4 = (f32[5,256]{1,0:T(8,128)S(1)}, f32[5,256]{1,0:T(8,128)}, u32[]{:S(2)}) copy-start(f32[5,256]{1,0:T(8,128)} %rest_9_.2) | copy-start | bytes 15364
  50.0 61.2 %all-to-all-start = ((bf16[8,128,1024]{2,1,0:T(8,128)(2,1)}), bf16[8,128,1024]{2,1,0:T(8,128)(2,1)S(1)}, u32[]{:S(2)}, u32[]{:S(2)}) async-start(bf16[8,128,1024]{2,1,0:T(8,128)(2,1)} %bitcast.34), calls=%async_computation | async-start | bytes 4194304 | tf_op jit(solution)/shard_map/all_to_all | solution.py:759
  56.9 17.1 %copy-start.3 = (f32[5,1024]{1,0:T(8,128)S(1)}, f32[5,1024]{1,0:T(8,128)}, u32[]{:S(2)}) copy-start(f32[5,1024]{1,0:T(8,128)} %rest_9_.3) | copy-start | bytes 61444
  56.9 17.1 %copy-start.6 = (f32[4,128,1024]{2,1,0:T(8,128)S(1)}, f32[4,128,1024]{2,1,0:T(8,128)}, u32[]{:S(2)}) copy-start(f32[4,128,1024]{2,1,0:T(8,128)} %copy-done.5) | copy-start | bytes 6291460
  92.8 18.4 %copy-start.1 = (f32[1024]{0:T(1024)S(1)}, f32[1024]{0:T(1024)}, u32[]{:S(2)}) copy-start(f32[1024]{0:T(1024)} %param.25) | copy-start | bytes 12292
  92.8 4.4 %collective-permute-start.9 = (bf16[1056,128]{1,0:T(8,128)(2,1)}, bf16[1056,128]{1,0:T(8,128)(2,1)S(1)}, u32[]{:S(2)}, u32[]{:S(2)}) collective-permute-start(bf16[1056,128]{1,0:T(8,128)(2,1)} %get-tuple-element.77), channel_id=1, source_target_pairs={{0,248},{8,0},{16,8},{24,16},{32,24},{40,32},{48,40},{56,48},{64,5... | collective-permute-start | bytes 811016 | tf_op jit(solution)/shard_map/ppermute | solution.py:645
  92.9 6.0 %collective-permute-start.10 = (bf16[1056,128]{1,0:T(8,128)(2,1)S(1)}, bf16[1056,128]{1,0:T(8,128)(2,1)S(1)}, u32[]{:S(2)}, u32[]{:S(2)}) collective-permute-start(bf16[1056,128]{1,0:T(8,128)(2,1)S(1)} %get-tuple-element.78), channel_id=1, source_target_pairs={{0,8},{8,16},{16,24},{24,32},{32,40},{40,48},{48,56},{56,64},{64,7... | collective-permute-start | bytes 811016 | tf_op jit(solution)/shard_map/ppermute | solution.py:645

commit v3 on v2

--- a/solution.py
+++ b/solution.py
@@ -131,6 +131,8 @@
 def pack_kernel(offsets, here, x, bc, dt, *rest):
     count = len(offsets)
     outs, (stage, dt_all, dt_turned, sems, out_sems, dt_sem) = rest[:count], rest[count:]
+    direct = count == 1
+    parts = list(outs) if direct else [stage.at[n] for n in range(count)]
     dt_load = pltpu.make_async_copy(dt, dt_all, dt_sem)
     dt_load.start()
     loads = []
@@ -147,7 +149,7 @@
             [
                 pltpu.make_async_copy(
                     source,
-                    stage.at[n, SRC_ROWS * i : SRC_ROWS * (i + 1), :],
+                    parts[n].at[SRC_ROWS * i : SRC_ROWS * (i + 1), :],
                     sems.at[n * (TILES + BC_TILES) + i],
                 )
                 for i, source in enumerate(sources)
@@ -161,11 +163,12 @@
     for n, d in enumerate(offsets):
         to = (here[0] + d) % TENSOR
         heads = pl.ds(pl.multiple_of(to * GH, GH), GH)
-        stage[n, DT_ROW:BLOCK_ROWS, :] = dt_turned[heads, :]
+        parts[n][DT_ROW:BLOCK_ROWS, :] = dt_turned[heads, :]
         for copy in loads[n]:
             copy.wait()
-        stores.append(pltpu.make_async_copy(stage.at[n], outs[n], out_sems.at[n]))
-        stores[-1].start()
+        if not direct:
+            stores.append(pltpu.make_async_copy(parts[n], outs[n], out_sems.at[n]))
+            stores[-1].start()
     for copy in stores:
         copy.wait()
 
@@ -510,9 +513,14 @@
     count = len(offsets)
     blocks = pl.pallas_call(
         functools.partial(pack_kernel, offsets),
-        out_shape=(pltpu.HBM((BLOCK_ROWS, LANES), BF16),) * count,
+        out_shape=(
+            jax.ShapeDtypeStruct((BLOCK_ROWS, LANES), BF16)
+            if count == 1
+            else pltpu.HBM((BLOCK_ROWS, LANES), BF16),
+        )
+        * count,
         in_specs=[SMEM, HBM, HBM, HBM],
-        out_specs=(HBM,) * count,
+        out_specs=(VMEM if count == 1 else HBM,) * count,
         scratch_shapes=[
             pltpu.VMEM((count, BLOCK_ROWS, LANES), BF16),
             pltpu.VMEM((SRC_ROWS, HEADS), BF16),

time: 117 us -> 118 us (level)
  the two profiles are of different devices: /device:TPU:36 before, /device:TPU:1 now
where the time goes in v3:
time: 118 us; the launch traced here: 117 us
  Pallas kernels  39.8 us (34%)
  waiting for transfers between devices  30.5 us (26%)
  starting transfers between devices  28.2 us (24%)
  local copies, waits for them, and re-layouts  7.39 us (6%)
  other arithmetic  5.92 us (5%)
  between operations  5.1 us (4%)
    pallas_call x1, Pallas kernels, scan(): pl.pallas_call(main_kernel, out_shape=(pltpu.HBM((ROWS, GC), F32), jax.Sh...  19.3 us
    ppermute x7, starting transfers between devices, rotated(): return lax.ppermute(value, 'tensor', pairs)  17.5 us
    ppermute x7, waiting for transfers between devices, rotated(): return lax.ppermute(value, 'tensor', pairs)  13.1 us
    ppermute x4, waiting for transfers between devices, shifted(): return lax.ppermute(value, 'dp', pairs)  9.61 us
    all_to_all x1, waiting for transfers between devices, shards(): lax.all_to_all(z_sent, 'tensor', split_axis=0, concat_axis=0, tiled=True)  7.85 us
    pallas_call x3, Pallas kernels, pack(): pl.pallas_call(functools.partial(pack_kernel, offsets), out_shape=(jax.Sh...  6.58 us
    all_to_all x1, starting transfers between devices, shards(): lax.all_to_all(z_sent, 'tensor', split_axis=0, concat_axis=0, tiled=True)  6.08 us
    pallas_call x1, Pallas kernels, prep(): pl.pallas_call(prep_kernel, out_shape=(jax.ShapeDtypeStruct((CHUNKS, STAT...  5.41 us
  transfers between devices with their start and end apart: 12, of which 7 were waited for; matrix products, arithmetic and copies ran while one was open for 10% of the time, Pallas kernels for 30%

profile of v3, /device:TPU:1, one launch (start us, length us, event | category | flops | bytes accessed | tf_op | source)
XLA Modules:
  0.0 116.9 jit_solution(9425194677755081787)
XLA Ops:
  0.6 1.1 pack.3
  1.8 0.0 copy-start.10
  1.8 0.0 copy-start.7
  1.8 0.0 copy-start.8
  1.8 7.8 %collective-permute-start.6 = (bf16[1296,128]{1,0:T(8,128)(2,1)S(1)}, bf16[1296,128]{1,0:T(8,128)(2,1)S(1)}, u32[]{:S(2)}, u32[]{:S(2)}) collective-permute-start(bf16[1296,128]{1,0:T(8,128)(2,1)S(1)} %pack.3), channel_id=1, source_target_pairs={{0,4},{1,5},{2,6},{3,7},{4,0},{5,1},{6,2},{7,3},{8,12},{9,13},{10,... | collective-permute-start | bytes 995336 | tf_op jit(solution)/shard_map/ppermute | solution.py:659
  9.6 2.2 %pack.4 = (bf16[1296,128]{1,0:T(8,128)(2,1)}, bf16[1296,128]{1,0:T(8,128)(2,1)}) custom-call(s32[1]{0:T(128)} %bitcast.2.here, bf16[128,8192]{1,0:T(8,128)(2,1)} %x.11, bf16[128,2048]{1,0:T(8,128)(2,1)} %bc.5, bf16[128,128]{1,0:T(8,128)(2,1)} %dt.5), custom_call_target="tpu_custom_call" | custom-call | tf_op jit(solution)/shard_map/pack/pallas_call | solution.py:514
  11.9 0.1 collective-permute-start.3
  12.0 3.2 %collective-permute-start.2 = (bf16[1296,128]{1,0:T(8,128)(2,1)}, bf16[1296,128]{1,0:T(8,128)(2,1)}, u32[]{:S(2)}, u32[]{:S(2)}) collective-permute-start(bf16[1296,128]{1,0:T(8,128)(2,1)} %get-tuple-element.46), channel_id=1, source_target_pairs={{0,3},{1,4},{2,5},{3,6},{4,7},{5,0},{6,1},{7,2},{8,11},{9,12},{10,... | collective-permute-start | bytes 995336 | tf_op jit(solution)/shard_map/ppermute | solution.py:659
  15.2 0.6 fusion.2
  19.8 0.1 dynamic-slice_reduce_fusion.1
  19.9 0.0 copy-start.11
  20.0 3.2 %pack.5 = (bf16[1296,128]{1,0:T(8,128)(2,1)}, bf16[1296,128]{1,0:T(8,128)(2,1)}, bf16[1296,128]{1,0:T(8,128)(2,1)}, bf16[1296,128]{1,0:T(8,128)(2,1)}, bf16[1296,128]{1,0:T(8,128)(2,1)}) custom-call(s32[1]{0:T(128)} %bitcast.2.here, bf16[128,8192]{1,0:T(8,128)(2,1)} %x.11, bf16[128,2048]{1,0:T(8,128)(2,1)} %bc.5, bf16[128,128]{1,0:T(8,128)(2,1)} %dt.5), custom_call_target="tpu_custom_call" | custom-call | tf_op jit(solution)/shard_map/pack/pallas_call | solution.py:514
  23.2 1.4 %pad_add_fusion.slots = s32[2]{0:T(128)S(1)} fusion(s32[1]{0:T(128)} %bitcast.1, s32[1]{0:T(128)} %bitcast), kind=kLoop, calls=%fused_computation.36 | loop fusion | flops 2 | bytes 16 | tf_op jit(solution)/shard_map/stack | solution.py:733
  24.6 2.7 %movers.1 = (f32[1056,128]{1,0:T(8,128)}, f32[1056,128]{1,0:T(8,128)}) custom-call(s32[2]{0:T(128)S(1)} %pad_add_fusion.slots, f32[4,1024,128]{2,1,0:T(8,128)} %bitcast.31, f32[2,32,128]{2,1,0:T(8,128)S(1)} %pad_maximum_fusion.2.small), custom_call_target="tpu_custom_call" | custom-call | tf_op jit(solution)/shard_map/movers/pallas_call | solution.py:539
  27.3 2.7 %collective-permute-start = (f32[1056,128]{1,0:T(8,128)}, f32[1056,128]{1,0:T(8,128)S(1)}, u32[]{:S(2)}, u32[]{:S(2)}) collective-permute-start(f32[1056,128]{1,0:T(8,128)} %get-tuple-element.50), channel_id=1, source_target_pairs={{0,8},{8,16},{16,24},{24,32},{32,40},{40,48},{48,56},{56,64},{64,7... | collective-permute-start | bytes 1622024 | tf_op jit(solution)/shard_map/ppermute | solution.py:653
  30.0 0.0 collective-permute-start.1
  30.0 0.1 broadcast_in_dim.158
  30.1 0.1 broadcast_in_dim_reshape.4.rest_10_
  30.2 3.3 %copy.44 = bf16[16,8,8,1024]{3,2,0,1:T(8,128)(2,1)} copy(bf16[16,8,8,1024]{3,2,1,0:T(8,128)(2,1)} %bitcast.35) | data formatting | bytes 4194304 | tf_op jit(solution)/shard_map/reshape | solution.py:750
  33.5 0.2 convert_reduce_fusion
  33.7 0.1 select_reduce_fusion.2
  33.8 0.7 iota_compare_fusion.3
  34.5 0.1 pad_add_fusion.1.seg
  34.6 2.0 %collective-permute-done.lft = f32[1056,128]{1,0:T(8,128)S(1)} collective-permute-done((f32[1056,128]{1,0:T(8,128)}, f32[1056,128]{1,0:T(8,128)S(1)}, u32[]{:S(2)}, u32[]{:S(2)}) %collective-permute-start) | collective-permute-done | bytes 540704 | tf_op jit(solution)/shard_map/ppermute | solution.py:653
  36.7 2.7 %collective-permute-done.1.rgt = f32[1056,128]{1,0:T(8,128)} collective-permute-done((f32[1056,128]{1,0:T(8,128)}, f32[1056,128]{1,0:T(8,128)}, u32[]{:S(2)}, u32[]{:S(2)}) %collective-permute-start.1) | collective-permute-done | bytes 540704 | tf_op jit(solution)/shard_map/ppermute | solution.py:653
  39.4 0.7 slice.45
  40.2 0.1 copy.34
  40.3 0.2 select_reduce_fusion
  40.5 2.5 %collective-permute-start.5 = (bf16[1296,128]{1,0:T(8,128)(2,1)}, bf16[1296,128]{1,0:T(8,128)(2,1)}, u32[]{:S(2)}, u32[]{:S(2)}) collective-permute-start(bf16[1296,128]{1,0:T(8,128)(2,1)} %get-tuple-element.59), channel_id=1, source_target_pairs={{0,2},{1,3},{2,4},{3,5},{4,6},{5,7},{6,0},{7,1},{8,10},{9,11},{10,... | collective-permute-start | bytes 995336 | tf_op jit(solution)/shard_map/ppermute | solution.py:659
  43.0 1.2 %collective-permute-start.7 = (bf16[1296,128]{1,0:T(8,128)(2,1)}, bf16[1296,128]{1,0:T(8,128)(2,1)}, u32[]{:S(2)}, u32[]{:S(2)}) collective-permute-start(bf16[1296,128]{1,0:T(8,128)(2,1)} %get-tuple-element.61), channel_id=1, source_target_pairs={{0,6},{1,7},{2,0},{3,1},{4,2},{5,3},{6,4},{7,5},{8,14},{9,15},{10,... | collective-permute-start | bytes 995336 | tf_op jit(solution)/shard_map/ppermute | solution.py:659
  44.2 0.0 copy-start.12
  44.2 0.0 copy-start.13
  44.2 1.9 %initial.1.rest_17_ = f32[4,128,1024]{2,1,0:T(8,128)S(1)} custom-call(s32[16]{0:T(128)S(1)} %pad_add_fusion.1.seg, f32[4,1024,128]{2,1,0:T(8,128)S(1)} %bitcast.32, f32[1056,128]{1,0:T(8,128)S(1)} %collective-permute-done.lft, f32[1056,128]{1,0:T(8,128)} %collective-permute-done.1.rgt), custom_call_target="tpu_custom_call" | custom-call | flops 2000000000 | bytes 4194304 | tf_op jit(solution)/shard_map/initial/pallas_call | solution.py:551
  46.1 0.0 copy-start.5
  46.1 1.3 %copy-done.5 = f32[4,128,1024]{2,1,0:T(8,128)} copy-done((f32[4,128,1024]{2,1,0:T(8,128)}, f32[4,128,1024]{2,1,0:T(8,128)S(1)}, u32[]{:S(2)}) %copy-start.5) | copy-done | bytes 2097176
  47.4 0.0 collective-permute-done.3.rest_5_
  47.4 0.0 collective-permute-done.2.rest_3_
  47.4 1.9 %collective-permute-start.4 = (bf16[1296,128]{1,0:T(8,128)(2,1)}, bf16[1296,128]{1,0:T(8,128)(2,1)}, u32[]{:S(2)}, u32[]{:S(2)}) collective-permute-start(bf16[1296,128]{1,0:T(8,128)(2,1)} %get-tuple-element.57), channel_id=1, source_target_pairs={{0,1},{1,2},{2,3},{3,4},{4,5},{5,6},{6,7},{7,0},{8,9},{9,10},{10,1... | collective-permute-start | bytes 995336 | tf_op jit(solution)/shard_map/ppermute | solution.py:659
  49.4 0.7 collective-permute-start.8
  50.1 0.6 iota_compare_fusion.4
  50.8 0.0 collective-permute-done.6.rest_4_
  50.8 0.1 copy.37.rest_10_
  50.9 0.1 copy.38.rest_11_
  51.0 6.1 %all-to-all-start = ((bf16[8,128,1024]{2,1,0:T(8,128)(2,1)}), bf16[8,128,1024]{2,1,0:T(8,128)(2,1)S(1)}, u32[]{:S(2)}, u32[]{:S(2)}) async-start(bf16[8,128,1024]{2,1,0:T(8,128)(2,1)} %bitcast.34), calls=%async_computation | async-start | bytes 4194304 | tf_op jit(solution)/shard_map/all_to_all | solution.py:767
  57.1 0.0 copy-start.6
  57.1 0.0 collective-permute-done.5.rest_2_
  57.1 1.7 %collective-permute-done.7.rest_6_ = bf16[1296,128]{1,0:T(8,128)(2,1)} collective-permute-done((bf16[1296,128]{1,0:T(8,128)(2,1)}, bf16[1296,128]{1,0:T(8,128)(2,1)}, u32[]{:S(2)}, u32[]{:S(2)}) %collective-permute-start.7) | collective-permute-done | bytes 331808 | tf_op jit(solution)/shard_map/ppermute | solution.py:659
  58.8 11.4 %collective-permute-done.4.rest_1_ = bf16[1296,128]{1,0:T(8,128)(2,1)} collective-permute-done((bf16[1296,128]{1,0:T(8,128)(2,1)}, bf16[1296,128]{1,0:T(8,128)(2,1)}, u32[]{:S(2)}, u32[]{:S(2)}) %collective-permute-start.4) | collective-permute-done | bytes 331808 | tf_op jit(solution)/shard_map/ppermute | solution.py:659
  70.2 0.0 collective-permute-done.8.rest_7_
  70.2 5.4 %prep.1 = (bf16[4,128,256]{2,1,0:T(8,128)(2,1)S(1)}, bf16[1024,128]{1,0:T(8,128)(2,1)S(1)}, f32[4,256,256]{2,1,0:T(8,128)S(1)}, f32[4,256,128]{2,1,0:T(8,128)S(1...) custom-call(s32[16]{0:T(128)S(1)} %pad_add_fusion.1.seg, s32[1]{0:T(128)} %bitcast.2.here, ...), custom_call_target="tpu_custom_call" | custom-call | flops 6000000000 | bytes 8388608 | tf_op jit(solution)/shard_map/prep/pallas_call | solution.py:565
  75.6 19.3 %scan.1 = (f32[1024,1024]{1,0:T(8,128)}, f32[4,1024,128]{2,1,0:T(8,128)}, bf16[1056,128]{1,0:T(8,128)(2,1)}, bf16[1056,128]{1,0:T(8,128)(2,1)S(1)}, f32[16,1024]{1,0:T(8,128)S(1)}) custom-call(s32[16]{0:T(128)S(1)} %pad_add_fusion.1.seg, s32[1]{0:T(128)} %bitcast.2.here, bf16[1296,128]{1,0:T(8,128)(2,1)S(1)} %copy-done.2, ...), custom_call_target="tpu_custom_call" | custom-call | flops 20000000000 | bytes 16777216 | tf_op jit(solution)/shard_map/scan/pallas_call | solution.py:595
  95.0 0.0 copy-start.1
  95.0 0.7 collective-permute-start.9
  95.7 1.2 %collective-permute-start.10 = (bf16[1056,128]{1,0:T(8,128)(2,1)S(1)}, bf16[1056,128]{1,0:T(8,128)(2,1)S(1)}, u32[]{:S(2)}, u32[]{:S(2)}) collective-permute-start(bf16[1056,128]{1,0:T(8,128)(2,1)S(1)} %get-tuple-element.78), channel_id=1, source_target_pairs={{0,8},{8,16},{16,24},{24,32},{32,40},{40,48},{48,56},{56,64},{64,7... | collective-permute-start | bytes 811016 | tf_op jit(solution)/shard_map/ppermute | solution.py:653
  96.9 0.2 select_reduce_fusion.1
  97.2 4.3 %collective-permute-done.9 = bf16[1056,128]{1,0:T(8,128)(2,1)S(1)} collective-permute-done((bf16[1056,128]{1,0:T(8,128)(2,1)}, bf16[1056,128]{1,0:T(8,128)(2,1)S(1)}, u32[]{:S(2)}, u32[]{:S(2)}) %collective-permute-start.9) | collective-permute-done | bytes 270368 | tf_op jit(solution)/shard_map/ppermute | solution.py:653
  101.5 0.6 collective-permute-done.10
  102.0 0.1 select_select_fusion
  102.2 0.8 convert_dynamic-update-slice_fusion.1
  103.0 0.8 convert_dynamic-update-slice_fusion
  103.8 0.6 copy.41
  104.4 0.7 copy.40
  105.1 7.8 %all-to-all-done = bf16[8,128,1024]{2,1,0:T(8,128)(2,1)S(1)} async-done(((bf16[8,128,1024]{2,1,0:T(8,128)(2,1)}), bf16[8,128,1024]{2,1,0:T(8,128)(2,1)S(1)}, u32[]{:S(2)}, u32[]{:S(2)}) %all-to-all-start) | async-done | bytes 2097184 | tf_op jit(solution)/shard_map/all_to_all | solution.py:767
  112.9 3.8 %gate.1 = bf16[1024,1024]{1,0:T(8,128)(2,1)} custom-call(f32[1024,1024]{1,0:T(8,128)} %get-tuple-element.80.y_in, bf16[1024,1024]{1,0:T(8,128)(2,1)S(1)} %bitcast.30, f32[1,1024]{1,0:T(1,128)S(1)} %bitcast.33), custom_call_target="tpu_custom_call" | custom-call | flops 20000000 | bytes 8388608 | tf_op jit(solution)/shard_map/gate/pallas_call | solution.py:631
  (50 shorter events, 0.4 us)
Async XLA Ops:
  1.8 13.4 %copy-start.10 = (s32[128]{0:T(128)S(1)}, s32[128]{0:T(128)}, u32[]{:S(2)}) copy-start(s32[128]{0:T(128)} %param.30) | copy-start | bytes 1540
  1.8 16.6 %copy-start.7 = (f32[4,3,1024]{2,0,1:T(4,128)S(1)}, f32[4,3,1024]{2,0,1:T(4,128)}, u32[]{:S(2)}) copy-start(f32[4,3,1024]{2,0,1:T(4,128)} %param.27) | copy-start | bytes 147460
  1.8 18.0 %copy-start.8 = (f32[4,3,256]{2,0,1:T(4,128)S(1)}, f32[4,3,256]{2,0,1:T(4,128)}, u32[]{:S(2)}) copy-start(f32[4,3,256]{2,0,1:T(4,128)} %param.28) | copy-start | bytes 36868
  1.8 49.0 %collective-permute-start.6 = (bf16[1296,128]{1,0:T(8,128)(2,1)S(1)}, bf16[1296,128]{1,0:T(8,128)(2,1)S(1)}, u32[]{:S(2)}, u32[]{:S(2)}) collective-permute-start(bf16[1296,128]{1,0:T(8,128)(2,1)S(1)} %pack.3), channel_id=1, source_target_pairs={{0,4},{1,5},{2,6},{3,7},{4,0},{5,1},{6,2},{7,3},{8,12},{9,13},{10,... | collective-permute-start | bytes 995336 | tf_op jit(solution)/shard_map/ppermute | solution.py:659
  11.9 35.6 %collective-permute-start.3 = (bf16[1296,128]{1,0:T(8,128)(2,1)}, bf16[1296,128]{1,0:T(8,128)(2,1)}, u32[]{:S(2)}, u32[]{:S(2)}) collective-permute-start(bf16[1296,128]{1,0:T(8,128)(2,1)} %get-tuple-element.56), channel_id=1, source_target_pairs={{0,5},{1,6},{2,7},{3,0},{4,1},{5,2},{6,3},{7,4},{8,13},{9,14},{10,... | collective-permute-start | bytes 995336 | tf_op jit(solution)/shard_map/ppermute | solution.py:659
  12.0 35.5 %collective-permute-start.2 = (bf16[1296,128]{1,0:T(8,128)(2,1)}, bf16[1296,128]{1,0:T(8,128)(2,1)}, u32[]{:S(2)}, u32[]{:S(2)}) collective-permute-start(bf16[1296,128]{1,0:T(8,128)(2,1)} %get-tuple-element.46), channel_id=1, source_target_pairs={{0,3},{1,4},{2,5},{3,6},{4,7},{5,0},{6,1},{7,2},{8,11},{9,12},{10,... | collective-permute-start | bytes 995336 | tf_op jit(solution)/shard_map/ppermute | solution.py:659
  19.9 10.1 %copy-start.11 = (f32[16]{0:T(128)S(1)}, f32[16]{0:T(128)}, u32[]{:S(2)}) copy-start(f32[16]{0:T(128)} %param.24) | copy-start | bytes 196
  27.3 9.3 %collective-permute-start = (f32[1056,128]{1,0:T(8,128)}, f32[1056,128]{1,0:T(8,128)S(1)}, u32[]{:S(2)}, u32[]{:S(2)}) collective-permute-start(f32[1056,128]{1,0:T(8,128)} %get-tuple-element.50), channel_id=1, source_target_pairs={{0,8},{8,16},{16,24},{24,32},{32,40},{40,48},{48,56},{56,64},{64,7... | collective-permute-start | bytes 1622024 | tf_op jit(solution)/shard_map/ppermute | solution.py:653
  30.0 9.4 %collective-permute-start.1 = (f32[1056,128]{1,0:T(8,128)}, f32[1056,128]{1,0:T(8,128)}, u32[]{:S(2)}, u32[]{:S(2)}) collective-permute-start(f32[1056,128]{1,0:T(8,128)} %get-tuple-element.51), channel_id=1, source_target_pairs={{0,248},{8,0},{16,8},{24,16},{32,24},{40,32},{48,40},{56,48},{64,5... | collective-permute-start | bytes 1622024 | tf_op jit(solution)/shard_map/ppermute | solution.py:653
  30.2 3.3 %copy-start.9 = (s32[128]{0:T(128)S(1)}, s32[128]{0:T(128)}, u32[]{:S(2)}) copy-start(s32[128]{0:T(128)} %param.31) | copy-start | bytes 1540
  30.2 3.5 %copy-start.14 = (s32[128]{0:T(128)S(1)}, s32[128]{0:T(128)}, u32[]{:S(2)}) copy-start(s32[128]{0:T(128)} %param.29) | copy-start | bytes 1540
  30.2 14.0 %copy-start = (f32[4,16,64,128]{3,2,1,0:T(8,128)S(1)}, f32[4,16,64,128]{3,2,1,0:T(8,128)}, u32[]{:S(2)}) copy-start(f32[4,16,64,128]{3,2,1,0:T(8,128)} %param.26) | copy-start | bytes 6291460
  40.5 16.6 %collective-permute-start.5 = (bf16[1296,128]{1,0:T(8,128)(2,1)}, bf16[1296,128]{1,0:T(8,128)(2,1)}, u32[]{:S(2)}, u32[]{:S(2)}) collective-permute-start(bf16[1296,128]{1,0:T(8,128)(2,1)} %get-tuple-element.59), channel_id=1, source_target_pairs={{0,2},{1,3},{2,4},{3,5},{4,6},{5,7},{6,0},{7,1},{8,10},{9,11},{10,... | collective-permute-start | bytes 995336 | tf_op jit(solution)/shard_map/ppermute | solution.py:659
  43.0 15.9 %collective-permute-start.7 = (bf16[1296,128]{1,0:T(8,128)(2,1)}, bf16[1296,128]{1,0:T(8,128)(2,1)}, u32[]{:S(2)}, u32[]{:S(2)}) collective-permute-start(bf16[1296,128]{1,0:T(8,128)(2,1)} %get-tuple-element.61), channel_id=1, source_target_pairs={{0,6},{1,7},{2,0},{3,1},{4,2},{5,3},{6,4},{7,5},{8,14},{9,15},{10,... | collective-permute-start | bytes 995336 | tf_op jit(solution)/shard_map/ppermute | solution.py:659
  44.2 6.7 %copy-start.12 = (f32[16]{0:T(128)S(1)}, f32[16]{0:T(128)}, u32[]{:S(2)}) copy-start(f32[16]{0:T(128)} %param.22) | copy-start | bytes 196
  44.2 6.8 %copy-start.13 = (f32[16]{0:T(128)S(1)}, f32[16]{0:T(128)}, u32[]{:S(2)}) copy-start(f32[16]{0:T(128)} %param.23) | copy-start | bytes 196
  46.1 1.3 %copy-start.5 = (f32[4,128,1024]{2,1,0:T(8,128)}, f32[4,128,1024]{2,1,0:T(8,128)S(1)}, u32[]{:S(2)}) copy-start(f32[4,128,1024]{2,1,0:T(8,128)S(1)} %initial.1.rest_17_) | copy-start | bytes 6291460
  47.4 22.7 %collective-permute-start.4 = (bf16[1296,128]{1,0:T(8,128)(2,1)}, bf16[1296,128]{1,0:T(8,128)(2,1)}, u32[]{:S(2)}, u32[]{:S(2)}) collective-permute-start(bf16[1296,128]{1,0:T(8,128)(2,1)} %get-tuple-element.57), channel_id=1, source_target_pairs={{0,1},{1,2},{2,3},{3,4},{4,5},{5,6},{6,7},{7,0},{8,9},{9,10},{10,1... | collective-permute-start | bytes 995336 | tf_op jit(solution)/shard_map/ppermute | solution.py:659
  49.4 20.8 %collective-permute-start.8 = (bf16[1296,128]{1,0:T(8,128)(2,1)}, bf16[1296,128]{1,0:T(8,128)(2,1)}, u32[]{:S(2)}, u32[]{:S(2)}) collective-permute-start(bf16[1296,128]{1,0:T(8,128)(2,1)} %get-tuple-element.63), channel_id=1, source_target_pairs={{0,7},{1,0},{2,1},{3,2},{4,3},{5,4},{6,5},{7,6},{8,15},{9,8},{10,9... | collective-permute-start | bytes 995336 | tf_op jit(solution)/shard_map/ppermute | solution.py:659
  51.0 19.2 %copy-start.2 = (bf16[1296,128]{1,0:T(8,128)(2,1)S(1)}, bf16[1296,128]{1,0:T(8,128)(2,1)}, u32[]{:S(2)}) copy-start(bf16[1296,128]{1,0:T(8,128)(2,1)} %get-tuple-element.48.rest_0_) | copy-start | bytes 995332
  51.0 19.2 %copy-start.4 = (f32[5,256]{1,0:T(8,128)S(1)}, f32[5,256]{1,0:T(8,128)}, u32[]{:S(2)}) copy-start(f32[5,256]{1,0:T(8,128)} %rest_9_.2) | copy-start | bytes 15364
  51.0 61.9 %all-to-all-start = ((bf16[8,128,1024]{2,1,0:T(8,128)(2,1)}), bf16[8,128,1024]{2,1,0:T(8,128)(2,1)S(1)}, u32[]{:S(2)}, u32[]{:S(2)}) async-start(bf16[8,128,1024]{2,1,0:T(8,128)(2,1)} %bitcast.34), calls=%async_computation | async-start | bytes 4194304 | tf_op jit(solution)/shard_map/all_to_all | solution.py:767
  57.1 18.5 %copy-start.3 = (f32[5,1024]{1,0:T(8,128)S(1)}, f32[5,1024]{1,0:T(8,128)}, u32[]{:S(2)}) copy-start(f32[5,1024]{1,0:T(8,128)} %rest_9_.3) | copy-start | bytes 61444
  57.1 18.5 %copy-start.6 = (f32[4,128,1024]{2,1,0:T(8,128)S(1)}, f32[4,128,1024]{2,1,0:T(8,128)}, u32[]{:S(2)}) copy-start(f32[4,128,1024]{2,1,0:T(8,128)} %copy-done.5) | copy-start | bytes 6291460
  95.0 18.0 %copy-start.1 = (f32[1024]{0:T(1024)S(1)}, f32[1024]{0:T(1024)}, u32[]{:S(2)}) copy-start(f32[1024]{0:T(1024)} %param.25) | copy-start | bytes 12292
  95.0 6.5 %collective-permute-start.9 = (bf16[1056,128]{1,0:T(8,128)(2,1)}, bf16[1056,128]{1,0:T(8,128)(2,1)S(1)}, u32[]{:S(2)}, u32[]{:S(2)}) collective-permute-start(bf16[1056,128]{1,0:T(8,128)(2,1)} %get-tuple-element.77), channel_id=1, source_target_pairs={{0,248},{8,0},{16,8},{24,16},{32,24},{40,32},{48,40},{56,48},{64,5... | collective-permute-start | bytes 811016 | tf_op jit(solution)/shard_map/ppermute | solution.py:653
  95.7 6.3 %collective-permute-start.10 = (bf16[1056,128]{1,0:T(8,128)(2,1)S(1)}, bf16[1056,128]{1,0:T(8,128)(2,1)S(1)}, u32[]{:S(2)}, u32[]{:S(2)}) collective-permute-start(bf16[1056,128]{1,0:T(8,128)(2,1)S(1)} %get-tuple-element.78), channel_id=1, source_target_pairs={{0,8},{8,16},{16,24},{24,32},{32,40},{40,48},{48,56},{56,64},{64,7... | collective-permute-start | bytes 811016 | tf_op jit(solution)/shard_map/ppermute | solution.py:653

commit v4 on v3

--- a/solution.py
+++ b/solution.py
@@ -29,7 +29,7 @@
 DT_ROW = BC_ROW + BC_TILES * SRC_ROWS
 BLOCK_ROWS = DT_ROW + GH
 MOVER_ROWS = GC + 32
-GATE_ROWS = 128
+GATE_ROWS = 256
 ORDER = (4, 3, 5, 2, 6, 1, 7)
 FIRST = (4, 3, 5)
 SECOND = (2, 6)
@@ -117,12 +117,12 @@
         terms_ref[16 * i : 16 * i + 16, lanes] = part
 
 
-def copy_all(copies, sems):
+def copy_all(copies, sems, later=()):
     started = [
         pltpu.make_async_copy(source, target, sems.at[i])
         for i, (source, target) in enumerate(copies)
     ]
-    for copy in started:
+    for copy in [*started, *later]:
         copy.start()
     for copy in started:
         copy.wait()
@@ -206,14 +206,6 @@
     return (here[0] + (TENSOR - d)) % TENSOR
 
 
-def prep_kernel(
-    seg,
-    here,
-    *rest,
-):
-    prep_body(seg, here, rest[:TENSOR], *rest[TENSOR:])
-
-
 def prep_body(
     seg,
     here,
@@ -234,6 +226,7 @@
     b_rows,
     terms,
     sems,
+    loads,
 ):
     copies = []
     for d in range(TENSOR):
@@ -243,7 +236,7 @@
             part = blocks[d].at[BC_ROW + SRC_ROWS * i : BC_ROW + SRC_ROWS * (i + 1), :]
             copies.append((part, bc_rows.at[rows, LANES * i : LANES * (i + 1)]))
         copies.append((blocks[d].at[DT_ROW:BLOCK_ROWS, :], dt_rows.at[source]))
-    copy_all(copies, sems)
+    copy_all(copies, sems, loads)
     every = slice(0, 2 * STATE)
     last = last_rows(bc_rows, every, seg)
     last_out[...] = last
@@ -296,14 +289,33 @@
     dec_out[...] = mm(dec_hi, spread) + mm(dec_lo, spread)
 
 
-def main_kernel(seg, here, *rest):
-    main_body(seg, here, rest[:TENSOR], *rest[TENSOR:])
+def scan_kernel(seg, here, *rest):
+    blocks, rest = rest[:TENSOR], rest[TENSOR:]
+    conv_x, conv_bc, x_param, skip, bc_param, rate, bias, init = rest[:8]
+    y_out, own_out, lft_out, rgt_out, last_x, last_bc = rest[8:14]
+    prep_out, prep_scratch, scratch = rest[14:20], rest[20:25], rest[25:]
+    x_rows, x_sems = scratch[7], scratch[9]
+    loads = [pltpu.make_async_copy(init, scratch[3], x_sems.at[TENSOR * TILES])]
+    for d in range(TENSOR):
+        rows = pl.ds(pl.multiple_of(source_of(here, d) * SRC_ROWS, SRC_ROWS), SRC_ROWS)
+        for i in range(TILES):
+            part = blocks[d].at[SRC_ROWS * i : SRC_ROWS * (i + 1), :]
+            place = x_rows.at[rows, LANES * i : LANES * (i + 1)]
+            loads.append(pltpu.make_async_copy(part, place, x_sems.at[d * TILES + i]))
+    prep_body(
+        seg, here, blocks, conv_bc, bc_param, rate, bias, *prep_out, last_bc, *prep_scratch, loads
+    )
+    for copy in loads:
+        copy.wait()
+
+    main_body(
+        seg, conv_x, x_param, skip, *prep_out, last_bc, y_out, own_out, lft_out, rgt_out,
+        last_x, *scratch
+    )
 
 
 def main_body(
     seg,
-    here,
-    blocks,
     conv_state,
     param,
     skip,
@@ -313,7 +325,6 @@
     col_in,
     row_in,
     dec_in,
-    init_in,
     last_bc,
     y_out,
     own_out,
@@ -337,13 +348,6 @@
         rows = pl.ds(pl.multiple_of(c * Q, Q), Q)
         return pltpu.make_async_copy(y_stage.at[rows, :], y_out.at[rows, :], y_sems.at[c])
 
-    copies = []
-    for d in range(TENSOR):
-        rows = pl.ds(pl.multiple_of(source_of(here, d) * SRC_ROWS, SRC_ROWS), SRC_ROWS)
-        for i in range(TILES):
-            part = blocks[d].at[SRC_ROWS * i : SRC_ROWS * (i + 1), :]
-            copies.append((part, x_in.at[rows, LANES * i : LANES * (i + 1)]))
-    copy_all(copies, sems)
     terms[...] = jnp.zeros_like(terms)
     targets = boundary_targets((1, 128), 1, seg)
     for lt in range(GC // 256):
@@ -363,10 +367,6 @@
             lanes = slice(256 * lt, 256 * (lt + 1))
             value = conv_rows(x_in, r0, 64, lanes, param, terms, targets)
             x_conv[pl.ds(r0, 64), lanes] = value.astype(BF16)
-
-    @pl.loop(0, SLOTS)
-    def _(k):
-        state[k] = init_in[k]
 
     @pl.loop(0, CHUNKS)
     def _(c):
@@ -550,7 +550,7 @@
 def initial(seg, own, lft, rgt):
     return pl.pallas_call(
         init_kernel,
-        out_shape=jax.ShapeDtypeStruct((SLOTS, STATE, GC), F32),
+        out_shape=pltpu.HBM((SLOTS, STATE, GC), F32),
         in_specs=[SMEM] + [VMEM] * 3,
         out_specs=VMEM,
         compiler_params=params(8),
@@ -561,49 +561,31 @@
     )(seg, own, lft, rgt)
 
 
-def prep(seg, here, blocks, conv_state, param, rate, bias):
+def scan(seg, here, blocks, *operands):
     return pl.pallas_call(
-        prep_kernel,
-        out_shape=(
-            jax.ShapeDtypeStruct((CHUNKS, STATE, Q), BF16),
-            jax.ShapeDtypeStruct((ROWS, STATE), BF16),
-            jax.ShapeDtypeStruct((CHUNKS, Q, Q), F32),
-            jax.ShapeDtypeStruct((CHUNKS, Q, 128), F32),
-            jax.ShapeDtypeStruct((CHUNKS, GH, Q), F32),
-            jax.ShapeDtypeStruct((16, GC), F32),
-            jax.ShapeDtypeStruct((16, 2 * STATE), F32),
-        ),
-        in_specs=[SMEM, SMEM] + [ANY] * TENSOR + [VMEM] * 4,
-        out_specs=(VMEM,) * 7,
-        scratch_shapes=[
-            pltpu.VMEM((ROWS, 2 * STATE), BF16),
-            pltpu.VMEM((TENSOR, GH, LANES), BF16),
-            pltpu.VMEM((ROWS, STATE), BF16),
-            pltpu.VMEM((128, 2 * STATE), BF16),
-            pltpu.SemaphoreType.DMA(((BC_TILES + 1) * TENSOR,)),
-        ],
-        compiler_params=params(8),
-        cost_estimate=pl.CostEstimate(
-            flops=6_000_000_000, bytes_accessed=8 * MIB, transcendentals=500_000
-        ),
-        name="prep",
-    )(seg, here, *blocks, conv_state, param, rate, bias)
-
-
-def scan(seg, here, blocks, conv_state, param, skip, prepared, init):
-    b_t, c_rows, mix, col, row, dec, last_bc = prepared
-    return pl.pallas_call(
-        main_kernel,
+        scan_kernel,
         out_shape=(
             pltpu.HBM((ROWS, GC), F32),
             jax.ShapeDtypeStruct((SLOTS, GC, STATE), F32),
             jax.ShapeDtypeStruct((MOVER_ROWS, STATE), BF16),
             jax.ShapeDtypeStruct((MOVER_ROWS, STATE), BF16),
             jax.ShapeDtypeStruct((16, GC), F32),
+            jax.ShapeDtypeStruct((16, 2 * STATE), F32),
         ),
-        in_specs=[SMEM, SMEM] + [ANY] * TENSOR + [VMEM] * 11,
-        out_specs=(HBM,) + (VMEM,) * 4,
+        in_specs=[SMEM, SMEM] + [ANY] * TENSOR + [VMEM] * (len(operands) - 1) + [HBM],
+        out_specs=(HBM,) + (VMEM,) * 5,
         scratch_shapes=[
+            pltpu.VMEM((CHUNKS, STATE, Q), BF16),
+            pltpu.VMEM((ROWS, STATE), BF16),
+            pltpu.VMEM((CHUNKS, Q, Q), F32),
+            pltpu.VMEM((CHUNKS, Q, 128), F32),
+            pltpu.VMEM((CHUNKS, GH, Q), F32),
+            pltpu.VMEM((16, GC), F32),
+            pltpu.VMEM((ROWS, 2 * STATE), BF16),
+            pltpu.VMEM((TENSOR, GH, LANES), BF16),
+            pltpu.VMEM((ROWS, STATE), BF16),
+            pltpu.VMEM((128, 2 * STATE), BF16),
+            pltpu.SemaphoreType.DMA(((BC_TILES + 1) * TENSOR,)),
             pltpu.VMEM((128, GC), BF16),
             pltpu.VMEM((ROWS, GC), BF16),
             pltpu.VMEM((Q, GC), BF16),
@@ -613,18 +595,16 @@
             pltpu.VMEM((256, GC), BF16),
             pltpu.VMEM((ROWS, GC), BF16),
             pltpu.VMEM((32, STATE), F32),
-            pltpu.SemaphoreType.DMA((TENSOR * TILES,)),
+            pltpu.SemaphoreType.DMA((TENSOR * TILES + 1,)),
             pltpu.VMEM((ROWS, GC), F32),
             pltpu.SemaphoreType.DMA((CHUNKS,)),
         ],
-        compiler_params=params(20),
+        compiler_params=params(28),
         cost_estimate=pl.CostEstimate(
-            flops=20_000_000_000, bytes_accessed=16 * MIB, transcendentals=5_000_000
+            flops=26_000_000_000, bytes_accessed=16 * MIB, transcendentals=5_500_000
         ),
         name="scan",
-    )(
-        seg, here, *blocks, conv_state, param, skip, b_t, c_rows, mix, col, row, dec, init, last_bc
-    )
+    )(seg, here, *blocks, *operands)
 
 
 def gate(y, z_rows, gain):
@@ -768,28 +748,22 @@
     z_rows = z_rows.reshape(ROWS, GC)
 
     in_order = [blocks[d] for d in range(TENSOR)]
-    prepared = prep(
-        seg,
-        here_ref,
-        in_order,
-        conv_init[:, GC:],
-        conv_bc_param,
-        rate,
-        bias,
-    )
-    y, own_new, back_left, back_right, last_x = scan(
+    y, own_new, back_left, back_right, last_x, last_bc = scan(
         seg,
         here_ref,
         in_order,
         conv_init[:, :GC],
+        conv_init[:, GC:],
         conv_x_param,
         skip,
-        prepared,
-        init,
+        conv_bc_param,
+        rate,
+        bias,
+        in_hbm(init),
     )
     returned_right = shifted(back_left, -1)
     returned_left = shifted(back_right, 1)
-    last = jnp.concatenate([last_x, prepared[6]], axis=1)[: 3 * SLOTS].reshape(SLOTS, 3, width)
+    last = jnp.concatenate([last_x, last_bc], axis=1)[: 3 * SLOTS].reshape(SLOTS, 3, width)
 
     new_ssm = own_new
     for packed, slot in ((returned_right, slot_right), (returned_left, slot_left)):

time: 118 us -> 117 us (level)
  waiting for transfers between devices: 30.5 us -> 33 us
  local copies, waits for them, and re-layouts: 7.39 us -> 6.07 us
  Pallas kernels: 39.8 us -> 38.5 us
    all_to_all x1, waiting for transfers between devices: 7.85 us -> 10.5 us  [shards(): lax.all_to_all(z_sent, 'tensor', split_axis=0, concat_axis=0, tiled=True)]
    unnamed x33 -> x29, local copies, waits for them, and re-layouts: 2.65 us -> 1.33 us
    pallas_call x3 -> x2, Pallas kernels: 26.7 us -> 25.6 us  [the longest x1 22.3 us: scan(): pl.pallas_call(scan_kernel, out_shape=(pltpu.HBM((ROWS, GC), F32), jax.Sh...]
  transfers between devices with their start and end apart: 12 -> 12, of which waited for: 7 -> 7; matrix products, arithmetic and copies ran while one was open for 10% -> 10% of each run, Pallas kernels for 30% -> 29%
where the time goes in v4:
time: 117 us
  Pallas kernels  38.5 us (33%)
  waiting for transfers between devices  33 us (28%)
  starting transfers between devices  28.3 us (24%)
  local copies, waits for them, and re-layouts  6.07 us (5%)
  other arithmetic  5.92 us (5%)
  between operations  5.05 us (4%)
    pallas_call x1, Pallas kernels, scan(): pl.pallas_call(scan_kernel, out_shape=(pltpu.HBM((ROWS, GC), F32), jax.Sh...  22.3 us
    ppermute x7, starting transfers between devices, rotated(): return lax.ppermute(value, 'tensor', pairs)  17.5 us
    ppermute x7, waiting for transfers between devices, rotated(): return lax.ppermute(value, 'tensor', pairs)  13.1 us
    all_to_all x1, waiting for transfers between devices, shards(): lax.all_to_all(z_sent, 'tensor', split_axis=0, concat_axis=0, tiled=True)  10.5 us
    ppermute x4, waiting for transfers between devices, shifted(): return lax.ppermute(value, 'dp', pairs)  9.51 us
    pallas_call x3, Pallas kernels, pack(): pl.pallas_call(functools.partial(pack_kernel, offsets), out_shape=(jax.Sh...  6.57 us
    all_to_all x1, starting transfers between devices, shards(): lax.all_to_all(z_sent, 'tensor', split_axis=0, concat_axis=0, tiled=True)  6.19 us
    ppermute x4, starting transfers between devices, shifted(): return lax.ppermute(value, 'dp', pairs)  4.59 us
  transfers between devices with their start and end apart: 12, of which 7 were waited for; matrix products, arithmetic and copies ran while one was open for 10% of the time, Pallas kernels for 29%

profile of v4, /device:TPU:1, one launch (start us, length us, event | category | flops | bytes accessed | tf_op | source)
XLA Modules:
  0.0 116.8 jit_solution(16336654295053862290)
XLA Ops:
  0.6 1.1 pack.3
  1.8 0.0 copy-start.8
  1.8 0.0 copy-start.5
  1.8 0.0 copy-start.6
  1.8 7.8 %collective-permute-start.6 = (bf16[1296,128]{1,0:T(8,128)(2,1)S(1)}, bf16[1296,128]{1,0:T(8,128)(2,1)S(1)}, u32[]{:S(2)}, u32[]{:S(2)}) collective-permute-start(bf16[1296,128]{1,0:T(8,128)(2,1)S(1)} %pack.3), channel_id=1, source_target_pairs={{0,4},{1,5},{2,6},{3,7},{4,0},{5,1},{6,2},{7,3},{8,12},{9,13},{10,... | collective-permute-start | bytes 995336 | tf_op jit(solution)/shard_map/ppermute | solution.py:639
  9.6 2.2 %pack.4 = (bf16[1296,128]{1,0:T(8,128)(2,1)}, bf16[1296,128]{1,0:T(8,128)(2,1)}) custom-call(s32[1]{0:T(128)} %bitcast.2.here, bf16[128,8192]{1,0:T(8,128)(2,1)} %x.11, bf16[128,2048]{1,0:T(8,128)(2,1)} %bc.5, bf16[128,128]{1,0:T(8,128)(2,1)} %dt.5), custom_call_target="tpu_custom_call" | custom-call | tf_op jit(solution)/shard_map/pack/pallas_call | solution.py:514
  11.9 0.1 collective-permute-start.3
  12.0 3.2 %collective-permute-start.2 = (bf16[1296,128]{1,0:T(8,128)(2,1)}, bf16[1296,128]{1,0:T(8,128)(2,1)}, u32[]{:S(2)}, u32[]{:S(2)}) collective-permute-start(bf16[1296,128]{1,0:T(8,128)(2,1)} %get-tuple-element.40), channel_id=1, source_target_pairs={{0,3},{1,4},{2,5},{3,6},{4,7},{5,0},{6,1},{7,2},{8,11},{9,12},{10,... | collective-permute-start | bytes 995336 | tf_op jit(solution)/shard_map/ppermute | solution.py:639
  15.2 0.6 fusion.2
  18.4 0.0 copy-done.5
  19.8 0.1 dynamic-slice_reduce_fusion.1
  20.0 0.0 copy-start.9
  20.0 3.2 %pack.5 = (bf16[1296,128]{1,0:T(8,128)(2,1)}, bf16[1296,128]{1,0:T(8,128)(2,1)}, bf16[1296,128]{1,0:T(8,128)(2,1)}, bf16[1296,128]{1,0:T(8,128)(2,1)}, bf16[1296,128]{1,0:T(8,128)(2,1)}) custom-call(s32[1]{0:T(128)} %bitcast.2.here, bf16[128,8192]{1,0:T(8,128)(2,1)} %x.11, bf16[128,2048]{1,0:T(8,128)(2,1)} %bc.5, bf16[128,128]{1,0:T(8,128)(2,1)} %dt.5), custom_call_target="tpu_custom_call" | custom-call | tf_op jit(solution)/shard_map/pack/pallas_call | solution.py:514
  23.2 1.4 %pad_add_fusion.slots = s32[2]{0:T(128)S(1)} fusion(s32[1]{0:T(128)} %bitcast.1, s32[1]{0:T(128)} %bitcast), kind=kLoop, calls=%fused_computation.36 | loop fusion | flops 2 | bytes 16 | tf_op jit(solution)/shard_map/stack | solution.py:713
  24.6 2.7 %movers.1 = (f32[1056,128]{1,0:T(8,128)}, f32[1056,128]{1,0:T(8,128)}) custom-call(s32[2]{0:T(128)S(1)} %pad_add_fusion.slots, f32[4,1024,128]{2,1,0:T(8,128)} %bitcast.31, f32[2,32,128]{2,1,0:T(8,128)S(1)} %pad_maximum_fusion.2.small), custom_call_target="tpu_custom_call" | custom-call | tf_op jit(solution)/shard_map/movers/pallas_call | solution.py:539
  27.3 2.7 %collective-permute-start = (f32[1056,128]{1,0:T(8,128)}, f32[1056,128]{1,0:T(8,128)S(1)}, u32[]{:S(2)}, u32[]{:S(2)}) collective-permute-start(f32[1056,128]{1,0:T(8,128)} %get-tuple-element.44), channel_id=1, source_target_pairs={{0,8},{8,16},{16,24},{24,32},{32,40},{40,48},{48,56},{56,64},{64,7... | collective-permute-start | bytes 1622024 | tf_op jit(solution)/shard_map/ppermute | solution.py:633
  30.0 0.0 collective-permute-start.1
  30.0 0.1 broadcast_in_dim.158
  30.1 0.1 broadcast_in_dim_reshape.4.rest_11_
  30.2 3.3 %copy.44 = bf16[16,8,8,1024]{3,2,0,1:T(8,128)(2,1)} copy(bf16[16,8,8,1024]{3,2,1,0:T(8,128)(2,1)} %bitcast.35) | data formatting | bytes 4194304 | tf_op jit(solution)/shard_map/reshape | solution.py:730
  33.5 0.0 copy-done.7
  33.5 0.2 convert_reduce_fusion
  33.7 0.1 select_reduce_fusion.2
  33.8 0.7 iota_compare_fusion.3
  34.5 0.1 pad_add_fusion.1.seg
  34.6 2.0 %collective-permute-done.lft = f32[1056,128]{1,0:T(8,128)S(1)} collective-permute-done((f32[1056,128]{1,0:T(8,128)}, f32[1056,128]{1,0:T(8,128)S(1)}, u32[]{:S(2)}, u32[]{:S(2)}) %collective-permute-start) | collective-permute-done | bytes 540704 | tf_op jit(solution)/shard_map/ppermute | solution.py:633
  36.6 2.7 %collective-permute-done.1.rgt = f32[1056,128]{1,0:T(8,128)} collective-permute-done((f32[1056,128]{1,0:T(8,128)}, f32[1056,128]{1,0:T(8,128)}, u32[]{:S(2)}, u32[]{:S(2)}) %collective-permute-start.1) | collective-permute-done | bytes 540704 | tf_op jit(solution)/shard_map/ppermute | solution.py:633
  39.4 0.7 slice.45
  40.2 0.1 copy.34
  40.2 0.2 select_reduce_fusion
  40.5 2.5 %collective-permute-start.5 = (bf16[1296,128]{1,0:T(8,128)(2,1)}, bf16[1296,128]{1,0:T(8,128)(2,1)}, u32[]{:S(2)}, u32[]{:S(2)}) collective-permute-start(bf16[1296,128]{1,0:T(8,128)(2,1)} %get-tuple-element.53), channel_id=1, source_target_pairs={{0,2},{1,3},{2,4},{3,5},{4,6},{5,7},{6,0},{7,1},{8,10},{9,11},{10,... | collective-permute-start | bytes 995336 | tf_op jit(solution)/shard_map/ppermute | solution.py:639
  42.9 1.2 %collective-permute-start.7 = (bf16[1296,128]{1,0:T(8,128)(2,1)}, bf16[1296,128]{1,0:T(8,128)(2,1)}, u32[]{:S(2)}, u32[]{:S(2)}) collective-permute-start(bf16[1296,128]{1,0:T(8,128)(2,1)} %get-tuple-element.55), channel_id=1, source_target_pairs={{0,6},{1,7},{2,0},{3,1},{4,2},{5,3},{6,4},{7,5},{8,14},{9,15},{10,... | collective-permute-start | bytes 995336 | tf_op jit(solution)/shard_map/ppermute | solution.py:639
  44.1 0.0 copy-done
  44.1 0.0 copy-start.10
  44.2 0.0 copy-start.11
  44.2 3.3 %initial.1.rest_15_ = f32[4,128,1024]{2,1,0:T(8,128)} custom-call(s32[16]{0:T(128)S(1)} %pad_add_fusion.1.seg, f32[4,1024,128]{2,1,0:T(8,128)S(1)} %bitcast.32, f32[1056,128]{1,0:T(8,128)S(1)} %collective-permute-done.lft, f32[1056,128]{1,0:T(8,128)} %collective-permute-done.1.rgt), custom_call_target="tpu_custom_call" | custom-call | flops 2000000000 | bytes 4194304 | tf_op jit(solution)/shard_map/initial/pallas_call | solution.py:551
  47.4 0.0 collective-permute-done.3.rest_5_
  47.4 0.0 collective-permute-done.2.rest_3_
  47.4 1.9 %collective-permute-start.4 = (bf16[1296,128]{1,0:T(8,128)(2,1)}, bf16[1296,128]{1,0:T(8,128)(2,1)}, u32[]{:S(2)}, u32[]{:S(2)}) collective-permute-start(bf16[1296,128]{1,0:T(8,128)(2,1)} %get-tuple-element.51), channel_id=1, source_target_pairs={{0,1},{1,2},{2,3},{3,4},{4,5},{5,6},{6,7},{7,0},{8,9},{9,10},{10,1... | collective-permute-start | bytes 995336 | tf_op jit(solution)/shard_map/ppermute | solution.py:639
  49.4 0.7 collective-permute-start.8
  50.1 0.6 iota_compare_fusion.4
  50.8 0.0 collective-permute-done.6.rest_4_
  50.8 0.1 copy.37.rest_13_
  50.9 0.0 copy-done.11
  50.9 0.1 copy.38.rest_14_
  51.0 6.2 %all-to-all-start = ((bf16[8,128,1024]{2,1,0:T(8,128)(2,1)}), bf16[8,128,1024]{2,1,0:T(8,128)(2,1)S(1)}, u32[]{:S(2)}, u32[]{:S(2)}) async-start(bf16[8,128,1024]{2,1,0:T(8,128)(2,1)} %bitcast.34), calls=%async_computation | async-start | bytes 4194304 | tf_op jit(solution)/shard_map/all_to_all | solution.py:747
  57.2 0.0 collective-permute-done.5.rest_2_
  57.2 1.6 %collective-permute-done.7.rest_6_ = bf16[1296,128]{1,0:T(8,128)(2,1)} collective-permute-done((bf16[1296,128]{1,0:T(8,128)(2,1)}, bf16[1296,128]{1,0:T(8,128)(2,1)}, u32[]{:S(2)}, u32[]{:S(2)}) %collective-permute-start.7) | collective-permute-done | bytes 331808 | tf_op jit(solution)/shard_map/ppermute | solution.py:639
  58.8 11.4 %collective-permute-done.4.rest_1_ = bf16[1296,128]{1,0:T(8,128)(2,1)} collective-permute-done((bf16[1296,128]{1,0:T(8,128)(2,1)}, bf16[1296,128]{1,0:T(8,128)(2,1)}, u32[]{:S(2)}, u32[]{:S(2)}) %collective-permute-start.4) | collective-permute-done | bytes 331808 | tf_op jit(solution)/shard_map/ppermute | solution.py:639
  70.3 0.0 collective-permute-done.8.rest_7_
  70.3 22.3 %scan.1 = (f32[1024,1024]{1,0:T(8,128)}, f32[4,1024,128]{2,1,0:T(8,128)}, bf16[1056,128]{1,0:T(8,128)(2,1)}, bf16[1056,128]{1,0:T(8,128)(2,1)S(1)}, f32[16,1024]{1,0:T(8,128)S(1)}, /*index=5*/f32[16,256]{1,0:T(8,128)S(1)}) custom-call(s32[16]{0:T(128)S(1)} %pad_add_fusion.1.seg, s32[1]{0:T(128)} %bitcast.2.here, bf16[1296,128]{1,0:T(8,128)(2,1)S(1)} %copy-done.2, ...), custom_call_target="tpu_custom_call" | custom-call | flops 25999998976 | bytes 16777216 | tf_op jit(solution)/shard_map/scan/pallas_call | solution.py:565
  92.6 0.0 copy-start.1
  92.6 0.7 collective-permute-start.9
  93.3 1.2 %collective-permute-start.10 = (bf16[1056,128]{1,0:T(8,128)(2,1)S(1)}, bf16[1056,128]{1,0:T(8,128)(2,1)S(1)}, u32[]{:S(2)}, u32[]{:S(2)}) collective-permute-start(bf16[1056,128]{1,0:T(8,128)(2,1)S(1)} %get-tuple-element.65), channel_id=1, source_target_pairs={{0,8},{8,16},{16,24},{24,32},{32,40},{40,48},{48,56},{56,64},{64,7... | collective-permute-start | bytes 811016 | tf_op jit(solution)/shard_map/ppermute | solution.py:633
  94.6 0.2 select_reduce_fusion.1
  94.8 4.3 %collective-permute-done.9 = bf16[1056,128]{1,0:T(8,128)(2,1)S(1)} collective-permute-done((bf16[1056,128]{1,0:T(8,128)(2,1)}, bf16[1056,128]{1,0:T(8,128)(2,1)S(1)}, u32[]{:S(2)}, u32[]{:S(2)}) %collective-permute-start.9) | collective-permute-done | bytes 270368 | tf_op jit(solution)/shard_map/ppermute | solution.py:633
  99.1 0.4 collective-permute-done.10
  99.6 0.1 select_select_fusion
  99.7 0.8 convert_dynamic-update-slice_fusion.1
  100.5 0.8 convert_dynamic-update-slice_fusion
  101.3 0.6 copy.41
  102.0 0.7 copy.40
  102.6 10.5 %all-to-all-done = bf16[8,128,1024]{2,1,0:T(8,128)(2,1)S(1)} async-done(((bf16[8,128,1024]{2,1,0:T(8,128)(2,1)}), bf16[8,128,1024]{2,1,0:T(8,128)(2,1)S(1)}, u32[]{:S(2)}, u32[]{:S(2)}) %all-to-all-start) | async-done | bytes 2097184 | tf_op jit(solution)/shard_map/all_to_all | solution.py:747
  113.1 3.6 %gate.1 = bf16[1024,1024]{1,0:T(8,128)(2,1)} custom-call(f32[1024,1024]{1,0:T(8,128)} %get-tuple-element.68.y_in, bf16[1024,1024]{1,0:T(8,128)(2,1)S(1)} %bitcast.30, f32[1,1024]{1,0:T(1,128)S(1)} %bitcast.33), custom_call_target="tpu_custom_call" | custom-call | flops 20000000 | bytes 8388608 | tf_op jit(solution)/shard_map/gate/pallas_call | solution.py:611
  (45 shorter events, 0.4 us)
Async XLA Ops:
  1.8 13.4 %copy-start.8 = (s32[128]{0:T(128)S(1)}, s32[128]{0:T(128)}, u32[]{:S(2)}) copy-start(s32[128]{0:T(128)} %param.30) | copy-start | bytes 1540
  1.8 16.6 %copy-start.5 = (f32[4,3,1024]{2,0,1:T(4,128)S(1)}, f32[4,3,1024]{2,0,1:T(4,128)}, u32[]{:S(2)}) copy-start(f32[4,3,1024]{2,0,1:T(4,128)} %param.27) | copy-start | bytes 147460
  1.8 18.0 %copy-start.6 = (f32[4,3,256]{2,0,1:T(4,128)S(1)}, f32[4,3,256]{2,0,1:T(4,128)}, u32[]{:S(2)}) copy-start(f32[4,3,256]{2,0,1:T(4,128)} %param.28) | copy-start | bytes 36868
  1.8 49.0 %collective-permute-start.6 = (bf16[1296,128]{1,0:T(8,128)(2,1)S(1)}, bf16[1296,128]{1,0:T(8,128)(2,1)S(1)}, u32[]{:S(2)}, u32[]{:S(2)}) collective-permute-start(bf16[1296,128]{1,0:T(8,128)(2,1)S(1)} %pack.3), channel_id=1, source_target_pairs={{0,4},{1,5},{2,6},{3,7},{4,0},{5,1},{6,2},{7,3},{8,12},{9,13},{10,... | collective-permute-start | bytes 995336 | tf_op jit(solution)/shard_map/ppermute | solution.py:639
  11.9 35.6 %collective-permute-start.3 = (bf16[1296,128]{1,0:T(8,128)(2,1)}, bf16[1296,128]{1,0:T(8,128)(2,1)}, u32[]{:S(2)}, u32[]{:S(2)}) collective-permute-start(bf16[1296,128]{1,0:T(8,128)(2,1)} %get-tuple-element.50), channel_id=1, source_target_pairs={{0,5},{1,6},{2,7},{3,0},{4,1},{5,2},{6,3},{7,4},{8,13},{9,14},{10,... | collective-permute-start | bytes 995336 | tf_op jit(solution)/shard_map/ppermute | solution.py:639
  12.0 35.5 %collective-permute-start.2 = (bf16[1296,128]{1,0:T(8,128)(2,1)}, bf16[1296,128]{1,0:T(8,128)(2,1)}, u32[]{:S(2)}, u32[]{:S(2)}) collective-permute-start(bf16[1296,128]{1,0:T(8,128)(2,1)} %get-tuple-element.40), channel_id=1, source_target_pairs={{0,3},{1,4},{2,5},{3,6},{4,7},{5,0},{6,1},{7,2},{8,11},{9,12},{10,... | collective-permute-start | bytes 995336 | tf_op jit(solution)/shard_map/ppermute | solution.py:639
  20.0 10.1 %copy-start.9 = (f32[16]{0:T(128)S(1)}, f32[16]{0:T(128)}, u32[]{:S(2)}) copy-start(f32[16]{0:T(128)} %param.24) | copy-start | bytes 196
  27.3 9.3 %collective-permute-start = (f32[1056,128]{1,0:T(8,128)}, f32[1056,128]{1,0:T(8,128)S(1)}, u32[]{:S(2)}, u32[]{:S(2)}) collective-permute-start(f32[1056,128]{1,0:T(8,128)} %get-tuple-element.44), channel_id=1, source_target_pairs={{0,8},{8,16},{16,24},{24,32},{32,40},{40,48},{48,56},{56,64},{64,7... | collective-permute-start | bytes 1622024 | tf_op jit(solution)/shard_map/ppermute | solution.py:633
  30.0 9.4 %collective-permute-start.1 = (f32[1056,128]{1,0:T(8,128)}, f32[1056,128]{1,0:T(8,128)}, u32[]{:S(2)}, u32[]{:S(2)}) collective-permute-start(f32[1056,128]{1,0:T(8,128)} %get-tuple-element.45), channel_id=1, source_target_pairs={{0,248},{8,0},{16,8},{24,16},{32,24},{40,32},{48,40},{56,48},{64,5... | collective-permute-start | bytes 1622024 | tf_op jit(solution)/shard_map/ppermute | solution.py:633
  30.2 3.3 %copy-start.7 = (s32[128]{0:T(128)S(1)}, s32[128]{0:T(128)}, u32[]{:S(2)}) copy-start(s32[128]{0:T(128)} %param.31) | copy-start | bytes 1540
  30.2 3.5 %copy-start.12 = (s32[128]{0:T(128)S(1)}, s32[128]{0:T(128)}, u32[]{:S(2)}) copy-start(s32[128]{0:T(128)} %param.29) | copy-start | bytes 1540
  30.2 14.0 %copy-start = (f32[4,16,64,128]{3,2,1,0:T(8,128)S(1)}, f32[4,16,64,128]{3,2,1,0:T(8,128)}, u32[]{:S(2)}) copy-start(f32[4,16,64,128]{3,2,1,0:T(8,128)} %param.26) | copy-start | bytes 6291460
  40.5 16.7 %collective-permute-start.5 = (bf16[1296,128]{1,0:T(8,128)(2,1)}, bf16[1296,128]{1,0:T(8,128)(2,1)}, u32[]{:S(2)}, u32[]{:S(2)}) collective-permute-start(bf16[1296,128]{1,0:T(8,128)(2,1)} %get-tuple-element.53), channel_id=1, source_target_pairs={{0,2},{1,3},{2,4},{3,5},{4,6},{5,7},{6,0},{7,1},{8,10},{9,11},{10,... | collective-permute-start | bytes 995336 | tf_op jit(solution)/shard_map/ppermute | solution.py:639
  42.9 15.9 %collective-permute-start.7 = (bf16[1296,128]{1,0:T(8,128)(2,1)}, bf16[1296,128]{1,0:T(8,128)(2,1)}, u32[]{:S(2)}, u32[]{:S(2)}) collective-permute-start(bf16[1296,128]{1,0:T(8,128)(2,1)} %get-tuple-element.55), channel_id=1, source_target_pairs={{0,6},{1,7},{2,0},{3,1},{4,2},{5,3},{6,4},{7,5},{8,14},{9,15},{10,... | collective-permute-start | bytes 995336 | tf_op jit(solution)/shard_map/ppermute | solution.py:639
  44.1 6.7 %copy-start.10 = (f32[16]{0:T(128)S(1)}, f32[16]{0:T(128)}, u32[]{:S(2)}) copy-start(f32[16]{0:T(128)} %param.22) | copy-start | bytes 196
  44.2 6.8 %copy-start.11 = (f32[16]{0:T(128)S(1)}, f32[16]{0:T(128)}, u32[]{:S(2)}) copy-start(f32[16]{0:T(128)} %param.23) | copy-start | bytes 196
  47.4 22.8 %collective-permute-start.4 = (bf16[1296,128]{1,0:T(8,128)(2,1)}, bf16[1296,128]{1,0:T(8,128)(2,1)}, u32[]{:S(2)}, u32[]{:S(2)}) collective-permute-start(bf16[1296,128]{1,0:T(8,128)(2,1)} %get-tuple-element.51), channel_id=1, source_target_pairs={{0,1},{1,2},{2,3},{3,4},{4,5},{5,6},{6,7},{7,0},{8,9},{9,10},{10,1... | collective-permute-start | bytes 995336 | tf_op jit(solution)/shard_map/ppermute | solution.py:639
  49.4 20.9 %collective-permute-start.8 = (bf16[1296,128]{1,0:T(8,128)(2,1)}, bf16[1296,128]{1,0:T(8,128)(2,1)}, u32[]{:S(2)}, u32[]{:S(2)}) collective-permute-start(bf16[1296,128]{1,0:T(8,128)(2,1)} %get-tuple-element.57), channel_id=1, source_target_pairs={{0,7},{1,0},{2,1},{3,2},{4,3},{5,4},{6,5},{7,6},{8,15},{9,8},{10,9... | collective-permute-start | bytes 995336 | tf_op jit(solution)/shard_map/ppermute | solution.py:639
  51.0 19.3 %copy-start.2 = (bf16[1296,128]{1,0:T(8,128)(2,1)S(1)}, bf16[1296,128]{1,0:T(8,128)(2,1)}, u32[]{:S(2)}) copy-start(bf16[1296,128]{1,0:T(8,128)(2,1)} %get-tuple-element.42.rest_0_) | copy-start | bytes 995332
  51.0 19.3 %copy-start.3 = (f32[5,1024]{1,0:T(8,128)S(1)}, f32[5,1024]{1,0:T(8,128)}, u32[]{:S(2)}) copy-start(f32[5,1024]{1,0:T(8,128)} %rest_10_.1) | copy-start | bytes 61444
  51.0 19.3 %copy-start.4 = (f32[5,256]{1,0:T(8,128)S(1)}, f32[5,256]{1,0:T(8,128)}, u32[]{:S(2)}) copy-start(f32[5,256]{1,0:T(8,128)} %rest_12_.1) | copy-start | bytes 15364
  51.0 62.1 %all-to-all-start = ((bf16[8,128,1024]{2,1,0:T(8,128)(2,1)}), bf16[8,128,1024]{2,1,0:T(8,128)(2,1)S(1)}, u32[]{:S(2)}, u32[]{:S(2)}) async-start(bf16[8,128,1024]{2,1,0:T(8,128)(2,1)} %bitcast.34), calls=%async_computation | async-start | bytes 4194304 | tf_op jit(solution)/shard_map/all_to_all | solution.py:747
  92.6 20.5 %copy-start.1 = (f32[1024]{0:T(1024)S(1)}, f32[1024]{0:T(1024)}, u32[]{:S(2)}) copy-start(f32[1024]{0:T(1024)} %param.25) | copy-start | bytes 12292
  92.6 6.5 %collective-permute-start.9 = (bf16[1056,128]{1,0:T(8,128)(2,1)}, bf16[1056,128]{1,0:T(8,128)(2,1)S(1)}, u32[]{:S(2)}, u32[]{:S(2)}) collective-permute-start(bf16[1056,128]{1,0:T(8,128)(2,1)} %get-tuple-element.64), channel_id=1, source_target_pairs={{0,248},{8,0},{16,8},{24,16},{32,24},{40,32},{48,40},{56,48},{64,5... | collective-permute-start | bytes 811016 | tf_op jit(solution)/shard_map/ppermute | solution.py:633
  93.3 6.2 %collective-permute-start.10 = (bf16[1056,128]{1,0:T(8,128)(2,1)S(1)}, bf16[1056,128]{1,0:T(8,128)(2,1)S(1)}, u32[]{:S(2)}, u32[]{:S(2)}) collective-permute-start(bf16[1056,128]{1,0:T(8,128)(2,1)S(1)} %get-tuple-element.65), channel_id=1, source_target_pairs={{0,8},{8,16},{16,24},{24,32},{32,40},{40,48},{48,56},{56,64},{64,7... | collective-permute-start | bytes 811016 | tf_op jit(solution)/shard_map/ppermute | solution.py:633

commit v5 on v4

--- a/solution.py
+++ b/solution.py
@@ -29,7 +29,8 @@
 DT_ROW = BC_ROW + BC_TILES * SRC_ROWS
 BLOCK_ROWS = DT_ROW + GH
 MOVER_ROWS = GC + 32
-GATE_ROWS = 256
+GATE_ROWS = 128
+HEAD_ROWS = 128
 ORDER = (4, 3, 5, 2, 6, 1, 7)
 FIRST = (4, 3, 5)
 SECOND = (2, 6)
@@ -292,8 +293,8 @@
 def scan_kernel(seg, here, *rest):
     blocks, rest = rest[:TENSOR], rest[TENSOR:]
     conv_x, conv_bc, x_param, skip, bc_param, rate, bias, init = rest[:8]
-    y_out, own_out, lft_out, rgt_out, last_x, last_bc = rest[8:14]
-    prep_out, prep_scratch, scratch = rest[14:20], rest[20:25], rest[25:]
+    y_head, y_out, own_out, lft_out, rgt_out, last_x, last_bc = rest[8:15]
+    prep_out, prep_scratch, scratch = rest[15:21], rest[21:26], rest[26:]
     x_rows, x_sems = scratch[7], scratch[9]
     loads = [pltpu.make_async_copy(init, scratch[3], x_sems.at[TENSOR * TILES])]
     for d in range(TENSOR):
@@ -309,7 +310,7 @@
         copy.wait()
 
     main_body(
-        seg, conv_x, x_param, skip, *prep_out, last_bc, y_out, own_out, lft_out, rgt_out,
+        seg, conv_x, x_param, skip, *prep_out, last_bc, y_head, y_out, own_out, lft_out, rgt_out,
         last_x, *scratch
     )
 
@@ -326,6 +327,7 @@
     row_in,
     dec_in,
     last_bc,
+    y_head,
     y_out,
     own_out,
     lft_out,
@@ -428,6 +430,10 @@
                 y_stage[pl.ds(r0 + 128 * half, 128), lanes] = total
         store(c).start()
 
+        @pl.when(c == 0)
+        def _():
+            y_head[...] = y_stage[0:HEAD_ROWS, :]
+
     def send_back(k, out):
         for b in range(GC // 128):
             part = slice(128 * b, 128 * (b + 1))
@@ -465,7 +471,9 @@
         store(c).wait()
 
 
-def gate_kernel(y_in, z_in, gain, out, y_stage, stage, load_sems, sems):
+def gate_kernel(y_head, y_in, z_in, gain, out, y_stage, stage, load_sems, sems):
+    head, count = HEAD_ROWS // GATE_ROWS, ROWS // GATE_ROWS
+
     def rows_of(i):
         return pl.ds(pl.multiple_of(i * GATE_ROWS, GATE_ROWS), GATE_ROWS)
 
@@ -477,20 +485,27 @@
     def store(i):
         return pltpu.make_async_copy(stage.at[rows_of(i), :], out.at[rows_of(i), :], sems.at[i])
 
-    for i in range(ROWS // GATE_ROWS):
-        load(i).start()
-
-    @pl.loop(0, ROWS // GATE_ROWS)
-    def _(i):
-        load(i).wait()
+    def gate_rows(i, y_ref):
         for part in range(GATE_ROWS // 16):
             rows = pl.ds(pl.multiple_of(i * GATE_ROWS + 16 * part, 16), 16)
-            gated = y_stage[rows, :] * silu(z_in[rows, :].astype(F32))
+            gated = y_ref[rows, :] * silu(z_in[rows, :].astype(F32))
             mean = jnp.sum(gated * gated, axis=1, keepdims=True) * (1.0 / GC)
             stage[rows, :] = (gated * lax.rsqrt(mean + EPSILON) * gain[...]).astype(BF16)
         store(i).start()
 
-    @pl.loop(0, ROWS // GATE_ROWS)
+    for i in range(head, count):
+        load(i).start()
+
+    @pl.loop(0, head)
+    def _(i):
+        gate_rows(i, y_head)
+
+    @pl.loop(head, count)
+    def _(i):
+        load(i).wait()
+        gate_rows(i, y_stage)
+
+    @pl.loop(0, count)
     def _(i):
         store(i).wait()
 
@@ -565,6 +580,7 @@
     return pl.pallas_call(
         scan_kernel,
         out_shape=(
+            jax.ShapeDtypeStruct((HEAD_ROWS, GC), F32),
             pltpu.HBM((ROWS, GC), F32),
             jax.ShapeDtypeStruct((SLOTS, GC, STATE), F32),
             jax.ShapeDtypeStruct((MOVER_ROWS, STATE), BF16),
@@ -573,7 +589,7 @@
             jax.ShapeDtypeStruct((16, 2 * STATE), F32),
         ),
         in_specs=[SMEM, SMEM] + [ANY] * TENSOR + [VMEM] * (len(operands) - 1) + [HBM],
-        out_specs=(HBM,) + (VMEM,) * 5,
+        out_specs=(VMEM, HBM) + (VMEM,) * 5,
         scratch_shapes=[
             pltpu.VMEM((CHUNKS, STATE, Q), BF16),
             pltpu.VMEM((ROWS, STATE), BF16),
@@ -607,11 +623,11 @@
     )(seg, here, *blocks, *operands)
 
 
-def gate(y, z_rows, gain):
+def gate(y_head, y, z_rows, gain):
     return pl.pallas_call(
         gate_kernel,
         out_shape=jax.ShapeDtypeStruct((ROWS, GC), BF16),
-        in_specs=[HBM, VMEM, VMEM],
+        in_specs=[VMEM, HBM, VMEM, VMEM],
         out_specs=ANY,
         scratch_shapes=[
             pltpu.VMEM((ROWS, GC), F32),
@@ -624,7 +640,7 @@
             flops=20_000_000, bytes_accessed=8 * MIB, transcendentals=1_000_000
         ),
         name="gate",
-    )(in_hbm(y), z_rows, gain)
+    )(y_head, in_hbm(y), z_rows, gain)
 
 
 def shifted(value, steps):
@@ -717,7 +733,7 @@
     from_left = shifted(move_right, 1)
     from_right = shifted(move_left, -1)
     for d in SECOND:
-        blocks[d] = rotated(after(packed[d], from_left, from_right), d)
+        blocks[d] = rotated(packed[d], d)
 
     def small_of(packed):
         return packed[GC : GC + lines].reshape(1, 3, width)
@@ -748,7 +764,7 @@
     z_rows = z_rows.reshape(ROWS, GC)
 
     in_order = [blocks[d] for d in range(TENSOR)]
-    y, own_new, back_left, back_right, last_x, last_bc = scan(
+    y_head, y, own_new, back_left, back_right, last_x, last_bc = scan(
         seg,
         here_ref,
         in_order,
@@ -778,7 +794,7 @@
     new_cx, new_cbc = new_conv[:, :, :GC], new_conv[:, :, GC:]
 
     y, new_ssm, new_cx, new_cbc = lax.optimization_barrier((y, new_ssm, new_cx, new_cbc))
-    y_out = gate(y, z_rows, gain)
+    y_out = gate(y_head, y, z_rows, gain)
     return y_out, new_ssm.reshape(ssm_state.shape), new_cx, new_cbc
 
 

time: 117 us -> 116 us (level)
  the two profiles are of different devices: /device:TPU:1 before, /device:TPU:36 now
where the time goes in v5:
time: 116 us; the launch traced here: 115 us
  Pallas kernels  38.5 us (33%)
  starting transfers between devices  33.2 us (29%)
  waiting for transfers between devices  25.8 us (22%)
  local copies, waits for them, and re-layouts  6.78 us (6%)
  other arithmetic  5.92 us (5%)
  between operations  5.07 us (4%)
    ppermute x7, starting transfers between devices, rotated(): return lax.ppermute(value, 'tensor', pairs)  23.2 us
    pallas_call x1, Pallas kernels, scan(): pl.pallas_call(scan_kernel, out_shape=(jax.ShapeDtypeStruct((HEAD_ROWS, G...  22.3 us
    ppermute x7, waiting for transfers between devices, rotated(): return lax.ppermute(value, 'tensor', pairs)  9.89 us
    ppermute x4, waiting for transfers between devices, shifted(): return lax.ppermute(value, 'dp', pairs)  8.01 us
    all_to_all x1, waiting for transfers between devices, shards(): lax.all_to_all(z_sent, 'tensor', split_axis=0, concat_axis=0, tiled=True)  7.87 us
    all_to_all x1, starting transfers between devices, shards(): lax.all_to_all(z_sent, 'tensor', split_axis=0, concat_axis=0, tiled=True)  7.54 us
    pallas_call x3, Pallas kernels, pack(): pl.pallas_call(functools.partial(pack_kernel, offsets), out_shape=(jax.Sh...  6.59 us
    pallas_call x1, Pallas kernels, gate(): pl.pallas_call(gate_kernel, out_shape=jax.ShapeDtypeStruct((ROWS, GC), BF...  3.54 us
  transfers between devices with their start and end apart: 12, of which 5 were waited for; matrix products, arithmetic and copies ran while one was open for 10% of the time, Pallas kernels for 29%

profile of v5, /device:TPU:36, one launch (start us, length us, event | category | flops | bytes accessed | tf_op | source)
XLA Modules:
  0.0 115.2 jit_solution(14480447274499623803)
XLA Ops:
  0.6 1.1 pack.3
  1.8 0.0 copy-start.9
  1.8 0.0 copy-start.6
  1.8 0.0 copy-start.7
  1.8 6.4 %collective-permute-start.6 = (bf16[1296,128]{1,0:T(8,128)(2,1)S(1)}, bf16[1296,128]{1,0:T(8,128)(2,1)}, u32[]{:S(2)}, u32[]{:S(2)}) collective-permute-start(bf16[1296,128]{1,0:T(8,128)(2,1)S(1)} %pack.3), channel_id=1, source_target_pairs={{0,4},{1,5},{2,6},{3,7},{4,0},{5,1},{6,2},{7,3},{8,12},{9,13},{10,... | collective-permute-start | bytes 995336 | tf_op jit(solution)/shard_map/ppermute | solution.py:655
  8.2 2.2 %pack.4 = (bf16[1296,128]{1,0:T(8,128)(2,1)}, bf16[1296,128]{1,0:T(8,128)(2,1)}) custom-call(s32[1]{0:T(128)} %bitcast.2.here, bf16[128,8192]{1,0:T(8,128)(2,1)} %x.11, bf16[128,2048]{1,0:T(8,128)(2,1)} %bc.5, bf16[128,128]{1,0:T(8,128)(2,1)} %dt.5), custom_call_target="tpu_custom_call" | custom-call | tf_op jit(solution)/shard_map/pack/pallas_call | solution.py:529
  10.4 0.2 collective-permute-start.3
  10.6 4.9 %collective-permute-start.2 = (bf16[1296,128]{1,0:T(8,128)(2,1)}, bf16[1296,128]{1,0:T(8,128)(2,1)}, u32[]{:S(2)}, u32[]{:S(2)}) collective-permute-start(bf16[1296,128]{1,0:T(8,128)(2,1)} %get-tuple-element.39), channel_id=1, source_target_pairs={{0,3},{1,4},{2,5},{3,6},{4,7},{5,0},{6,1},{7,2},{8,11},{9,12},{10,... | collective-permute-start | bytes 995336 | tf_op jit(solution)/shard_map/ppermute | solution.py:655
  15.6 0.0 copy-done.9
  15.6 0.6 fusion.2
  18.8 0.0 copy-done.6
  20.1 0.1 dynamic-slice_reduce_fusion.1
  20.3 0.0 copy-start.10
  20.3 3.2 %pack.5 = (bf16[1296,128]{1,0:T(8,128)(2,1)}, bf16[1296,128]{1,0:T(8,128)(2,1)}, bf16[1296,128]{1,0:T(8,128)(2,1)}, bf16[1296,128]{1,0:T(8,128)(2,1)}, bf16[1296,128]{1,0:T(8,128)(2,1)}) custom-call(s32[1]{0:T(128)} %bitcast.2.here, bf16[128,8192]{1,0:T(8,128)(2,1)} %x.11, bf16[128,2048]{1,0:T(8,128)(2,1)} %bc.5, bf16[128,128]{1,0:T(8,128)(2,1)} %dt.5), custom_call_target="tpu_custom_call" | custom-call | tf_op jit(solution)/shard_map/pack/pallas_call | solution.py:529
  23.5 1.4 %pad_add_fusion.slots = s32[2]{0:T(128)S(1)} fusion(s32[1]{0:T(128)} %bitcast.1, s32[1]{0:T(128)} %bitcast), kind=kLoop, calls=%fused_computation.36 | loop fusion | flops 2 | bytes 16 | tf_op jit(solution)/shard_map/stack | solution.py:729
  24.9 2.7 %movers.1 = (f32[1056,128]{1,0:T(8,128)}, f32[1056,128]{1,0:T(8,128)}) custom-call(s32[2]{0:T(128)S(1)} %pad_add_fusion.slots, f32[4,1024,128]{2,1,0:T(8,128)} %bitcast.31, f32[2,32,128]{2,1,0:T(8,128)S(1)} %pad_maximum_fusion.2.small), custom_call_target="tpu_custom_call" | custom-call | tf_op jit(solution)/shard_map/movers/pallas_call | solution.py:554
  27.6 0.1 collective-permute-start
  27.7 1.7 %collective-permute-start.1 = (f32[1056,128]{1,0:T(8,128)}, f32[1056,128]{1,0:T(8,128)}, u32[]{:S(2)}, u32[]{:S(2)}) collective-permute-start(f32[1056,128]{1,0:T(8,128)} %get-tuple-element.44), channel_id=1, source_target_pairs={{0,248},{8,0},{16,8},{24,16},{32,24},{40,32},{48,40},{56,48},{64,5... | collective-permute-start | bytes 1622024 | tf_op jit(solution)/shard_map/ppermute | solution.py:649
  29.5 0.1 broadcast_in_dim.158
  29.5 0.1 broadcast_in_dim_reshape.4.rest_11_
  29.6 3.3 %copy.44 = bf16[16,8,8,1024]{3,2,0,1:T(8,128)(2,1)} copy(bf16[16,8,8,1024]{3,2,1,0:T(8,128)(2,1)} %bitcast.35) | data formatting | bytes 4194304 | tf_op jit(solution)/shard_map/reshape | solution.py:746
  32.9 0.2 convert_reduce_fusion
  33.1 0.1 select_reduce_fusion.2
  33.3 0.7 iota_compare_fusion.3
  34.0 0.1 pad_add_fusion.1.seg
  34.1 2.7 %collective-permute-done.lft = f32[1056,128]{1,0:T(8,128)S(1)} collective-permute-done((f32[1056,128]{1,0:T(8,128)}, f32[1056,128]{1,0:T(8,128)S(1)}, u32[]{:S(2)}, u32[]{:S(2)}) %collective-permute-start) | collective-permute-done | bytes 540704 | tf_op jit(solution)/shard_map/ppermute | solution.py:649
  36.7 1.5 %collective-permute-start.5 = (bf16[1296,128]{1,0:T(8,128)(2,1)}, bf16[1296,128]{1,0:T(8,128)(2,1)}, u32[]{:S(2)}, u32[]{:S(2)}) collective-permute-start(bf16[1296,128]{1,0:T(8,128)(2,1)} %get-tuple-element.51), channel_id=1, source_target_pairs={{0,2},{1,3},{2,4},{3,5},{4,6},{5,7},{6,0},{7,1},{8,10},{9,11},{10,... | collective-permute-start | bytes 995336 | tf_op jit(solution)/shard_map/ppermute | solution.py:655
  38.2 0.0 collective-permute-done.1.rgt
  38.2 2.7 %collective-permute-start.7 = (bf16[1296,128]{1,0:T(8,128)(2,1)}, bf16[1296,128]{1,0:T(8,128)(2,1)}, u32[]{:S(2)}, u32[]{:S(2)}) collective-permute-start(bf16[1296,128]{1,0:T(8,128)(2,1)} %get-tuple-element.52), channel_id=1, source_target_pairs={{0,6},{1,7},{2,0},{3,1},{4,2},{5,3},{6,4},{7,5},{8,14},{9,15},{10,... | collective-permute-start | bytes 995336 | tf_op jit(solution)/shard_map/ppermute | solution.py:655
  41.0 0.7 slice.45
  41.8 0.1 copy.34
  41.8 0.2 select_reduce_fusion
  42.1 0.0 copy-start.11
  42.1 0.0 copy-start.12
  42.1 3.3 %initial.1.rest_15_ = f32[4,128,1024]{2,1,0:T(8,128)} custom-call(s32[16]{0:T(128)S(1)} %pad_add_fusion.1.seg, f32[4,1024,128]{2,1,0:T(8,128)S(1)} %bitcast.32, f32[1056,128]{1,0:T(8,128)S(1)} %collective-permute-done.lft, f32[1056,128]{1,0:T(8,128)} %collective-permute-done.1.rgt), custom_call_target="tpu_custom_call" | custom-call | flops 2000000000 | bytes 4194304 | tf_op jit(solution)/shard_map/initial/pallas_call | solution.py:566
  45.3 0.0 collective-permute-done.3.rest_5_
  45.4 0.0 collective-permute-done.2.rest_3_
  45.4 0.0 collective-permute-start.4
  45.4 7.5 %collective-permute-start.8 = (bf16[1296,128]{1,0:T(8,128)(2,1)}, bf16[1296,128]{1,0:T(8,128)(2,1)}, u32[]{:S(2)}, u32[]{:S(2)}) collective-permute-start(bf16[1296,128]{1,0:T(8,128)(2,1)} %get-tuple-element.54), channel_id=1, source_target_pairs={{0,7},{1,0},{2,1},{3,2},{4,3},{5,4},{6,5},{7,6},{8,15},{9,8},{10,9... | collective-permute-start | bytes 995336 | tf_op jit(solution)/shard_map/ppermute | solution.py:655
  52.9 0.6 iota_compare_fusion.4
  53.6 0.0 collective-permute-done.6.rest_4_
  53.6 0.1 copy.37.rest_13_
  53.7 0.0 copy-done.12
  53.7 0.1 copy.38.rest_14_
  53.8 7.5 %all-to-all-start = ((bf16[8,128,1024]{2,1,0:T(8,128)(2,1)}), bf16[8,128,1024]{2,1,0:T(8,128)(2,1)S(1)}, u32[]{:S(2)}, u32[]{:S(2)}) async-start(bf16[8,128,1024]{2,1,0:T(8,128)(2,1)} %bitcast.34), calls=%async_computation | async-start | bytes 4194304 | tf_op jit(solution)/shard_map/all_to_all | solution.py:763
  61.3 0.0 collective-permute-done.5.rest_2_
  61.3 0.0 collective-permute-done.7.rest_6_
  61.3 9.9 %collective-permute-done.4.rest_1_ = bf16[1296,128]{1,0:T(8,128)(2,1)S(1)} collective-permute-done((bf16[1296,128]{1,0:T(8,128)(2,1)}, bf16[1296,128]{1,0:T(8,128)(2,1)S(1)}, u32[]{:S(2)}, u32[]{:S(2)}) %collective-permute-start.4) | collective-permute-done | bytes 331808 | tf_op jit(solution)/shard_map/ppermute | solution.py:655
  71.2 0.0 collective-permute-done.8.rest_7_
  71.2 22.3 %scan.1 = (f32[128,1024]{1,0:T(8,128)S(1)}, f32[1024,1024]{1,0:T(8,128)}, f32[4,1024,128]{2,1,0:T(8,128)}, bf16[1056,128]{1,0:T(8,128)(2,1)}, bf16[1056,128]{1,0...) custom-call(s32[16]{0:T(128)S(1)} %pad_add_fusion.1.seg, s32[1]{0:T(128)} %bitcast.2.here, ...), custom_call_target="tpu_custom_call" | custom-call | flops 25999998976 | bytes 16777216 | tf_op jit(solution)/shard_map/scan/pallas_call | solution.py:580
  93.6 0.0 copy-start.3
  93.6 0.7 copy-done.3
  94.3 0.0 collective-permute-start.9
  94.4 0.6 collective-permute-start.10
  94.9 0.2 select_reduce_fusion.1
  95.2 3.4 %collective-permute-done.9 = bf16[1056,128]{1,0:T(8,128)(2,1)S(1)} collective-permute-done((bf16[1056,128]{1,0:T(8,128)(2,1)}, bf16[1056,128]{1,0:T(8,128)(2,1)S(1)}, u32[]{:S(2)}, u32[]{:S(2)}) %collective-permute-start.9) | collective-permute-done | bytes 270368 | tf_op jit(solution)/shard_map/ppermute | solution.py:649
  98.6 1.9 %collective-permute-done.10 = bf16[1056,128]{1,0:T(8,128)(2,1)S(1)} collective-permute-done((bf16[1056,128]{1,0:T(8,128)(2,1)}, bf16[1056,128]{1,0:T(8,128)(2,1)S(1)}, u32[]{:S(2)}, u32[]{:S(2)}) %collective-permute-start.10) | collective-permute-done | bytes 270368 | tf_op jit(solution)/shard_map/ppermute | solution.py:649
  100.5 0.1 select_select_fusion
  100.7 0.8 convert_dynamic-update-slice_fusion.1
  101.5 0.8 convert_dynamic-update-slice_fusion
  102.3 0.6 copy.41
  102.9 0.7 copy.40
  103.6 7.9 %all-to-all-done = bf16[8,128,1024]{2,1,0:T(8,128)(2,1)S(1)} async-done(((bf16[8,128,1024]{2,1,0:T(8,128)(2,1)}), bf16[8,128,1024]{2,1,0:T(8,128)(2,1)S(1)}, u32[]{:S(2)}, u32[]{:S(2)}) %all-to-all-start) | async-done | bytes 2097184 | tf_op jit(solution)/shard_map/all_to_all | solution.py:763
  111.5 3.5 %gate.1 = bf16[1024,1024]{1,0:T(8,128)(2,1)} custom-call(f32[128,1024]{1,0:T(8,128)S(1)} %get-tuple-element.59.y_head, f32[1024,1024]{1,0:T(8,128)} %get-tuple-element.66.y_in, bf16[1024,1024]{1,0:T(8,128)(2,1)S(1)} %bitcast.30, f32[1,1024]{1,0:T(1,128)S(1)} %bitcast.33), custom_call_target="tpu_custom_call" | custom-call | flops 20000000 | bytes 8388608 | tf_op jit(solution)/shard_map/gate/pallas_call | solution.py:627
  (47 shorter events, 0.4 us)
Async XLA Ops:
  1.8 13.8 %copy-start.9 = (s32[128]{0:T(128)S(1)}, s32[128]{0:T(128)}, u32[]{:S(2)}) copy-start(s32[128]{0:T(128)} %param.30) | copy-start | bytes 1540
  1.8 17.0 %copy-start.6 = (f32[4,3,1024]{2,0,1:T(4,128)S(1)}, f32[4,3,1024]{2,0,1:T(4,128)}, u32[]{:S(2)}) copy-start(f32[4,3,1024]{2,0,1:T(4,128)} %param.27) | copy-start | bytes 147460
  1.8 18.3 %copy-start.7 = (f32[4,3,256]{2,0,1:T(4,128)S(1)}, f32[4,3,256]{2,0,1:T(4,128)}, u32[]{:S(2)}) copy-start(f32[4,3,256]{2,0,1:T(4,128)} %param.28) | copy-start | bytes 36868
  1.8 51.8 %collective-permute-start.6 = (bf16[1296,128]{1,0:T(8,128)(2,1)S(1)}, bf16[1296,128]{1,0:T(8,128)(2,1)}, u32[]{:S(2)}, u32[]{:S(2)}) collective-permute-start(bf16[1296,128]{1,0:T(8,128)(2,1)S(1)} %pack.3), channel_id=1, source_target_pairs={{0,4},{1,5},{2,6},{3,7},{4,0},{5,1},{6,2},{7,3},{8,12},{9,13},{10,... | collective-permute-start | bytes 995336 | tf_op jit(solution)/shard_map/ppermute | solution.py:655
  10.4 34.9 %collective-permute-start.3 = (bf16[1296,128]{1,0:T(8,128)(2,1)}, bf16[1296,128]{1,0:T(8,128)(2,1)}, u32[]{:S(2)}, u32[]{:S(2)}) collective-permute-start(bf16[1296,128]{1,0:T(8,128)(2,1)} %get-tuple-element.49), channel_id=1, source_target_pairs={{0,5},{1,6},{2,7},{3,0},{4,1},{5,2},{6,3},{7,4},{8,13},{9,14},{10,... | collective-permute-start | bytes 995336 | tf_op jit(solution)/shard_map/ppermute | solution.py:655
  10.6 34.7 %collective-permute-start.2 = (bf16[1296,128]{1,0:T(8,128)(2,1)}, bf16[1296,128]{1,0:T(8,128)(2,1)}, u32[]{:S(2)}, u32[]{:S(2)}) collective-permute-start(bf16[1296,128]{1,0:T(8,128)(2,1)} %get-tuple-element.39), channel_id=1, source_target_pairs={{0,3},{1,4},{2,5},{3,6},{4,7},{5,0},{6,1},{7,2},{8,11},{9,12},{10,... | collective-permute-start | bytes 995336 | tf_op jit(solution)/shard_map/ppermute | solution.py:655
  20.3 9.2 %copy-start.10 = (f32[16]{0:T(128)S(1)}, f32[16]{0:T(128)}, u32[]{:S(2)}) copy-start(f32[16]{0:T(128)} %param.24) | copy-start | bytes 196
  27.6 9.1 %collective-permute-start = (f32[1056,128]{1,0:T(8,128)}, f32[1056,128]{1,0:T(8,128)S(1)}, u32[]{:S(2)}, u32[]{:S(2)}) collective-permute-start(f32[1056,128]{1,0:T(8,128)} %get-tuple-element.43), channel_id=1, source_target_pairs={{0,8},{8,16},{16,24},{24,32},{32,40},{40,48},{48,56},{56,64},{64,7... | collective-permute-start | bytes 1622024 | tf_op jit(solution)/shard_map/ppermute | solution.py:649
  27.7 10.5 %collective-permute-start.1 = (f32[1056,128]{1,0:T(8,128)}, f32[1056,128]{1,0:T(8,128)}, u32[]{:S(2)}, u32[]{:S(2)}) collective-permute-start(f32[1056,128]{1,0:T(8,128)} %get-tuple-element.44), channel_id=1, source_target_pairs={{0,248},{8,0},{16,8},{24,16},{32,24},{40,32},{48,40},{56,48},{64,5... | collective-permute-start | bytes 1622024 | tf_op jit(solution)/shard_map/ppermute | solution.py:649
  29.6 3.3 %copy-start.8 = (s32[128]{0:T(128)S(1)}, s32[128]{0:T(128)}, u32[]{:S(2)}) copy-start(s32[128]{0:T(128)} %param.31) | copy-start | bytes 1540
  29.6 3.5 %copy-start.13 = (s32[128]{0:T(128)S(1)}, s32[128]{0:T(128)}, u32[]{:S(2)}) copy-start(s32[128]{0:T(128)} %param.29) | copy-start | bytes 1540
  29.6 12.4 %copy-start = (f32[4,16,64,128]{3,2,1,0:T(8,128)S(1)}, f32[4,16,64,128]{3,2,1,0:T(8,128)}, u32[]{:S(2)}) copy-start(f32[4,16,64,128]{3,2,1,0:T(8,128)} %param.26) | copy-start | bytes 6291460
  36.7 24.6 %collective-permute-start.5 = (bf16[1296,128]{1,0:T(8,128)(2,1)}, bf16[1296,128]{1,0:T(8,128)(2,1)}, u32[]{:S(2)}, u32[]{:S(2)}) collective-permute-start(bf16[1296,128]{1,0:T(8,128)(2,1)} %get-tuple-element.51), channel_id=1, source_target_pairs={{0,2},{1,3},{2,4},{3,5},{4,6},{5,7},{6,0},{7,1},{8,10},{9,11},{10,... | collective-permute-start | bytes 995336 | tf_op jit(solution)/shard_map/ppermute | solution.py:655
  38.2 23.1 %collective-permute-start.7 = (bf16[1296,128]{1,0:T(8,128)(2,1)}, bf16[1296,128]{1,0:T(8,128)(2,1)}, u32[]{:S(2)}, u32[]{:S(2)}) collective-permute-start(bf16[1296,128]{1,0:T(8,128)(2,1)} %get-tuple-element.52), channel_id=1, source_target_pairs={{0,6},{1,7},{2,0},{3,1},{4,2},{5,3},{6,4},{7,5},{8,14},{9,15},{10,... | collective-permute-start | bytes 995336 | tf_op jit(solution)/shard_map/ppermute | solution.py:655
  42.1 11.5 %copy-start.11 = (f32[16]{0:T(128)S(1)}, f32[16]{0:T(128)}, u32[]{:S(2)}) copy-start(f32[16]{0:T(128)} %param.22) | copy-start | bytes 196
  42.1 11.6 %copy-start.12 = (f32[16]{0:T(128)S(1)}, f32[16]{0:T(128)}, u32[]{:S(2)}) copy-start(f32[16]{0:T(128)} %param.23) | copy-start | bytes 196
  45.4 25.9 %collective-permute-start.4 = (bf16[1296,128]{1,0:T(8,128)(2,1)}, bf16[1296,128]{1,0:T(8,128)(2,1)S(1)}, u32[]{:S(2)}, u32[]{:S(2)}) collective-permute-start(bf16[1296,128]{1,0:T(8,128)(2,1)} %get-tuple-element.50), channel_id=1, source_target_pairs={{0,1},{1,2},{2,3},{3,4},{4,5},{5,6},{6,7},{7,0},{8,9},{9,10},{10,1... | collective-permute-start | bytes 995336 | tf_op jit(solution)/shard_map/ppermute | solution.py:655
  45.4 25.8 %collective-permute-start.8 = (bf16[1296,128]{1,0:T(8,128)(2,1)}, bf16[1296,128]{1,0:T(8,128)(2,1)}, u32[]{:S(2)}, u32[]{:S(2)}) collective-permute-start(bf16[1296,128]{1,0:T(8,128)(2,1)} %get-tuple-element.54), channel_id=1, source_target_pairs={{0,7},{1,0},{2,1},{3,2},{4,3},{5,4},{6,5},{7,6},{8,15},{9,8},{10,9... | collective-permute-start | bytes 995336 | tf_op jit(solution)/shard_map/ppermute | solution.py:655
  53.8 17.4 %copy-start.2 = (bf16[1296,128]{1,0:T(8,128)(2,1)S(1)}, bf16[1296,128]{1,0:T(8,128)(2,1)}, u32[]{:S(2)}) copy-start(bf16[1296,128]{1,0:T(8,128)(2,1)} %get-tuple-element.41.rest_0_) | copy-start | bytes 995332
  53.8 17.4 %copy-start.4 = (f32[5,1024]{1,0:T(8,128)S(1)}, f32[5,1024]{1,0:T(8,128)}, u32[]{:S(2)}) copy-start(f32[5,1024]{1,0:T(8,128)} %rest_10_.1) | copy-start | bytes 61444
  53.8 17.4 %copy-start.5 = (f32[5,256]{1,0:T(8,128)S(1)}, f32[5,256]{1,0:T(8,128)}, u32[]{:S(2)}) copy-start(f32[5,256]{1,0:T(8,128)} %rest_12_.1) | copy-start | bytes 15364
  53.8 57.7 %all-to-all-start = ((bf16[8,128,1024]{2,1,0:T(8,128)(2,1)}), bf16[8,128,1024]{2,1,0:T(8,128)(2,1)S(1)}, u32[]{:S(2)}, u32[]{:S(2)}) async-start(bf16[8,128,1024]{2,1,0:T(8,128)(2,1)} %bitcast.34), calls=%async_computation | async-start | bytes 4194304 | tf_op jit(solution)/shard_map/all_to_all | solution.py:763
  93.6 0.7 copy-start.3
  94.3 17.2 %copy-start.1 = (f32[1024]{0:T(1024)S(1)}, f32[1024]{0:T(1024)}, u32[]{:S(2)}) copy-start(f32[1024]{0:T(1024)} %param.25) | copy-start | bytes 12292
  94.3 4.3 %collective-permute-start.9 = (bf16[1056,128]{1,0:T(8,128)(2,1)}, bf16[1056,128]{1,0:T(8,128)(2,1)S(1)}, u32[]{:S(2)}, u32[]{:S(2)}) collective-permute-start(bf16[1056,128]{1,0:T(8,128)(2,1)} %get-tuple-element.62), channel_id=1, source_target_pairs={{0,248},{8,0},{16,8},{24,16},{32,24},{40,32},{48,40},{56,48},{64,5... | collective-permute-start | bytes 811016 | tf_op jit(solution)/shard_map/ppermute | solution.py:649
  94.4 6.2 %collective-permute-start.10 = (bf16[1056,128]{1,0:T(8,128)(2,1)}, bf16[1056,128]{1,0:T(8,128)(2,1)S(1)}, u32[]{:S(2)}, u32[]{:S(2)}) collective-permute-start(bf16[1056,128]{1,0:T(8,128)(2,1)} %copy-done.3), channel_id=1, source_target_pairs={{0,8},{8,16},{16,24},{24,32},{32,40},{40,48},{48,56},{56,64},{64,7... | collective-permute-start | bytes 811016 | tf_op jit(solution)/shard_map/ppermute | solution.py:649
